TPU v7x, 32 devices: a whole 2x2x4 slice. The times are simulated.
32 devices in a mesh: fsdp: 4 (over z), ctx: 2 (over y), tp: 4 (over x, core).
Axes of the slice: x: 2, y: 2, z: 4, core: 2. Of those that a mesh axis runs over, the one named last changes fastest.
Arguments:
- tokens: bfloat16 [4, 1024, 2560], P('fsdp', 'ctx'), may hold values from -40 to 40
- segments: int32 [4, 1024], P('fsdp'), may hold values from 0 to 3, as said below
- attn_gain: bfloat16 [2560], P(('fsdp', 'ctx')), may hold values from 0.25 to 1.75
- q_weight: bfloat16 [2560, 2560], P(('fsdp', 'ctx'), 'tp'), may hold values from -0.125 to 0.125
- k_weight: bfloat16 [2560, 640], P(('fsdp', 'ctx'), 'tp'), may hold values from -0.125 to 0.125
- v_weight: bfloat16 [2560, 640], P(('fsdp', 'ctx'), 'tp'), may hold values from -0.125 to 0.125
- o_weight: bfloat16 [2560, 2560], P('tp', ('fsdp', 'ctx')), may hold values from -0.5 to 0.5
- ffn_gain: bfloat16 [2560], P(('fsdp', 'ctx')), may hold values from 0.25 to 1.75
- gate_weight: bfloat16 [2560, 6912], P(('fsdp', 'ctx'), 'tp'), may hold values from -0.125 to 0.125
- up_weight: bfloat16 [2560, 6912], P(('fsdp', 'ctx'), 'tp'), may hold values from -0.125 to 0.125
- down_weight: bfloat16 [6912, 2560], P('tp', ('fsdp', 'ctx')), may hold values from -0.078125 to 0.078125
- cotangent: bfloat16 [4, 1024, 2560], P('fsdp', 'ctx'), may hold values from -6 to 6
Outputs:
- output: bfloat16 [4, 1024, 2560], P('fsdp', 'ctx')
- input_grad: bfloat16 [4, 1024, 2560], P('fsdp', 'ctx')
- attn_gain_grad: float32 [2560], P(('fsdp', 'ctx'))
- q_grad: float32 [2560, 2560], P(('fsdp', 'ctx'), 'tp')
- k_grad: float32 [2560, 640], P(('fsdp', 'ctx'), 'tp')
- v_grad: float32 [2560, 640], P(('fsdp', 'ctx'), 'tp')
- o_grad: float32 [2560, 2560], P('tp', ('fsdp', 'ctx'))
- ffn_gain_grad: float32 [2560], P(('fsdp', 'ctx'))
- gate_grad: float32 [2560, 6912], P(('fsdp', 'ctx'), 'tp')
- up_grad: float32 [2560, 6912], P(('fsdp', 'ctx'), 'tp')
- down_grad: float32 [6912, 2560], P('tp', ('fsdp', 'ctx'))
Inputs may be any that keep to these rules, and one draw needn't show every extreme that they name: `segments`: in each sequence four documents numbered 0 to 3 in order of position; document 1 covers at least positions 256 to 767.
All inputs are finite; a program needn't handle non-finite values.
Results may differ from a plain program's by a relative error of at most 0.014.
Values may be sent and summed in bfloat16 or wider, within the bound.
A program may use at most 256 MiB of HBM per device.

v0:
```python
import math

import jax
import jax.numpy as jnp
from jax import lax
from jax.sharding import PartitionSpec as P

HEAD_DIM = 80


NORM_EPS = 1e-05
ROPE_BASE = 10000.0
MASK_FILL = -1000000000.0


def rope_tables(segments, head_dim):
    n_seqs, full_len = segments.shape
    position = jnp.arange(full_len, dtype=jnp.int32)
    change = jnp.concatenate(
        [jnp.ones((n_seqs, 1), dtype=bool), segments[:, 1:] != segments[:, :-1]], axis=1
    )
    starts = lax.cummax(jnp.where(change, position[None, :], 0), axis=1)
    offset = (position[None, :] - starts).astype(jnp.float32)
    frequency = jnp.exp(
        jnp.arange(head_dim // 2, dtype=jnp.float32) * (-2.0 * math.log(ROPE_BASE) / head_dim)
    )
    angles = offset[:, :, None] * frequency[None, None, :]
    return (jnp.cos(angles)[:, :, None, :], jnp.sin(angles)[:, :, None, :])


def rotate(values, cos_t, sin_t):
    half_dim = values.shape[-1] // 2
    front_half = values[..., :half_dim]
    back_half = values[..., half_dim:]
    return jnp.concatenate(
        [front_half * cos_t - back_half * sin_t, back_half * cos_t + front_half * sin_t], axis=-1
    )


def rotate_back(values, cos_t, sin_t):
    half_dim = values.shape[-1] // 2
    front_half = values[..., :half_dim]
    back_half = values[..., half_dim:]
    return jnp.concatenate(
        [front_half * cos_t + back_half * sin_t, back_half * cos_t - front_half * sin_t], axis=-1
    )


def norm_back(inputs, root_val, gain_vec, d_normed):
    scaled = d_normed * gain_vec
    d_inputs = root_val * scaled - inputs * (root_val * root_val * root_val) * jnp.mean(
        scaled * inputs, axis=-1, keepdims=True
    )
    d_gain = jnp.sum(d_normed * inputs * root_val, axis=0)
    return (d_inputs, d_gain)


def body(
    tokens,
    segments,
    attn_gain,
    q_weight,
    k_weight,
    v_weight,
    o_weight,
    ffn_gain,
    gate_weight,
    up_weight,
    down_weight,
    cotangent,
):
    n_seqs, half_len, model_dim = tokens.shape
    full_len = segments.shape[1]
    n_rows = n_seqs * half_len
    head_dim = HEAD_DIM
    q_local = q_weight.shape[1] // head_dim
    kv_local = k_weight.shape[1] // head_dim
    groups = q_local // kv_local
    kv_here = kv_local // lax.axis_size("ctx")
    block_len = min(512, full_len)
    n_blocks = full_len // block_len
    score_scale = head_dim ** (-0.5)

    def reduce_all(value_in):
        return lax.psum(value_in, "tp")

    gain_one, q_full, k_full, v_full, gain_two, gate_full, up_full = (
        lax.all_gather(attn_gain, ("fsdp", "ctx"), axis=0, tiled=True),
        lax.all_gather(q_weight, ("fsdp", "ctx"), axis=0, tiled=True),
        lax.all_gather(k_weight, ("fsdp", "ctx"), axis=0, tiled=True),
        lax.all_gather(v_weight, ("fsdp", "ctx"), axis=0, tiled=True),
        lax.all_gather(ffn_gain, ("fsdp", "ctx"), axis=0, tiled=True),
        lax.all_gather(gate_weight, ("fsdp", "ctx"), axis=0, tiled=True),
        lax.all_gather(up_weight, ("fsdp", "ctx"), axis=0, tiled=True),
    )
    o_full, down_full = (
        lax.all_gather(o_weight, ("fsdp", "ctx"), axis=1, tiled=True),
        lax.all_gather(down_weight, ("fsdp", "ctx"), axis=1, tiled=True),
    )
    gain_one = gain_one.astype(jnp.float32)
    gain_two = gain_two.astype(jnp.float32)
    tok_f32 = tokens.reshape(n_rows, model_dim).astype(jnp.float32)
    root_attn = lax.rsqrt(jnp.mean(tok_f32 * tok_f32, axis=-1, keepdims=True) + NORM_EPS)
    norm_attn = (tok_f32 * root_attn * gain_one).astype(jnp.bfloat16)
    cos_all, sin_all = rope_tables(segments, head_dim)
    tok_start = lax.axis_index("ctx") * half_len
    cos_here = lax.dynamic_slice_in_dim(cos_all, tok_start, half_len, 1)
    sin_here = lax.dynamic_slice_in_dim(sin_all, tok_start, half_len, 1)
    q_pre = jnp.dot(norm_attn, q_full, preferred_element_type=jnp.float32).reshape(
        n_seqs, half_len, q_local, head_dim
    )
    k_pre = jnp.dot(norm_attn, k_full, preferred_element_type=jnp.float32).reshape(
        n_seqs, half_len, kv_local, head_dim
    )
    q_send = (
        rotate(q_pre, cos_here, sin_here)
        .astype(jnp.bfloat16)
        .reshape(n_seqs, half_len, q_local * head_dim)
    )
    k_send = (
        rotate(k_pre, cos_here, sin_here)
        .astype(jnp.bfloat16)
        .reshape(n_seqs, half_len, kv_local * head_dim)
    )
    v_send = (
        jnp.dot(norm_attn, v_full, preferred_element_type=jnp.float32)
        .astype(jnp.bfloat16)
        .reshape(n_seqs, half_len, kv_local * head_dim)
    )
    q_heads, k_heads, v_heads = (
        lax.all_to_all(q_send, "ctx", split_axis=2, concat_axis=1, tiled=True),
        lax.all_to_all(k_send, "ctx", split_axis=2, concat_axis=1, tiled=True),
        lax.all_to_all(v_send, "ctx", split_axis=2, concat_axis=1, tiled=True),
    )
    q_heads = q_heads.reshape(n_seqs, full_len, kv_here, groups, head_dim)
    k_heads = k_heads.reshape(n_seqs, full_len, kv_here, head_dim)
    v_heads = v_heads.reshape(n_seqs, full_len, kv_here, head_dim)
    key_pos = jnp.arange(full_len, dtype=jnp.int32)

    def masked_scores(q_block, q_start):
        scores = (
            jnp.einsum("bqkgd,bskd->bkgqs", q_block, k_heads, preferred_element_type=jnp.float32)
            * score_scale
        )
        seg_rows = segments[:, q_start : q_start + block_len]
        q_pos = q_start + jnp.arange(block_len, dtype=jnp.int32)
        allowed = (seg_rows[:, :, None] == segments[:, None, :]) & (
            key_pos[None, None, :] <= q_pos[None, :, None]
        )
        return jnp.where(allowed[:, None, None], scores, MASK_FILL)

    row_maxes = []
    row_totals = []
    seq_idx = 0
    out_blocks = []
    for block_idx in range(n_blocks):
        q_start = block_idx * block_len
        scores = masked_scores(
            q_heads[seq_idx : seq_idx + 1, q_start : q_start + block_len], q_start
        )
        row_max = jnp.max(scores, axis=-1, keepdims=True)
        exp_scores = jnp.exp(scores - row_max)
        row_total = jnp.sum(exp_scores, axis=-1, keepdims=True)
        prob_low = (exp_scores / row_total).astype(jnp.bfloat16)
        out_blocks.append(
            jnp.einsum(
                "bkgqs,bskd->bqkgd", prob_low, v_heads, preferred_element_type=jnp.float32
            ).astype(jnp.bfloat16)
        )
        row_maxes.append(row_max)
        row_totals.append(row_total)
    seq_outs = jnp.concatenate(out_blocks, axis=1)
    attn_heads = seq_outs.reshape(n_seqs, full_len, kv_here * groups * head_dim)
    attn_local = lax.all_to_all(attn_heads, "ctx", split_axis=1, concat_axis=2, tiled=True).reshape(
        n_rows, q_local * head_dim
    )
    attn_proj = jnp.dot(attn_local, o_full, preferred_element_type=jnp.float32)
    resid_mid = tok_f32 + reduce_all(attn_proj)
    root_ffn = lax.rsqrt(jnp.mean(resid_mid * resid_mid, axis=-1, keepdims=True) + NORM_EPS)
    norm_rows = (resid_mid * root_ffn * gain_two).astype(jnp.bfloat16)
    gate_val = jnp.dot(norm_rows, gate_full, preferred_element_type=jnp.float32)
    up_val = jnp.dot(norm_rows, up_full, preferred_element_type=jnp.float32)
    sig_gate = jax.nn.sigmoid(gate_val)
    hidden = (gate_val * sig_gate * up_val).astype(jnp.bfloat16)
    ffn_proj = jnp.dot(hidden, down_full, preferred_element_type=jnp.float32)
    output = (resid_mid + reduce_all(ffn_proj)).astype(jnp.bfloat16)
    d_out = cotangent.reshape(n_rows, model_dim)
    down_grad = jnp.einsum("tf,td->fd", hidden, d_out, preferred_element_type=jnp.float32)
    d_hidden = jnp.einsum("td,fd->tf", d_out, down_full, preferred_element_type=jnp.float32)
    d_up = (d_hidden * gate_val * sig_gate).astype(jnp.bfloat16)
    d_gate = (d_hidden * up_val * sig_gate * (1.0 + gate_val * (1.0 - sig_gate))).astype(
        jnp.bfloat16
    )
    gate_grad = jnp.einsum("td,tf->df", norm_rows, d_gate, preferred_element_type=jnp.float32)
    up_grad = jnp.einsum("td,tf->df", norm_rows, d_up, preferred_element_type=jnp.float32)
    d_norm_ffn = jnp.einsum(
        "tf,df->td", d_gate, gate_full, preferred_element_type=jnp.float32
    ) + jnp.einsum("tf,df->td", d_up, up_full, preferred_element_type=jnp.float32)
    d_mid_norm, gain_two_grad = norm_back(resid_mid, root_ffn, gain_two, reduce_all(d_norm_ffn))
    d_mid = d_out.astype(jnp.float32) + d_mid_norm
    d_proj = d_mid.astype(jnp.bfloat16)
    o_grad = jnp.einsum("tq,td->qd", attn_local, d_proj, preferred_element_type=jnp.float32)
    d_attn = (
        jnp.einsum("td,qd->tq", d_proj, o_full, preferred_element_type=jnp.float32)
        .astype(jnp.bfloat16)
        .reshape(n_seqs, half_len, q_local * head_dim)
    )
    d_attn_heads = lax.all_to_all(d_attn, "ctx", split_axis=2, concat_axis=1, tiled=True).reshape(
        n_seqs, full_len, kv_here, groups, head_dim
    )
    seq_idx = 0
    dk_sum = jnp.zeros((1, full_len, kv_here, head_dim), jnp.float32)
    dv_sum = jnp.zeros((1, full_len, kv_here, head_dim), jnp.float32)
    dq_blocks = []
    for block_idx in range(n_blocks):
        q_start = block_idx * block_len
        q_block = q_heads[seq_idx : seq_idx + 1, q_start : q_start + block_len]
        scores = masked_scores(q_block, q_start)
        kept_idx = seq_idx * n_blocks + block_idx
        prob_f32 = jnp.exp(scores - row_maxes[kept_idx]) / row_totals[kept_idx]
        prob_low = prob_f32.astype(jnp.bfloat16)
        d_block = d_attn_heads[seq_idx : seq_idx + 1, q_start : q_start + block_len]
        dv_sum = dv_sum + jnp.einsum(
            "bkgqs,bqkgd->bskd", prob_low, d_block, preferred_element_type=jnp.float32
        )
        d_prob = jnp.einsum(
            "bqkgd,bskd->bkgqs", d_block, v_heads, preferred_element_type=jnp.float32
        )
        d_score = (prob_f32 * (d_prob - jnp.sum(prob_f32 * d_prob, axis=-1, keepdims=True))).astype(
            jnp.bfloat16
        )
        dq_blocks.append(
            (
                jnp.einsum(
                    "bkgqs,bskd->bqkgd", d_score, k_heads, preferred_element_type=jnp.float32
                )
                * score_scale
            ).astype(jnp.bfloat16)
        )
        dk_sum = (
            dk_sum
            + jnp.einsum("bkgqs,bqkgd->bskd", d_score, q_block, preferred_element_type=jnp.float32)
            * score_scale
        )
    dq_seqs = jnp.concatenate(dq_blocks, axis=1)
    dk_seqs = dk_sum.astype(jnp.bfloat16)
    dv_seqs = dv_sum.astype(jnp.bfloat16)
    dq_heads = dq_seqs.reshape(n_seqs, full_len, kv_here * groups * head_dim)
    dk_heads = dk_seqs.reshape(n_seqs, full_len, kv_here * head_dim)
    dv_heads = dv_seqs.reshape(n_seqs, full_len, kv_here * head_dim)
    dq_local, dk_local, dv_local = (
        lax.all_to_all(dq_heads, "ctx", split_axis=1, concat_axis=2, tiled=True),
        lax.all_to_all(dk_heads, "ctx", split_axis=1, concat_axis=2, tiled=True),
        lax.all_to_all(dv_heads, "ctx", split_axis=1, concat_axis=2, tiled=True),
    )
    dq_pre = (
        rotate_back(
            dq_local.astype(jnp.float32).reshape(n_seqs, half_len, q_local, head_dim),
            cos_here,
            sin_here,
        )
        .astype(jnp.bfloat16)
        .reshape(n_rows, q_local * head_dim)
    )
    dk_pre = (
        rotate_back(
            dk_local.astype(jnp.float32).reshape(n_seqs, half_len, kv_local, head_dim),
            cos_here,
            sin_here,
        )
        .astype(jnp.bfloat16)
        .reshape(n_rows, kv_local * head_dim)
    )
    dv_pre = dv_local.reshape(n_rows, kv_local * head_dim)
    q_grad = jnp.einsum("td,tc->dc", norm_attn, dq_pre, preferred_element_type=jnp.float32)
    k_grad = jnp.einsum("td,tc->dc", norm_attn, dk_pre, preferred_element_type=jnp.float32)
    v_grad = jnp.einsum("td,tc->dc", norm_attn, dv_pre, preferred_element_type=jnp.float32)
    d_norm_attn = jnp.einsum("tc,dc->td", dq_pre, q_full, preferred_element_type=jnp.float32)
    d_norm_attn = d_norm_attn + jnp.einsum(
        "tc,dc->td", dk_pre, k_full, preferred_element_type=jnp.float32
    )
    d_norm_attn = d_norm_attn + jnp.einsum(
        "tc,dc->td", dv_pre, v_full, preferred_element_type=jnp.float32
    )
    d_in_norm, gain_one_grad = norm_back(tok_f32, root_attn, gain_one, reduce_all(d_norm_attn))
    input_grad = (d_mid + d_in_norm).astype(jnp.bfloat16)
    row_grads = (
        lax.psum_scatter(gain_one_grad, ("fsdp", "ctx"), scatter_dimension=0, tiled=True),
        lax.psum_scatter(q_grad, ("fsdp", "ctx"), scatter_dimension=0, tiled=True),
        lax.psum_scatter(k_grad, ("fsdp", "ctx"), scatter_dimension=0, tiled=True),
        lax.psum_scatter(v_grad, ("fsdp", "ctx"), scatter_dimension=0, tiled=True),
        lax.psum_scatter(gain_two_grad, ("fsdp", "ctx"), scatter_dimension=0, tiled=True),
        lax.psum_scatter(gate_grad, ("fsdp", "ctx"), scatter_dimension=0, tiled=True),
        lax.psum_scatter(up_grad, ("fsdp", "ctx"), scatter_dimension=0, tiled=True),
    )
    col_grads = (
        lax.psum_scatter(
            o_grad.astype(jnp.bfloat16), ("fsdp", "ctx"), scatter_dimension=1, tiled=True
        ).astype(jnp.float32),
        lax.psum_scatter(
            down_grad.astype(jnp.bfloat16), ("fsdp", "ctx"), scatter_dimension=1, tiled=True
        ).astype(jnp.float32),
    )
    return (
        output.reshape(n_seqs, half_len, model_dim),
        input_grad.reshape(n_seqs, half_len, model_dim),
        row_grads[0],
        row_grads[1],
        row_grads[2],
        row_grads[3],
        col_grads[0],
        row_grads[4],
        row_grads[5],
        row_grads[6],
        col_grads[1],
    )


def solution(mesh):
    return jax.shard_map(
        body,
        mesh=mesh,
        in_specs=(
            P("fsdp", "ctx", None),
            P("fsdp", None),
            P(("fsdp", "ctx")),
            P(("fsdp", "ctx"), "tp"),
            P(("fsdp", "ctx"), "tp"),
            P(("fsdp", "ctx"), "tp"),
            P("tp", ("fsdp", "ctx")),
            P(("fsdp", "ctx")),
            P(("fsdp", "ctx"), "tp"),
            P(("fsdp", "ctx"), "tp"),
            P("tp", ("fsdp", "ctx")),
            P("fsdp", "ctx", None),
        ),
        out_specs=(
            P("fsdp", "ctx", None),
            P("fsdp", "ctx", None),
            P(("fsdp", "ctx")),
            P(("fsdp", "ctx"), "tp"),
            P(("fsdp", "ctx"), "tp"),
            P(("fsdp", "ctx"), "tp"),
            P("tp", ("fsdp", "ctx")),
            P(("fsdp", "ctx")),
            P(("fsdp", "ctx"), "tp"),
            P(("fsdp", "ctx"), "tp"),
            P("tp", ("fsdp", "ctx")),
        ),
        check_vma=False,
    )
```

profile of v0, /device:TPU:0, one launch (start us, length us, event | category | flops | bytes accessed | tf_op | source)
XLA Modules:
  0.0 2307.4 jit_solution(6737094705396896363)
XLA Ops:
  13.3 39.2 %all-reduce.6 = (bf16[2560]{0:T(1024)(128)(2,1)S(1)}, bf16[2560]{0:T(1024)(128)(2,1)}) all-reduce(bf16[2560]{0:T(1024)(128)(2,1)S(1)} %dynamic-update-slice, bf16[2560]{0:T(1024)(128)(2,1)S(1)} %dynamic-update-slice.1), channel_id=1, replica_groups=mesh['fsdp'=4,'ctx'=2,'tp'=4] {'fsdp','ctx'}, use_global_device_ids=true, to_apply=%add | all-reduce | flops 5120 | bytes 20480
  52.5 35.3 %all-gather.1 = bf16[8,320,160]{1,2,0:T(8,128)(2,1)S(1)} all-gather(bf16[1,320,160]{1,2,0:T(8,128)(2,1)} %bitcast.444), channel_id=1, replica_groups=mesh['fsdp'=4,'ctx'=2,'tp'=4] {'fsdp','ctx'}, dimensions={0}, use_global_device_ids=true | all-gather | bytes 921600 | tf_op jit(solution)/shard_map/all_gather | solution.py:90
  97.0 4.0 all-to-all-start.1
  101.8 34.2 %all-gather = bf16[8,320,160]{1,2,0:T(8,128)(2,1)S(1)} all-gather(bf16[1,320,160]{1,2,0:T(8,128)(2,1)} %bitcast.445), channel_id=1, replica_groups=mesh['fsdp'=4,'ctx'=2,'tp'=4] {'fsdp','ctx'}, dimensions={0}, use_global_device_ids=true | all-gather | bytes 921600 | tf_op jit(solution)/shard_map/all_gather | solution.py:91
  141.2 3.2 reduce.10
  146.0 5.6 copy.141
  151.7 3.9 fusion.63
  155.9 3.8 all-to-all-start
  161.8 5.6 reduce.12
  168.6 4.3 all-to-all-start.2
  193.2 3.7 fusion.7
  203.0 4.8 copy.146
  207.8 7.4 reduce.13
  217.8 11.6 all_to_all.108
  229.5 3.1 reshape.841
  240.0 6.7 fusion.133
  248.8 98.9 %all-reduce.11.cloned.1.call-done = f32[512,2560]{1,0:T(8,128)} async-done(((f32[512,2560]{1,0:T(8,128)}), f32[512,2560]{1,0:T(8,128)}) %all-reduce.11.cloned.1.call-update) | async-done | bytes 5242896 | tf_op jit(solution)/shard_map/psum | solution.py:85
  347.7 3.2 multiply_reduce_fusion.2
  355.2 129.6 %all-gather.14.cloned.1.call-done = bf16[2560,1728]{1,0:T(8,128)(2,1)} async-done(((bf16[320,1728]{1,0:T(8,128)(2,1)}), bf16[2560,1728]{1,0:T(8,128)(2,1)}) %all-gather.14.cloned.1.call-update) | async-done | bytes 8847376 | tf_op jit(solution)/shard_map/all_gather | solution.py:94
  484.8 10.9 fusion.135
  495.7 124.2 %all-gather.12.cloned.1.call-done = bf16[2560,1728]{1,0:T(8,128)(2,1)} async-done(((bf16[320,1728]{1,0:T(8,128)(2,1)}), bf16[2560,1728]{1,0:T(8,128)(2,1)}) %all-gather.12.cloned.1.call-update) | async-done | bytes 8847376 | tf_op jit(solution)/shard_map/all_gather | solution.py:93
  619.9 11.1 fusion.134
  631.0 124.0 %all-gather.16.cloned.1.call-done = bf16[1728,2560]{0,1:T(8,128)(2,1)} async-done(((bf16[1728,320]{0,1:T(8,128)(2,1)}), bf16[1728,2560]{0,1:T(8,128)(2,1)}) %all-gather.16.cloned.1.call-update) | async-done | bytes 8847376 | tf_op jit(solution)/shard_map/all_gather | solution.py:98
  755.0 15.7 multiply_convert_fusion.1
  770.7 8.2 fusion.137
  779.0 10.4 convolution_add_fusion
  789.4 100.9 %all-reduce.13.cloned.1.call-done = f32[512,2560]{1,0:T(8,128)} async-done(((f32[512,2560]{1,0:T(8,128)}), f32[512,2560]{1,0:T(8,128)}) %all-reduce.13.cloned.1.call-update) | async-done | bytes 5242896 | tf_op jit(solution)/shard_map/psum | solution.py:85
  890.3 6.1 multiply_reduce_fusion
  896.6 4.1 subtract_add_fusion
  903.0 3.1 fusion.68
  906.1 3.9 copy.149
  910.0 6.4 reduce.14
  918.6 13.8 all_to_all.109
  940.7 5.0 fusion.87
  945.8 7.1 fusion
  960.9 3.4 all-to-all-start.7
  964.4 9.3 fusion.31
  980.0 5.7 fusion.3
  987.1 5.0 fusion.30
  1000.4 8.1 all_to_all.110
  1014.1 11.7 fusion.136
  1029.8 4.9 copy.153
  1034.6 7.7 reduce.15
  1044.9 4.3 all-to-all-start.5
  1049.3 4.2 fusion.139
  1053.5 4.1 all-to-all-done.5
  1057.5 3.2 reshape.845
  1060.7 3.6 copy.154
  1071.3 3.2 add_add_fusion
  1074.9 6.8 convolution_convert_fusion.1
  1081.7 10.7 convolution_convert_fusion
  1092.5 5.1 fusion.53
  1097.7 13.6 fusion.141
  1111.6 13.6 fusion.140
  1129.5 184.0 %all-reduce.15.cloned.1.call-done = (f32[512,2560]{1,0:T(8,128)}, f32[512,2560]{1,0:T(8,128)}) async-done(((f32[512,2560]{1,0:T(8,128)}, f32[512,2560]{1,0:T(8,128)}), (f32[512,2560]{1,0:T(8,128)}, f32[512,2560]{1,0:T(8,128)})) %all-reduce.15.cloned.1.call-update) | async-done | bytes 10485776 | tf_op jit(solution)/shard_map/psum | solution.py:85
  1313.5 4.1 fusion.27
  1317.6 38.2 %all-reduce.4 = (f32[2560]{0:T(1024)S(1)}, f32[2560]{0:T(1024)S(1)}) all-reduce(f32[2560]{0:T(1024)S(1)} %get-tuple-element.13, f32[2560]{0:T(1024)S(1)} %copy-done.41), channel_id=2, replica_groups=mesh['fsdp'=4,'ctx'=2,'tp'=4] {'fsdp','ctx'}, use_global_device_ids=true, to_apply=%region_17.18.clone | all-reduce | flops 5120 | bytes 40960
  1357.1 6.5 fusion.42
  1363.6 4.5 fusion.43
  1368.1 25.9 %reduce-scatter.14.cloned.1.call-done = bf16[640,320]{0,1:T(8,128)(2,1)} async-done(((bf16[640,2560]{0,1:T(8,128)(2,1)}), bf16[640,320]{0,1:T(8,128)(2,1)}) %reduce-scatter.14.cloned.1.call-update) | async-done | bytes 409616 | tf_op jit(solution)/shard_map/reduce_scatter | solution.py:297
  1395.9 160.8 %reduce-scatter.20.cloned.1.call-done = bf16[1728,320]{0,1:T(8,128)(2,1)} async-done(((bf16[1728,2560]{0,1:T(8,128)(2,1)}), bf16[1728,320]{0,1:T(8,128)(2,1)}) %reduce-scatter.20.cloned.1.call-update) | async-done | bytes 1105936 | tf_op jit(solution)/shard_map/reduce_scatter | solution.py:300
  1559.5 122.2 %reduce-scatter.12.cloned.1.call-done = f32[320,640]{1,0:T(8,128)} async-done(((f32[2560,640]{1,0:T(8,128)}), f32[320,640]{1,0:T(8,128)}) %reduce-scatter.12.cloned.1.call-update) | async-done | bytes 819216 | tf_op jit(solution)/shard_map/reduce_scatter | solution.py:289
  1681.7 309.9 %reduce-scatter.18.cloned.1.call-done = f32[320,1728]{1,0:T(8,128)} async-done(((f32[2560,1728]{1,0:T(8,128)}), f32[320,1728]{1,0:T(8,128)}) %reduce-scatter.18.cloned.1.call-update) | async-done | bytes 2211856 | tf_op jit(solution)/shard_map/reduce_scatter | solution.py:294
  1991.6 308.8 %reduce-scatter.16.cloned.1.call-done = f32[320,1728]{1,0:T(8,128)} async-done(((f32[2560,1728]{1,0:T(8,128)}), f32[320,1728]{1,0:T(8,128)}) %reduce-scatter.16.cloned.1.call-update) | async-done | bytes 2211856 | tf_op jit(solution)/shard_map/reduce_scatter | solution.py:293
  (248 shorter events, 134.6 us)
Async XLA Ops:
  7.2 84.2 %copy-start.1 = (bf16[1,512,2560]{2,1,0:T(8,128)(2,1)S(1)}, bf16[1,512,2560]{2,1,0:T(8,128)(2,1)}, u32[]{:S(2)}) copy-start(bf16[1,512,2560]{2,1,0:T(8,128)(2,1)} %param.12) | copy-start | bytes 7864324
  7.2 138.9 %all-gather.8.cloned.1.call-start = ((), (), s32[]{:S(2)}) async-start(), calls=%async_computation.15 | async-start | bytes 3686400 | tf_op jit(solution)/shard_map/all_gather | solution.py:89
  52.5 99.1 %copy-start.34 = (f32[2560]{0:T(1024)}, f32[2560]{0:T(1024)S(1)}, u32[]{:S(2)}) copy-start(f32[2560]{0:T(1024)S(1)} %convert_element_type.253) | copy-start | bytes 30724
  90.9 2.9 copy-start.13
  91.4 2.7 copy-start.23
  91.4 64.2 %copy-start.21 = (f32[512,40]{0,1:T(8,128)}, f32[512,40]{0,1:T(8,128)S(1)}, u32[]{:S(2)}) copy-start(f32[512,40]{0,1:T(8,128)S(1)} %get-tuple-element.34) | copy-start | bytes 245764
  92.0 9.8 copy-start.38
  92.6 59.1 %copy-start.39 = (f32[512]{0:T(512)}, f32[512]{0:T(512)S(1)}, u32[]{:S(2)}) copy-start(f32[512]{0:T(512)S(1)} %get-tuple-element.41) | copy-start | bytes 6148
  97.0 58.9 %all-to-all-start.1 = ((bf16[2,2,20480]{2,1,0:T(2,128)(2,1)}), bf16[2,2,20480]{2,1,0:T(2,128)(2,1)}, u32[]{:S(2)}, u32[]{:S(2)}) async-start(bf16[2,2,20480]{2,1,0:T(2,128)(2,1)} %reshape.836), calls=%async_computation.1 | async-start | bytes 327680 | tf_op jit(solution)/shard_map/all_to_all | solution.py:132
  101.0 139.0 %all-gather.10.cloned.1.call-start = ((), (), s32[]{:S(2)}) async-start(), calls=%async_computation.16 | async-start | bytes 3686400 | tf_op jit(solution)/shard_map/all_gather | solution.py:97
  139.1 12.6 copy-start.16
  151.7 3.9 copy-start.24
  155.9 12.7 all-to-all-start
  168.6 4.3 copy-start.33
  168.6 11.7 all-to-all-start.2
  172.9 174.7 %all-reduce.11.cloned.1.call-start = ((), (), s32[]{:S(2)}) async-start(), calls=%async_computation.17 | async-start | bytes 10485760 | tf_op jit(solution)/shard_map/psum | solution.py:85
  175.8 15.6 copy-start.27
  188.6 2.9 copy-start.18
  191.4 8.0 copy-start.7
  193.2 3.8 copy-start.6
  193.2 3.7 copy-start.36
  246.8 238.0 %all-gather.14.cloned.1.call-start = ((), (), s32[]{:S(2)}) async-start(), calls=%async_computation.19 | async-start | bytes 10321920 | tf_op jit(solution)/shard_map/all_gather | solution.py:94
  247.4 372.5 %all-gather.12.cloned.1.call-start = ((), (), s32[]{:S(2)}) async-start(), calls=%async_computation.18 | async-start | bytes 10321920 | tf_op jit(solution)/shard_map/all_gather | solution.py:93
  247.9 507.1 %all-gather.16.cloned.1.call-start = ((), (), s32[]{:S(2)}) async-start(), calls=%async_computation.20 | async-start | bytes 10321920 | tf_op jit(solution)/shard_map/all_gather | solution.py:98
  248.5 641.8 %all-reduce.13.cloned.1.call-start = ((), (), s32[]{:S(2)}) async-start(), calls=%async_computation.21 | async-start | bytes 10485760 | tf_op jit(solution)/shard_map/psum | solution.py:85
  350.9 2.3 copy-start
  770.7 8.2 copy-start.45
  890.3 6.1 copy-start.10
  890.3 6.4 copy-start.20
  896.6 6.4 copy-start.44
  900.7 2.3 copy-start.9
  940.7 5.0 copy-start.12
  940.7 5.0 copy-start.32
  940.7 12.1 slice-start
  945.8 7.1 slice-start.1
  960.9 12.8 all-to-all-start.7
  964.3 161.6 %reduce-scatter.24.cloned.1.call-start = ((), (), s32[]{:S(2)}) async-start(), calls=%async_computation.28 | async-start | bytes 2949120
  964.3 12.7 copy-start.35
  964.4 12.6 copy-start.40
  976.3 3.7 copy-start.37
  980.0 147.7 %reduce-scatter.22.cloned.1.call-start = ((), (), s32[]{:S(2)}) async-start(), calls=%async_computation.27 | async-start | bytes 2949120
  980.0 5.7 copy-start.2
  980.0 5.7 copy-start.19
  994.2 16.2 copy-start.22
  994.2 16.2 copy-start.25
  1014.1 11.7 copy-start.3
  1014.1 11.7 copy-start.28
  1028.8 20.5 copy-start.14
  1044.9 12.6 all-to-all-start.5
  1049.2 264.3 %all-reduce.15.cloned.1.call-start = ((), (), s32[]{:S(2)}) async-start(), calls=%async_computation.29 | async-start | bytes 20971520 | tf_op jit(solution)/shard_map/psum | solution.py:85
  1053.5 14.8 copy-start.26
  1066.5 2.4 copy-start.15
  1068.6 2.6 slice-start.2
  1068.6 2.6 copy-start.17
  1068.6 2.6 copy-start.31
  1068.9 2.4 slice-start.3
  1074.6 319.4 %reduce-scatter.14.cloned.1.call-start = ((), (), s32[]{:S(2)}) async-start(), calls=%async_computation.23 | async-start | bytes 3686400 | tf_op jit(solution)/shard_map/reduce_scatter | solution.py:297
  1081.7 475.0 %reduce-scatter.20.cloned.1.call-start = ((), (), s32[]{:S(2)}) async-start(), calls=%async_computation.26 | async-start | bytes 10321920 | tf_op jit(solution)/shard_map/reduce_scatter | solution.py:300
  1092.5 589.2 %reduce-scatter.12.cloned.1.call-start = ((), (), s32[]{:S(2)}) async-start(), calls=%async_computation.22 | async-start | bytes 7372800 | tf_op jit(solution)/shard_map/reduce_scatter | solution.py:289
  1097.6 894.0 %reduce-scatter.18.cloned.1.call-start = ((), (), s32[]{:S(2)}) async-start(), calls=%async_computation.25 | async-start | bytes 20643840 | tf_op jit(solution)/shard_map/reduce_scatter | solution.py:294
  1111.3 1189.1 %reduce-scatter.16.cloned.1.call-start = ((), (), s32[]{:S(2)}) async-start(), calls=%async_computation.24 | async-start | bytes 20643840 | tf_op jit(solution)/shard_map/reduce_scatter | solution.py:293
  1125.2 192.5 %copy-start.41 = (f32[2560]{0:T(1024)S(1)}, f32[2560]{0:T(1024)}, u32[]{:S(2)}) copy-start(f32[2560]{0:T(1024)} %get-tuple-element.11) | copy-start | bytes 30724
  1357.1 6.5 copy-start.8
  1357.1 6.5 copy-start.42
  (6 other events, 9.3 us)
Sparse Core Ops, SparseCore 0:
  10.2 82.5 all-gather.7
  104.0 66.5 all-gather.9
  246.9 100.7 all-reduce.10
  349.7 135.0 all-gather.13
  486.8 133.0 all-gather.11
  621.9 133.0 all-gather.15
  789.5 100.6 all-reduce.12
  980.1 71.4 reduce-scatter.23
  1055.6 69.3 reduce-scatter.21
  1127.5 185.9 all-reduce.14
  1317.1 76.8 reduce-scatter.13
  1397.9 158.7 reduce-scatter.19
  1560.9 120.7 reduce-scatter.11
  1686.6 304.9 reduce-scatter.17
  1996.0 304.4 reduce-scatter.15
where the time goes:
time: 2320 us; the launch traced here: 2310 us
  waiting for transfers between devices  1700 us (73%)
  matrix products  184 us (8%)
  blocking collectives  181 us (8%)
  local copies, waits for them, and re-layouts  110 us (5%)
  other arithmetic  97.9 us (4%)
    psum x3, waiting for transfers between devices, reduce_all(): return lax.psum(value_in, 'tp')  384 us
    reduce_scatter x1, waiting for transfers between devices, body(): lax.psum_scatter(up_grad, ('fsdp', 'ctx'), scatter_dimension=0, tiled=True)  310 us
    reduce_scatter x1, waiting for transfers between devices, body(): lax.psum_scatter(gate_grad, ('fsdp', 'ctx'), scatter_dimension=0, tiled=T...  309 us
    reduce_scatter x1, waiting for transfers between devices, body(): lax.psum_scatter(down_grad.astype(jnp.bfloat16), ('fsdp', 'ctx'), scatter...  161 us
    all_gather x1, waiting for transfers between devices, body(): lax.all_gather(up_weight, ('fsdp', 'ctx'), axis=0, tiled=True)  130 us
    all_gather x1, waiting for transfers between devices, body(): lax.all_gather(gate_weight, ('fsdp', 'ctx'), axis=0, tiled=True)  124 us
    all_gather x1, waiting for transfers between devices, body(): lax.all_gather(down_weight, ('fsdp', 'ctx'), axis=1, tiled=True)  124 us
    reduce_scatter x1, waiting for transfers between devices, body(): lax.psum_scatter(q_grad, ('fsdp', 'ctx'), scatter_dimension=0, tiled=True)  122 us
  transfers between devices with their start and end apart: 20, of which 13 were waited for; matrix products, arithmetic and copies ran while one was open for 12% of the time, Pallas kernels for 0%

commit v1 on v0

v1 whole, which is shorter than its diff:
```python
import math

import jax
import jax.numpy as jnp
from jax import lax
from jax.experimental import pallas as pl
from jax.experimental.pallas import tpu as pltpu
from jax.sharding import PartitionSpec as P

HEAD_DIM = 80
HALF = HEAD_DIM // 2
LANES = 128
NORM_EPS = 1e-05
ROPE_BASE = 10000.0
MASK_FILL = -1000000000.0
F32 = jnp.float32
BF16 = jnp.bfloat16


def pp(value, axis, mask):
    size = lax.axis_size(axis)
    return lax.ppermute(value, axis, [(i, i ^ mask) for i in range(size)])


def dot(a, b, dims=((1,), (0,))):
    return lax.dot_general(a, b, (dims, ((), ())), preferred_element_type=F32)


def in_order(bit, mine, other, axis=0):
    return jnp.where(
        bit == 0, jnp.stack([mine, other], axis), jnp.stack([other, mine], axis)
    )


def pick(blocks, index):
    return lax.dynamic_index_in_dim(blocks, index, 0, keepdims=False)


def attend_kernel(scale, block, qkv, cos, sin, seg_col, seg_row, sel, attn, rot, stats):
    full_len = qkv.shape[0]
    n_q = rot.shape[1] // LANES - 2
    cos_t, sin_t = cos[...], sin[...]
    for h in range(n_q + 1):
        u = qkv[:, h * LANES : (h + 1) * LANES]
        rot[:, h * LANES : (h + 1) * LANES] = (u * cos_t + pltpu.roll(u, 64, 1) * sin_t).astype(BF16)
    rot[:, (n_q + 1) * LANES :] = qkv[:, (n_q + 1) * LANES :].astype(BF16)
    for i in range(full_len // block):
        rows = slice(i * block, (i + 1) * block)
        keys = (i + 1) * block
        q_pos = i * block + lax.broadcasted_iota(jnp.int32, (block, keys), 0)
        k_pos = lax.broadcasted_iota(jnp.int32, (block, keys), 1)
        allowed = (seg_col[rows, :] == seg_row[:, :keys]) & (k_pos <= q_pos)
        k = rot[:keys, n_q * LANES : (n_q + 1) * LANES]
        v = rot[:keys, (n_q + 1) * LANES :]
        outs, maxes, totals = [], [], []
        for h in range(n_q):
            s = dot(rot[rows, h * LANES : (h + 1) * LANES], k, ((1,), (1,))) * scale
            s = jnp.where(allowed, s, MASK_FILL)
            top = jnp.max(s, axis=1, keepdims=True)
            e = jnp.exp(s - top)
            total = jnp.sum(e, axis=1, keepdims=True)
            outs.append(dot((e * (1.0 / total)).astype(BF16), v).astype(BF16))
            maxes.append(top)
            totals.append(total)
        attn[rows, :] = dot(jnp.concatenate(outs, axis=1), sel[...]).astype(BF16)
        stats[rows, :] = jnp.concatenate(maxes + totals, axis=1)


def attend_back_kernel(
    scale, block, rot, d_attn, stats, cos, sin, seg_col, seg_row, sel, d_qkv, dk_sum, dv_sum
):
    full_len = rot.shape[0]
    n_q = rot.shape[1] // LANES - 2
    dk_sum[...] = jnp.zeros_like(dk_sum)
    dv_sum[...] = jnp.zeros_like(dv_sum)

    def back(u, at):
        return (u * cos[at, :] - pltpu.roll(u, 64, 1) * sin[at, :]).astype(BF16)

    for i in range(full_len // block):
        rows = slice(i * block, (i + 1) * block)
        keys = (i + 1) * block
        q_pos = i * block + lax.broadcasted_iota(jnp.int32, (block, keys), 0)
        k_pos = lax.broadcasted_iota(jnp.int32, (block, keys), 1)
        allowed = (seg_col[rows, :] == seg_row[:, :keys]) & (k_pos <= q_pos)
        k = rot[:keys, n_q * LANES : (n_q + 1) * LANES]
        v = rot[:keys, (n_q + 1) * LANES :]
        d_out = dot(d_attn[rows, :], sel[...], ((1,), (1,))).astype(BF16)
        stat = stats[rows, :]
        for h in range(n_q):
            q = rot[rows, h * LANES : (h + 1) * LANES]
            d_h = d_out[:, h * LANES : (h + 1) * LANES]
            s = dot(q, k, ((1,), (1,))) * scale
            s = jnp.where(allowed, s, MASK_FILL)
            p = jnp.exp(s - stat[:, h : h + 1]) * (1.0 / stat[:, n_q + h : n_q + h + 1])
            dv_sum[:keys, :] += dot(p.astype(BF16), d_h, ((0,), (0,)))
            d_p = dot(d_h, v, ((1,), (1,)))
            d_s = (p * (d_p - jnp.sum(p * d_p, axis=1, keepdims=True))).astype(BF16)
            d_q = (dot(d_s, k) * scale).astype(BF16).astype(F32)
            d_qkv[rows, h * LANES : (h + 1) * LANES] = back(d_q, rows)
            dk_sum[:keys, :] += dot(d_s, q, ((0,), (0,)))
    d_k = (dk_sum[...] * scale).astype(BF16).astype(F32)
    d_qkv[:, n_q * LANES : (n_q + 1) * LANES] = back(d_k, slice(None))
    d_qkv[:, (n_q + 1) * LANES :] = dv_sum[...].astype(BF16)


VMEM_LIMIT = 56 * 1024 * 1024


def attend(qkv, cos, sin, seg_col, seg_row, sel, scale):
    full_len, width = qkv.shape
    n_q = width // LANES - 2
    return pl.pallas_call(
        lambda *refs: attend_kernel(scale, min(256, full_len), *refs),
        out_shape=(
            jax.ShapeDtypeStruct((full_len, sel.shape[1]), BF16),
            jax.ShapeDtypeStruct((full_len, width), BF16),
            jax.ShapeDtypeStruct((full_len, 2 * n_q), F32),
        ),
        compiler_params=pltpu.CompilerParams(vmem_limit_bytes=VMEM_LIMIT),
        cost_estimate=pl.CostEstimate(
            flops=2 * n_q * full_len * full_len * LANES,
            bytes_accessed=full_len * width * 6,
            transcendentals=n_q * full_len * full_len // 2,
        ),
        name="attend",
    )(qkv, cos, sin, seg_col, seg_row, sel)


def attend_back(rot, d_attn, stats, cos, sin, seg_col, seg_row, sel, scale):
    full_len, width = rot.shape
    n_q = width // LANES - 2
    return pl.pallas_call(
        lambda *refs: attend_back_kernel(scale, min(256, full_len), *refs),
        out_shape=jax.ShapeDtypeStruct((full_len, width), BF16),
        scratch_shapes=[pltpu.VMEM((full_len, LANES), F32), pltpu.VMEM((full_len, LANES), F32)],
        compiler_params=pltpu.CompilerParams(vmem_limit_bytes=VMEM_LIMIT),
        cost_estimate=pl.CostEstimate(
            flops=5 * n_q * full_len * full_len * LANES,
            bytes_accessed=full_len * width * 6,
            transcendentals=n_q * full_len * full_len // 2,
        ),
        name="attend_back",
    )(rot, d_attn, stats, cos, sin, seg_col, seg_row, sel)


def gather_layer(own):
    half = own.shape[-1] // 2
    a, b = own[:, :half], own[:, half:]
    a1 = jnp.stack([a, pp(a, "tp", 2)])
    b1 = jnp.stack([b, pp(b, "ctx", 1)])
    a2 = jnp.stack([a1, pp(a1, "ctx", 1)])
    b2 = jnp.stack([b1, pp(b1, "tp", 2)], axis=1)
    mine = jnp.concatenate([a2, b2], axis=-1)
    return jnp.stack([mine, pp(mine, "tp", 1)], axis=2)


def scatter_layer(lhs, rhs, dims=((1,), (0,))):
    rows, depth = lhs.shape[-2:]

    def product(part):
        return dot(part.reshape(4 * rows, depth), rhs, dims).reshape(2, 2, rows, -1)

    sent = pp(product(lhs[:, :, 1]).astype(BF16), "tp", 1)
    kept = product(lhs[:, :, 0]) + sent.astype(F32)
    half = kept.shape[-1] // 2
    a, b = kept[..., :half], kept[..., half:]
    a1 = a[:, 0] + pp(a[:, 1].astype(BF16), "tp", 2).astype(F32)
    b1 = b[0] + pp(b[1].astype(BF16), "ctx", 1).astype(F32)
    a2 = a1[0] + pp(a1[1].astype(BF16), "ctx", 1).astype(F32)
    b2 = b1[0] + pp(b1[1].astype(BF16), "tp", 2).astype(F32)
    return jnp.concatenate([a2, b2], axis=-1)


def gather_tp(own):
    index = lax.axis_index("tp")
    pair = in_order(index // 2, own, pp(own, "tp", 2))
    return in_order(index % 2, pair, pp(pair, "tp", 1), axis=1).reshape(-1, own.shape[-1])


def sum_tp(value):
    value = value + pp(value, "tp", 1)
    return value + pp(value, "tp", 2)


def by_xor(value, parts, index):
    blocks = value.reshape(parts, -1, value.shape[-1])
    return jnp.stack([pick(blocks, index ^ r) for r in range(parts)])


def below(top):
    masks = []
    while top > 1:
        top //= 2
        masks.append(top)
    return masks


def gather_z(held, top):
    held = dict(held)
    for mask in below(top):
        for rel in list(held):
            held[rel ^ mask] = pp(held[rel], "fsdp", mask)
    return held


def place(held, index, axis):
    shape = list(next(iter(held.values())).shape)
    size = shape[axis]
    shape[axis] = size * len(held)
    out = jnp.zeros(shape, BF16)
    for rel, block in held.items():
        start = [0] * len(shape)
        start[axis] = (index ^ rel) * size
        out = lax.dynamic_update_slice(out, block, start)
    return out


def scatter_z(blocks, top):
    blocks = dict(blocks)
    for mask in reversed(below(top)):
        for rel in [r for r in blocks if r & mask]:
            blocks[rel ^ mask] = blocks[rel ^ mask] + pp(
                blocks.pop(rel).astype(BF16), "fsdp", mask
            ).astype(F32)
    return blocks


def split_z(value, n, index, axis):
    size = value.shape[axis] // n
    return {
        rel: lax.dynamic_slice_in_dim(value, (index ^ rel) * size, size, axis) for rel in range(n)
    }


def body(
    tokens,
    segments,
    attn_gain,
    q_weight,
    k_weight,
    v_weight,
    o_weight,
    ffn_gain,
    gate_weight,
    up_weight,
    down_weight,
    cotangent,
):
    n_z = lax.axis_size("fsdp")
    n_tp = lax.axis_size("tp")
    z, y, t = lax.axis_index("fsdp"), lax.axis_index("ctx"), lax.axis_index("tp")
    zb = z // (n_z // 2)
    _, half_len, width = tokens.shape
    full_len = segments.shape[1]
    rows = half_len // n_tp
    depth = q_weight.shape[0]
    q_cols = q_weight.shape[1] // 2
    kv_cols = k_weight.shape[1] // 2
    units = gate_weight.shape[1] // 4
    n_q = q_cols // HEAD_DIM
    scale = HEAD_DIM ** (-0.5)
    me = y * n_tp + t

    def two(w):
        return w.reshape(w.shape[0], 2, -1).transpose(1, 0, 2)

    extra = jnp.stack([attn_gain, ffn_gain], axis=1)
    extra = jnp.broadcast_to(jnp.pad(extra, ((0, 0), (0, 30)))[None], (2, depth, 32))
    packed = jnp.concatenate([two(q_weight), two(k_weight), two(v_weight), extra], axis=2)
    compact = packed.shape[2]
    in_blk = in_order(y, pick(packed, y), pp(pick(packed, 1 - y), "ctx", 1)).reshape(2 * depth, -1)
    w_in = place(gather_z({0: in_blk}, n_z), z, 0)

    x_here = tokens.reshape(half_len, width)
    x_half = pp(pick(x_here.reshape(2, half_len // 2, width), t % 2), "ctx", 1)
    x_other = in_order(t % 2, x_half, pp(x_half, "tp", 1)).reshape(half_len, width)
    x_all = in_order(y, x_here, x_other).reshape(full_len, width)

    o_two = o_weight.reshape(2, q_cols, depth)
    o_blk = jnp.concatenate(
        list(in_order(y, pick(o_two, y), pp(pick(o_two, 1 - y), "ctx", 1))), axis=1
    )
    w_o = place(gather_z({0: o_blk}, n_z), z, 1)

    def four(w):
        return w.reshape(depth, 2, 2, units).transpose(1, 2, 0, 3)

    gu = jnp.concatenate([four(gate_weight), four(up_weight)], axis=3)
    gu_y = gu.transpose(1, 0, 2, 3)
    gu_blk = in_order(y, pick(gu_y, y), pp(pick(gu_y, 1 - y), "ctx", 1), axis=1).reshape(
        2, 2 * depth, 2 * units
    )
    w_gu = place(
        gather_z({0: pick(gu_blk, zb), n_z // 2: pp(pick(gu_blk, 1 - zb), "fsdp", n_z // 2)}, n_z // 2),
        z,
        0,
    )
    dn_y = down_weight.reshape(2, 2, units, depth).transpose(1, 0, 2, 3)
    dn_pair = in_order(y, pick(dn_y, y), pp(pick(dn_y, 1 - y), "ctx", 1))
    dn_blk = jnp.concatenate([dn_pair[0], dn_pair[1]], axis=2)
    w_dn = place(
        gather_z({0: pick(dn_blk, zb), n_z // 2: pp(pick(dn_blk, 1 - zb), "fsdp", n_z // 2)}, n_z // 2),
        z,
        1,
    )

    seg = segments.reshape(full_len)
    start = jnp.sum((seg[None, :] < seg[:, None]).astype(jnp.int32), axis=1)
    offset = (jnp.arange(full_len, dtype=jnp.int32) - start).astype(F32)
    lane = jnp.arange(LANES)
    within = lane % 64
    frequency = jnp.where(
        within < HALF, jnp.exp(within.astype(F32) * (-2.0 * math.log(ROPE_BASE) / HEAD_DIM)), 0.0
    )
    angles = offset[:, None] * frequency[None, :]
    cos = jnp.cos(angles)
    sin = jnp.sin(angles) * jnp.where(lane < 64, -1.0, 1.0)[None, :]
    seg_col, seg_row = seg[:, None], seg[None, :]

    col = jnp.arange(compact)
    at = col % HEAD_DIM
    head = col // HEAD_DIM
    spot = jnp.where(head < n_q + 1, at + jnp.where(at >= HALF, 64 - HALF, 0), at) + head * LANES
    spot = jnp.where(head < n_q + 2, spot, -1)
    spread = (spot[:, None] == jnp.arange((n_q + 2) * LANES)[None, :]).astype(BF16)
    c320 = jnp.arange(q_cols)
    sel = (
        jnp.arange(n_q * LANES)[:, None]
        == ((c320 // HEAD_DIM) * LANES + c320 % HEAD_DIM)[None, :]
    ).astype(BF16)

    gain_one = w_in[:, compact - 32].astype(F32)[None, :]
    gain_two = w_in[:, compact - 31].astype(F32)[None, :]
    w_heads = dot(w_in, spread).astype(BF16)
    x_f32 = x_all.astype(F32)
    root_all = lax.rsqrt(jnp.mean(x_f32 * x_f32, axis=1, keepdims=True) + NORM_EPS)
    norm_attn = (x_f32 * root_all * gain_one).astype(BF16)
    qkv = dot(norm_attn, w_heads)
    attn, rot, stats = attend(qkv, cos, sin, seg_col, seg_row, sel, scale)
    attn_rel = by_xor(attn, 2 * n_tp, me)
    x_mine = lax.dynamic_slice_in_dim(x_here, t * rows, rows, 0).astype(F32)
    mid = x_mine + scatter_layer(attn_rel.reshape(2, 2, 2, rows, q_cols), w_o)
    root_ffn = lax.rsqrt(jnp.mean(mid * mid, axis=1, keepdims=True) + NORM_EPS)
    norm_ffn = (mid * root_ffn * gain_two).astype(BF16)

    def both(own):
        return gather_layer(own), gather_layer(pp(own, "fsdp", n_z // 2))

    dy_mine = lax.dynamic_slice_in_dim(cotangent.reshape(half_len, width), t * rows, rows, 0)
    dy_pair = both(dy_mine)
    norm_pair = both(norm_ffn)

    def mlp(norm, dy):
        norm = norm.reshape(full_len, width)
        dy = dy.reshape(full_len, width)
        gate_up = dot(norm, w_gu)
        gate, up = gate_up[:, :units], gate_up[:, units:]
        sig = jax.nn.sigmoid(gate)
        hidden = (gate * sig * up).astype(BF16)
        d_hidden = dot(dy, w_dn, ((1,), (1,)))
        d_up = (d_hidden * gate * sig).astype(BF16)
        d_gate = (d_hidden * up * sig * (1.0 + gate * (1.0 - sig))).astype(BF16)
        return hidden, jnp.concatenate([d_gate, d_up], axis=1), norm, dy

    own_mlp, far_mlp = mlp(norm_pair[0], dy_pair[0]), mlp(norm_pair[1], dy_pair[1])

    def shape8(v):
        return v.reshape(2, 2, 2, rows, v.shape[-1])

    def scatter_both(own, far, rhs, dims=((1,), (0,))):
        sent = pp(scatter_layer(shape8(far), rhs, dims).astype(BF16), "fsdp", n_z // 2)
        return scatter_layer(shape8(own), rhs, dims) + sent.astype(F32)

    d_norm = scatter_both(own_mlp[1], far_mlp[1], w_gu, ((1,), (1,)))
    ffn = scatter_both(own_mlp[0], far_mlp[0], w_dn)
    output = gather_tp((mid + ffn).astype(BF16))

    gu_g = dot(own_mlp[2], own_mlp[1], ((0,), (0,))) + dot(far_mlp[2], far_mlp[1], ((0,), (0,)))
    dn_g = dot(own_mlp[0], own_mlp[3], ((0,), (0,))) + dot(far_mlp[0], far_mlp[3], ((0,), (0,)))

    def norm_back(inputs, root, gain, d_normed):
        scaled = d_normed * gain
        return root * scaled - inputs * (root * root * root) * jnp.mean(
            scaled * inputs, axis=1, keepdims=True
        )

    d_mid = dy_mine.astype(F32) + norm_back(mid, root_ffn, gain_two, d_norm)
    d_proj = gather_layer(d_mid.astype(BF16)).reshape(full_len, width)
    o_g = dot(attn_rel.reshape(full_len, q_cols), d_proj, ((0,), (0,)))
    d_attn = dot(d_proj, w_o, ((1,), (1,))).astype(BF16)
    d_attn = by_xor(d_attn, 2 * n_tp, me).reshape(full_len, q_cols)
    d_qkv = attend_back(rot, d_attn, stats, cos, sin, seg_col, seg_row, sel, scale)
    d_rel = by_xor(d_qkv, 2 * n_tp, me)
    d_norm_attn = scatter_layer(shape8(d_rel), w_heads, ((1,), (1,)))
    root_mine = lax.rsqrt(jnp.mean(x_mine * x_mine, axis=1, keepdims=True) + NORM_EPS)
    d_in = d_mid + norm_back(x_mine, root_mine, gain_one, d_norm_attn)
    input_grad = gather_tp(d_in.astype(BF16))
    d_packed = dot(d_qkv, spread, ((1,), (1,))).astype(BF16)
    in_g = dot(norm_attn, d_packed, ((0,), (0,)))

    def to_owner_y(blocks, rows_axis):
        mine, theirs = pick(blocks, y), pick(blocks, 1 - y)
        return in_order(y, mine, pp(theirs.astype(BF16), "ctx", 1).astype(F32))

    def half_z(blocks):
        top = n_z // 2
        left = scatter_z(blocks, top)
        return in_order(zb, left[0], pp(left[top].astype(BF16), "fsdp", top).astype(F32))

    gu_two = half_z(split_z(gu_g, n_z, z, 0))
    gu_four = to_owner_y(gu_two.reshape(2, 2, depth, 2 * units).transpose(1, 0, 2, 3), 0)
    gu_four = gu_four.transpose(2, 1, 0, 3)
    gate_grad = gu_four[..., :units].reshape(depth, 4 * units)
    up_grad = gu_four[..., units:].reshape(depth, 4 * units)

    dn_two = half_z(split_z(dn_g, n_z, z, 1))
    dn_four = to_owner_y(dn_two.reshape(2, units, 2, depth).transpose(2, 0, 1, 3), 1)
    down_grad = dn_four.transpose(1, 0, 2, 3).reshape(4 * units, depth)

    o_one = scatter_z(split_z(o_g, n_z, z, 1), n_z)[0]
    o_grad = to_owner_y(o_one.reshape(q_cols, 2, depth).transpose(1, 0, 2), 1).reshape(
        2 * q_cols, depth
    )

    in_one = scatter_z(split_z(in_g, n_z, z, 0), n_z)[0]
    in_two = to_owner_y(in_one.reshape(2, depth, compact), 0)

    def columns(lo, hi):
        return jnp.concatenate([in_two[0, :, lo:hi], in_two[1, :, lo:hi]], axis=1)

    q_grad = columns(0, q_cols)
    k_grad = columns(q_cols, q_cols + kv_cols)
    v_grad = columns(q_cols + kv_cols, q_cols + 2 * kv_cols)

    def gain_sum(pairs):
        return sum(jnp.sum(w.astype(F32) * g, axis=1) for w, g in pairs)

    gains = sum_tp(
        jnp.stack(
            [
                gain_sum(((q_weight, q_grad), (k_weight, k_grad), (v_weight, v_grad))),
                gain_sum(((gate_weight, gate_grad), (up_weight, up_grad))),
            ]
        )
    ) / jnp.stack([attn_gain, ffn_gain]).astype(F32)

    return (
        output[None],
        input_grad[None],
        gains[0],
        q_grad,
        k_grad,
        v_grad,
        o_grad,
        gains[1],
        gate_grad,
        up_grad,
        down_grad,
    )


def solution(mesh):
    specs = dict(
        tok=P("fsdp", "ctx", None),
        gain=P(("fsdp", "ctx")),
        row=P(("fsdp", "ctx"), "tp"),
        col=P("tp", ("fsdp", "ctx")),
    )
    tok, gain, row, col = specs["tok"], specs["gain"], specs["row"], specs["col"]
    return jax.shard_map(
        body,
        mesh=mesh,
        in_specs=(tok, P("fsdp", None), gain, row, row, row, col, gain, row, row, col, tok),
        out_specs=(tok, tok, gain, row, row, row, col, gain, row, row, col),
        check_vma=False,
    )
```

time: 2320 us -> 1080 us (0.47)
  waiting for transfers between devices: 1700 us -> 500 us
  blocking collectives: 181 us -> 0 us
  local copies, waits for them, and re-layouts: 110 us -> 192 us
  starting transfers between devices: 21.1 us -> 94.5 us
  matrix products: 184 us -> 119 us
  other arithmetic: 97.9 us -> 136 us
  Pallas kernels: 0 us -> 27.6 us
    reduce_scatter x5 -> x0, waiting for transfers between devices: 928 us -> none  [the longest x1 310 us: body(): lax.psum_scatter(up_grad, ('fsdp', 'ctx'), scatter_dimension=0, tiled=True)]
    ppermute x0 -> x99, waiting for transfers between devices: none -> 500 us  [pp(): return lax.ppermute(value, axis, [(i, i ^ mask) for i in range(size)])]
    psum x3 -> x0, waiting for transfers between devices: 384 us -> none  [reduce_all(): return lax.psum(value_in, 'tp')]
    all_gather x5 -> x0, waiting for transfers between devices: 378 us -> none  [the longest x1 130 us: body(): lax.all_gather(up_weight, ('fsdp', 'ctx'), axis=0, tiled=True)]
    ppermute x0 -> x99, starting transfers between devices: none -> 94.5 us  [pp(): return lax.ppermute(value, axis, [(i, i ^ mask) for i in range(size)])]
    unnamed x2 -> x0, blocking collectives: 77.4 us -> none
    all_gather x2 -> x0, blocking collectives: 69.5 us -> none  [the longest x1 35.3 us: body(): lax.all_gather(k_weight, ('fsdp', 'ctx'), axis=0, tiled=True)]
    dot_general x31 -> x25, matrix products: 178 us -> 119 us  [dot(): return lax.dot_general(a, b, (dims, ((), ())), preferred_element_type=F32)]
  transfers between devices with their start and end apart: 20 -> 99, of which waited for: 13 -> 45; matrix products, arithmetic and copies ran while one was open for 12% -> 40% of each run, Pallas kernels for 0% -> 3%
where the time goes in v1:
time: 1080 us; the launch traced here: 1070 us
  waiting for transfers between devices  500 us (46%)
  local copies, waits for them, and re-layouts  192 us (18%)
  other arithmetic  136 us (13%)
  matrix products  119 us (11%)
  starting transfers between devices  94.5 us (9%)
  Pallas kernels  27.6 us (3%)
    ppermute x99, waiting for transfers between devices, pp(): return lax.ppermute(value, axis, [(i, i ^ mask) for i in range(size)])  500 us
    dot_general x25, matrix products, dot(): return lax.dot_general(a, b, (dims, ((), ())), preferred_element_type=F32)  119 us
    ppermute x99, starting transfers between devices, pp(): return lax.ppermute(value, axis, [(i, i ^ mask) for i in range(size)])  94.5 us
    select_n x15, other arithmetic, in_order(): jnp.where(bit == 0, jnp.stack([mine, other], axis), jnp.stack([other, min...  35.6 us
    unnamed x238, local copies, waits for them, and re-layouts  27.4 us
    another operation x10, other arithmetic, gather_layer(): return jnp.stack([mine, pp(mine, 'tp', 1)], axis=2)  27.3 us
  transfers between devices with their start and end apart: 99, of which 45 were waited for; matrix products, arithmetic and copies ran while one was open for 40% of the time, Pallas kernels for 3%

profile of v1, /device:TPU:0, one launch (start us, length us, event | category | flops | bytes accessed | tf_op | source)
XLA Modules:
  0.0 1072.3 jit_solution(155396701758611242)
XLA Ops:
  25.9 4.9 reshape.592
  30.8 16.7 %collective-permute-done.6 = bf16[320,320]{1,0:T(8,128)(2,1)} collective-permute-done((bf16[320,320]{1,0:T(8,128)(2,1)S(1)}, bf16[320,320]{1,0:T(8,128)(2,1)}, u32[]{:S(2)}, u32[]{:S(2)}) %collective-permute-start.6) | collective-permute-done | bytes 204832 | tf_op jit(solution)/shard_map/ppermute | solution.py:22
  60.5 4.2 constant_dynamic-slice_fusion.4
  65.7 5.7 reshape.589
  71.4 5.6 reshape.590
  79.4 16.2 %collective-permute-done.3 = bf16[640,512]{1,0:T(8,128)(2,1)} collective-permute-done((bf16[640,512]{1,0:T(8,128)(2,1)}, bf16[640,512]{1,0:T(8,128)(2,1)}, u32[]{:S(2)}, u32[]{:S(2)}) %collective-permute-start.3) | collective-permute-done | bytes 655392 | tf_op jit(solution)/shard_map/ppermute | solution.py:22
  95.9 7.4 collective-permute-done.7
  115.6 26.0 %collective-permute-done.9 = bf16[320,640]{1,0:T(8,128)(2,1)} collective-permute-done((bf16[320,640]{1,0:T(8,128)(2,1)}, bf16[320,640]{1,0:T(8,128)(2,1)}, u32[]{:S(2)}, u32[]{:S(2)}) %collective-permute-start.9) | collective-permute-done | bytes 409632 | tf_op jit(solution)/shard_map/ppermute | solution.py:22
  148.8 6.0 convolution_convert_fusion
  164.7 9.6 fusion.152.refs_0_
  174.3 12.0 %attend.1 = (bf16[1024,320]{1,0:T(8,128)(2,1)}, bf16[1024,768]{1,0:T(8,128)(2,1)}, f32[1024,8]{1,0:T(8,128)}) custom-call(f32[1024,768]{1,0:T(8,128)} %fusion.152.refs_0_, f32[1024,128]{1,0:T(8,128)} %get-tuple-element.234.refs_1_.refs_3_, f32[1024,128]{1,0:T(8,128)} %get-tuple-element.233.refs_2_.refs_4_, s32[1024,1]{1,0:T(8,128)} %copy.585.refs_3_.refs_5_, ...), custom_call_target="tpu_custom_call" | custom-call | flops 1073741824 | bytes 4718592 | tf_op jit(solution)/shard_map/attend/pallas_call | solution.py:113
  198.2 11.3 %dynamic-slice_maximum_fusion.1 = (bf16[2,1,320,864]{3,1,0,2:T(2,128)(2,1)}, bf16[2,1,320,864]{3,1,0,2:T(2,128)(2,1)S(1)}) fusion(s32[]{:T(128)S(6)} %select_n.441, bf16[2,2,320,432]{3,1,0,2:T(2,128)(2,1)S(1)} %bitcast.545, bf16[2,2,320,432]{3,1,0,2:T(2,128)(2,1)S(1)} %bitcast.544, s32[]{:T(128)S(6)} %select_n.442), kind=kLoop, calls=%fused_computation.55 | loop fusion | flops 4423680 | bytes 4423688 | tf_op jit(solution)/shard_map/concatenate | solution.py:289
  229.8 16.3 %collective-permute-done.58 = bf16[128,1280]{1,0:T(8,128)(2,1)S(1)} collective-permute-done((bf16[128,1280]{1,0:T(8,128)(2,1)S(1)}, bf16[128,1280]{1,0:T(8,128)(2,1)S(1)}, u32[]{:S(2)}, u32[]{:S(2)}) %collective-permute-start.58) | collective-permute-done | bytes 327712 | tf_op jit(solution)/shard_map/ppermute | solution.py:22
  250.0 8.6 collective-permute-done.48
  275.4 11.4 %collective-permute-done.11 = bf16[2,128,1280]{2,1,0:T(8,128)(2,1)S(1)} collective-permute-done((bf16[2,128,1280]{2,1,0:T(8,128)(2,1)S(1)}, bf16[2,128,1280]{2,1,0:T(8,128)(2,1)S(1)}, u32[]{:S(2)}, u32[]{:S(2)}) %collective-permute-start.11) | collective-permute-done | bytes 655392 | tf_op jit(solution)/shard_map/ppermute | solution.py:22
  287.5 13.4 %collective-permute-done.13 = bf16[2,128,1280]{2,1,0:T(8,128)(2,1)S(1)} collective-permute-done((bf16[2,128,1280]{2,1,0:T(8,128)(2,1)S(1)}, bf16[2,128,1280]{2,1,0:T(8,128)(2,1)S(1)}, u32[]{:S(2)}, u32[]{:S(2)}) %collective-permute-start.13) | collective-permute-done | bytes 655392 | tf_op jit(solution)/shard_map/ppermute | solution.py:22
  301.6 6.4 collective-permute-done.12
  308.6 8.3 collective-permute-done.14
  321.3 10.6 broadcast_select_fusion
  337.2 5.9 collective-permute-start.21
  345.8 6.0 collective-permute-done.17
  356.3 28.2 %collective-permute-done.27 = bf16[432,640]{1,0:T(8,128)(2,1)S(1)} collective-permute-done((bf16[432,640]{1,0:T(8,128)(2,1)}, bf16[432,640]{1,0:T(8,128)(2,1)S(1)}, u32[]{:S(2)}, u32[]{:S(2)}) %collective-permute-start.27) | collective-permute-done | bytes 552992 | tf_op jit(solution)/shard_map/ppermute | solution.py:22
  390.8 33.8 %collective-permute-done.33 = bf16[128,2560]{1,0:T(8,128)(2,1)S(1)} collective-permute-done((bf16[128,2560]{1,0:T(8,128)(2,1)S(1)}, bf16[128,2560]{1,0:T(8,128)(2,1)S(1)}, u32[]{:S(2)}, u32[]{:S(2)}) %collective-permute-start.33) | collective-permute-done | bytes 655392 | tf_op jit(solution)/shard_map/ppermute | solution.py:22
  428.9 21.4 %collective-permute-done.23 = bf16[640,864]{0,1:T(8,128)(2,1)S(1)} collective-permute-done((bf16[640,864]{0,1:T(8,128)(2,1)S(1)}, bf16[640,864]{0,1:T(8,128)(2,1)S(1)}, u32[]{:S(2)}, u32[]{:S(2)}) %collective-permute-start.23) | collective-permute-done | bytes 1105952 | tf_op jit(solution)/shard_map/ppermute | solution.py:22
  452.7 8.2 collective-permute-done.36
  481.6 4.7 fusion.153
  486.4 4.5 multiply_convert_fusion.3
  500.7 5.7 reshape.596
  506.4 6.4 fusion.146
  512.8 6.6 convolution_convert_fusion.3
  519.5 7.9 fusion.137
  530.9 4.7 fusion.154
  551.2 5.5 reshape.598
  556.7 10.2 convolution_add_fusion
  574.7 6.4 convolution_convert_fusion.2
  593.7 18.5 %collective-permute-done.85 = bf16[640,864]{0,1:T(8,128)(2,1)} collective-permute-done((bf16[640,864]{0,1:T(8,128)(2,1)}, bf16[640,864]{0,1:T(8,128)(2,1)}, u32[]{:S(2)}, u32[]{:S(2)}) %collective-permute-start.85) | collective-permute-done | bytes 1105952 | tf_op jit(solution)/shard_map/ppermute | solution.py:22
  612.2 22.1 %collective-permute-done.86 = bf16[640,864]{0,1:T(8,128)(2,1)} collective-permute-done((bf16[640,864]{0,1:T(8,128)(2,1)}, bf16[640,864]{0,1:T(8,128)(2,1)}, u32[]{:S(2)}, u32[]{:S(2)}) %collective-permute-start.86) | collective-permute-done | bytes 1105952 | tf_op jit(solution)/shard_map/ppermute | solution.py:22
  634.3 5.0 convert_add_fusion.7
  643.0 4.3 convert_add_fusion.4
  650.4 4.7 convert_add_fusion.2
  655.3 9.3 collective-permute-done.29
  673.3 5.1 convert_add_fusion.1
  685.4 5.3 collective-permute-done.30
  692.7 17.7 %collective-permute-done.54 = bf16[128,1280]{1,0:T(8,128)(2,1)S(1)} collective-permute-done((bf16[128,1280]{1,0:T(8,128)(2,1)S(1)}, bf16[128,1280]{1,0:T(8,128)(2,1)S(1)}, u32[]{:S(2)}, u32[]{:S(2)}) %collective-permute-start.54) | collective-permute-done | bytes 327712 | tf_op jit(solution)/shard_map/ppermute | solution.py:22
  713.4 12.2 %collective-permute-done.64 = bf16[2,128,1280]{2,1,0:T(8,128)(2,1)S(1)} collective-permute-done((bf16[2,128,1280]{2,1,0:T(8,128)(2,1)S(1)}, bf16[2,128,1280]{2,1,0:T(8,128)(2,1)S(1)}, u32[]{:S(2)}, u32[]{:S(2)}) %collective-permute-start.64) | collective-permute-done | bytes 655392 | tf_op jit(solution)/shard_map/ppermute | solution.py:22
  730.3 9.7 collective-permute-done.65
  741.6 5.5 collective-permute-done.67
  750.6 37.7 %collective-permute-done.68 = bf16[128,2560]{1,0:T(8,128)(2,1)S(1)} collective-permute-done((bf16[128,2560]{1,0:T(8,128)(2,1)S(1)}, bf16[128,2560]{1,0:T(8,128)(2,1)S(1)}, u32[]{:S(2)}, u32[]{:S(2)}) %collective-permute-start.68) | collective-permute-done | bytes 655392 | tf_op jit(solution)/shard_map/ppermute | solution.py:22
  788.6 13.6 %collective-permute-done.44 = bf16[128,2560]{1,0:T(8,128)(2,1)S(1)} collective-permute-done((bf16[128,2560]{1,0:T(8,128)(2,1)S(1)}, bf16[128,2560]{1,0:T(8,128)(2,1)S(1)}, u32[]{:S(2)}, u32[]{:S(2)}) %collective-permute-start.44) | collective-permute-done | bytes 655392 | tf_op jit(solution)/shard_map/ppermute | solution.py:22
  821.2 12.2 %collective-permute-done.71 = bf16[128,1280]{1,0:T(8,128)(2,1)S(1)} collective-permute-done((bf16[128,1280]{1,0:T(8,128)(2,1)}, bf16[128,1280]{1,0:T(8,128)(2,1)S(1)}, u32[]{:S(2)}, u32[]{:S(2)}) %collective-permute-start.71) | collective-permute-done | bytes 327712 | tf_op jit(solution)/shard_map/ppermute | solution.py:22
  846.4 4.9 reshape.609
  857.1 13.8 %collective-permute-done.88 = bf16[2,320,864]{2,0,1:T(2,128)(2,1)} collective-permute-done((bf16[2,320,864]{2,0,1:T(2,128)(2,1)}, bf16[2,320,864]{2,0,1:T(2,128)(2,1)}, u32[]{:S(2)}, u32[]{:S(2)}) %collective-permute-start.88) | collective-permute-done | bytes 1105952 | tf_op jit(solution)/shard_map/ppermute | solution.py:22
  882.7 4.6 reshape.606
  890.1 5.1 reshape.605
  909.2 15.6 %attend_back.1 = bf16[1024,768]{1,0:T(8,128)(2,1)} custom-call(bf16[1024,768]{1,0:T(8,128)(2,1)} %get-tuple-element.15.refs_0_, bf16[1024,320]{1,0:T(8,128)(2,1)} %bitcast.605, f32[1024,8]{1,0:T(8,128)} %get-tuple-element.16.refs_2_, f32[1024,128]{1,0:T(8,128)} %get-tuple-element.234.refs_1_.refs_3_, f32[1024,128]{1,0:T(8,128)} %get-tuple-element.233.refs_2_.refs_4_, ...), custom_call_target="tpu_custom_call" | custom-call | flops 2684354560 | bytes 4718592 | tf_op jit(solution)/shard_map/attend_back/pallas_call | solution.py:133
  924.8 9.1 fusion.58
  962.9 19.2 %collective-permute-done.91 = bf16[320,640]{1,0:T(8,128)(2,1)S(1)} collective-permute-done((bf16[320,640]{1,0:T(8,128)(2,1)S(1)}, bf16[320,640]{1,0:T(8,128)(2,1)S(1)}, u32[]{:S(2)}, u32[]{:S(2)}) %collective-permute-start.91) | collective-permute-done | bytes 409632 | tf_op jit(solution)/shard_map/ppermute | solution.py:22
  986.4 9.4 collective-permute-done.81
  995.8 7.2 collective-permute-done.83
  1008.7 6.8 collective-permute-done.84
  1027.3 7.2 collective-permute-done.75
  1040.3 5.3 collective-permute-done.76
  1045.6 4.9 collective-permute-done.78
  1053.8 8.4 collective-permute-done.79
  (650 shorter events, 397.7 us)
Async XLA Ops:
  3.2 100.6 %collective-permute-start = (bf16[256,2560]{1,0:T(8,128)(2,1)}, bf16[256,2560]{1,0:T(8,128)(2,1)}, u32[]{:S(2)}, u32[]{:S(2)}) collective-permute-start(bf16[256,2560]{1,0:T(8,128)(2,1)} %dynamic-slice_bitcast_fusion.2), channel_id=1, source_target_pairs={{0,4},{4,0},{1,5},{5,1},{2,6},{6,2},{3,7},{7,3},{8,12},{12,8},{9,1... | collective-permute-start | bytes 3932168 | tf_op jit(solution)/shard_map/ppermute | solution.py:22
  12.0 36.8 %collective-permute-start.2 = (bf16[320,512]{1,0:T(8,128)(2,1)}, bf16[320,512]{1,0:T(8,128)(2,1)}, u32[]{:S(2)}, u32[]{:S(2)}) collective-permute-start(bf16[320,512]{1,0:T(8,128)(2,1)} %bitcast.508), channel_id=1, source_target_pairs={{0,4},{4,0},{1,5},{5,1},{2,6},{6,2},{3,7},{7,3},{8,12},{12,8},{9,1... | collective-permute-start | bytes 983048 | tf_op jit(solution)/shard_map/ppermute | solution.py:22
  14.3 33.2 %collective-permute-start.6 = (bf16[320,320]{1,0:T(8,128)(2,1)S(1)}, bf16[320,320]{1,0:T(8,128)(2,1)}, u32[]{:S(2)}, u32[]{:S(2)}) collective-permute-start(bf16[320,320]{1,0:T(8,128)(2,1)S(1)} %bitcast.601), channel_id=1, source_target_pairs={{0,4},{4,0},{1,5},{5,1},{2,6},{6,2},{3,7},{7,3},{8,12},{12,8},{9,1... | collective-permute-start | bytes 614408 | tf_op jit(solution)/shard_map/ppermute | solution.py:22
  54.4 41.1 %collective-permute-start.3 = (bf16[640,512]{1,0:T(8,128)(2,1)}, bf16[640,512]{1,0:T(8,128)(2,1)}, u32[]{:S(2)}, u32[]{:S(2)}) collective-permute-start(bf16[640,512]{1,0:T(8,128)(2,1)} %bitcast.13), channel_id=1, source_target_pairs={{0,16},{8,24},{16,0},{24,8},{1,17},{9,25},{17,1},{25,9},{2,18},{10... | collective-permute-start | bytes 1966088 | tf_op jit(solution)/shard_map/ppermute | solution.py:22
  58.4 44.9 %collective-permute-start.7 = (bf16[320,640]{1,0:T(8,128)(2,1)}, bf16[320,640]{1,0:T(8,128)(2,1)}, u32[]{:S(2)}, u32[]{:S(2)}) collective-permute-start(bf16[320,640]{1,0:T(8,128)(2,1)} %get-tuple-element.109), channel_id=1, source_target_pairs={{0,16},{8,24},{16,0},{24,8},{1,17},{9,25},{17,1},{25,9},{2,18},{10... | collective-permute-start | bytes 1228808 | tf_op jit(solution)/shard_map/ppermute | solution.py:22
  58.5 46.4 %collective-permute-start.8 = (bf16[320,640]{1,0:T(8,128)(2,1)}, bf16[320,640]{1,0:T(8,128)(2,1)}, u32[]{:S(2)}, u32[]{:S(2)}) collective-permute-start(bf16[320,640]{1,0:T(8,128)(2,1)} %get-tuple-element.109), channel_id=1, source_target_pairs={{0,8},{8,0},{16,24},{24,16},{1,9},{9,1},{17,25},{25,17},{2,10},{10... | collective-permute-start | bytes 1228808 | tf_op jit(solution)/shard_map/ppermute | solution.py:22
  60.3 50.6 %collective-permute-start.4 = (bf16[640,512]{1,0:T(8,128)(2,1)}, bf16[640,512]{1,0:T(8,128)(2,1)}, u32[]{:S(2)}, u32[]{:S(2)}) collective-permute-start(bf16[640,512]{1,0:T(8,128)(2,1)} %bitcast.13), channel_id=1, source_target_pairs={{0,8},{8,0},{16,24},{24,16},{1,9},{9,1},{17,25},{25,17},{2,10},{10... | collective-permute-start | bytes 1966088 | tf_op jit(solution)/shard_map/ppermute | solution.py:22
  95.6 48.4 %collective-permute-start.5 = (bf16[640,512]{1,0:T(8,128)(2,1)}, bf16[640,512]{1,0:T(8,128)(2,1)}, u32[]{:S(2)}, u32[]{:S(2)}) collective-permute-start(bf16[640,512]{1,0:T(8,128)(2,1)} %collective-permute-done.3), channel_id=1, source_target_pairs={{0,8},{8,0},{16,24},{24,16},{1,9},{9,1},{17,25},{25,17},{2,10},{10... | collective-permute-start | bytes 1966088 | tf_op jit(solution)/shard_map/ppermute | solution.py:22
  103.3 38.3 %collective-permute-start.9 = (bf16[320,640]{1,0:T(8,128)(2,1)}, bf16[320,640]{1,0:T(8,128)(2,1)}, u32[]{:S(2)}, u32[]{:S(2)}) collective-permute-start(bf16[320,640]{1,0:T(8,128)(2,1)} %collective-permute-done.7), channel_id=1, source_target_pairs={{0,8},{8,0},{16,24},{24,16},{1,9},{9,1},{17,25},{25,17},{2,10},{10... | collective-permute-start | bytes 1228808 | tf_op jit(solution)/shard_map/ppermute | solution.py:22
  103.8 50.9 %collective-permute-start.1 = (bf16[256,2560]{1,0:T(8,128)(2,1)}, bf16[256,2560]{1,0:T(8,128)(2,1)}, u32[]{:S(2)}, u32[]{:S(2)}) collective-permute-start(bf16[256,2560]{1,0:T(8,128)(2,1)} %collective-permute-done), channel_id=1, source_target_pairs={{0,1},{1,0},{2,3},{3,2},{4,5},{5,4},{6,7},{7,6},{8,9},{9,8},{10,11... | collective-permute-start | bytes 3932168 | tf_op jit(solution)/shard_map/ppermute | solution.py:22
  104.9 119.8 %collective-permute-start.57 = (bf16[128,2560]{1,0:T(8,128)(2,1)}, bf16[128,2560]{1,0:T(8,128)(2,1)}, u32[]{:S(2)}, u32[]{:S(2)}) collective-permute-start(bf16[128,2560]{1,0:T(8,128)(2,1)} %dynamic-slice_bitcast_fusion.3), channel_id=1, source_target_pairs={{0,16},{8,24},{16,0},{24,8},{1,17},{9,25},{17,1},{25,9},{2,18},{10... | collective-permute-start | bytes 1966088 | tf_op jit(solution)/shard_map/ppermute | solution.py:22
  110.9 111.5 %collective-permute-start.24 = (bf16[2,432,320]{1,2,0:T(8,128)(2,1)}, bf16[2,432,320]{1,2,0:T(8,128)(2,1)}, u32[]{:S(2)}, u32[]{:S(2)}) collective-permute-start(bf16[2,432,320]{1,2,0:T(8,128)(2,1)} %bitcast.504), channel_id=1, source_target_pairs={{0,4},{4,0},{1,5},{5,1},{2,6},{6,2},{3,7},{7,3},{8,12},{12,8},{9,1... | collective-permute-start | bytes 1658888 | tf_op jit(solution)/shard_map/ppermute | solution.py:22
  141.6 74.9 %collective-permute-start.47 = (bf16[128,1280]{1,0:T(8,128)(2,1)}, bf16[128,1280]{1,0:T(8,128)(2,1)}, u32[]{:S(2)}, u32[]{:S(2)}) collective-permute-start(bf16[128,1280]{1,0:T(8,128)(2,1)} %get-tuple-element.196), channel_id=1, source_target_pairs={{0,2},{1,3},{2,0},{3,1},{4,6},{5,7},{6,4},{7,5},{8,10},{9,11},{10,... | collective-permute-start | bytes 983048 | tf_op jit(solution)/shard_map/ppermute | solution.py:22
  144.0 74.9 %collective-permute-start.49 = (bf16[128,1280]{1,0:T(8,128)(2,1)}, bf16[128,1280]{1,0:T(8,128)(2,1)}, u32[]{:S(2)}, u32[]{:S(2)}) collective-permute-start(bf16[128,1280]{1,0:T(8,128)(2,1)} %get-tuple-element.195), channel_id=1, source_target_pairs={{0,4},{4,0},{1,5},{5,1},{2,6},{6,2},{3,7},{7,3},{8,12},{12,8},{9,1... | collective-permute-start | bytes 983048 | tf_op jit(solution)/shard_map/ppermute | solution.py:22
  198.1 64.7 %collective-permute-start.10 = (bf16[2,2,128,2560]{3,2,1,0:T(8,128)(2,1)}, bf16[2,2,128,2560]{3,2,1,0:T(8,128)(2,1)}, u32[]{:S(2)}, u32[]{:S(2)}) collective-permute-start(bf16[2,2,128,2560]{3,2,1,0:T(8,128)(2,1)} %convolution_convert_fusion.6), channel_id=1, source_target_pairs={{0,1},{1,0},{2,3},{3,2},{4,5},{5,4},{6,7},{7,6},{8,9},{9,8},{10,11... | collective-permute-start | bytes 7864328 | tf_op jit(solution)/shard_map/ppermute | solution.py:22
  216.5 54.3 %collective-permute-start.20 = (bf16[2,320,864]{2,1,0:T(8,128)(2,1)}, bf16[2,320,864]{2,1,0:T(8,128)(2,1)}, u32[]{:S(2)}, u32[]{:S(2)}) collective-permute-start(bf16[2,320,864]{2,1,0:T(8,128)(2,1)} %bitcast.578), channel_id=1, source_target_pairs={{0,4},{4,0},{1,5},{5,1},{2,6},{6,2},{3,7},{7,3},{8,12},{12,8},{9,1... | collective-permute-start | bytes 3317768 | tf_op jit(solution)/shard_map/ppermute | solution.py:22
  218.9 39.6 %collective-permute-start.48 = (bf16[2,128,1280]{2,1,0:T(8,128)(2,1)}, bf16[2,128,1280]{2,1,0:T(8,128)(2,1)}, u32[]{:S(2)}, u32[]{:S(2)}) collective-permute-start(bf16[2,128,1280]{2,1,0:T(8,128)(2,1)} %get-tuple-element.192), channel_id=1, source_target_pairs={{0,4},{4,0},{1,5},{5,1},{2,6},{6,2},{3,7},{7,3},{8,12},{12,8},{9,1... | collective-permute-start | bytes 1966088 | tf_op jit(solution)/shard_map/ppermute | solution.py:22
  222.3 36.2 %collective-permute-start.50 = (bf16[2,128,1280]{2,1,0:T(8,128)(2,1)}, bf16[2,128,1280]{2,1,0:T(8,128)(2,1)}, u32[]{:S(2)}, u32[]{:S(2)}) collective-permute-start(bf16[2,128,1280]{2,1,0:T(8,128)(2,1)} %get-tuple-element.198), channel_id=1, source_target_pairs={{0,2},{1,3},{2,0},{3,1},{4,6},{5,7},{6,4},{7,5},{8,10},{9,11},{10,... | collective-permute-start | bytes 1966088 | tf_op jit(solution)/shard_map/ppermute | solution.py:22
  246.1 91.1 %collective-permute-start.25 = (bf16[432,640]{1,0:T(8,128)(2,1)}, bf16[432,640]{1,0:T(8,128)(2,1)}, u32[]{:S(2)}, u32[]{:S(2)}) collective-permute-start(bf16[432,640]{1,0:T(8,128)(2,1)} %fusion.80), channel_id=1, source_target_pairs={{0,16},{8,24},{16,0},{24,8},{1,17},{9,25},{17,1},{25,9},{2,18},{10... | collective-permute-start | bytes 1658888 | tf_op jit(solution)/shard_map/ppermute | solution.py:22
  258.5 86.9 %collective-permute-start.26 = (bf16[432,640]{1,0:T(8,128)(2,1)}, bf16[432,640]{1,0:T(8,128)(2,1)}, u32[]{:S(2)}, u32[]{:S(2)}) collective-permute-start(bf16[432,640]{1,0:T(8,128)(2,1)} %get-tuple-element.107), channel_id=1, source_target_pairs={{0,8},{8,0},{16,24},{24,16},{1,9},{9,1},{17,25},{25,17},{2,10},{10... | collective-permute-start | bytes 1658888 | tf_op jit(solution)/shard_map/ppermute | solution.py:22
  262.8 82.9 %collective-permute-start.59 = (bf16[2,128,1280]{2,1,0:T(8,128)(2,1)}, bf16[2,128,1280]{2,1,0:T(8,128)(2,1)}, u32[]{:S(2)}, u32[]{:S(2)}) collective-permute-start(bf16[2,128,1280]{2,1,0:T(8,128)(2,1)} %get-tuple-element.200), channel_id=1, source_target_pairs={{0,4},{4,0},{1,5},{5,1},{2,6},{6,2},{3,7},{7,3},{8,12},{12,8},{9,1... | collective-permute-start | bytes 1966088 | tf_op jit(solution)/shard_map/ppermute | solution.py:22
  270.8 81.0 %collective-permute-start.61 = (bf16[2,128,1280]{2,1,0:T(8,128)(2,1)}, bf16[2,128,1280]{2,1,0:T(8,128)(2,1)}, u32[]{:S(2)}, u32[]{:S(2)}) collective-permute-start(bf16[2,128,1280]{2,1,0:T(8,128)(2,1)} %get-tuple-element.206), channel_id=1, source_target_pairs={{0,2},{1,3},{2,0},{3,1},{4,6},{5,7},{6,4},{7,5},{8,10},{9,11},{10,... | collective-permute-start | bytes 1966088 | tf_op jit(solution)/shard_map/ppermute | solution.py:22
  337.2 48.4 %collective-permute-start.21 = (bf16[640,864]{0,1:T(8,128)(2,1)}, bf16[640,864]{0,1:T(8,128)(2,1)S(1)}, u32[]{:S(2)}, u32[]{:S(2)}) collective-permute-start(bf16[640,864]{0,1:T(8,128)(2,1)} %bitcast.579), channel_id=1, source_target_pairs={{0,16},{8,24},{16,0},{24,8},{1,17},{9,25},{17,1},{25,9},{2,18},{10... | collective-permute-start | bytes 3317768 | tf_op jit(solution)/shard_map/ppermute | solution.py:22
  345.8 116.8 %collective-permute-start.51 = (bf16[2,2,128,2560]{3,2,0,1:T(8,128)(2,1)S(1)}, bf16[2,2,128,2560]{3,2,0,1:T(8,128)(2,1)S(1)}, u32[]{:S(2)}, u32[]{:S(2)}) collective-permute-start(bf16[2,2,128,2560]{3,2,0,1:T(8,128)(2,1)S(1)} %copy-done.37), channel_id=1, source_target_pairs={{0,1},{1,0},{2,3},{3,2},{4,5},{5,4},{6,7},{7,6},{8,9},{9,8},{10,11... | collective-permute-start | bytes 7864328 | tf_op jit(solution)/shard_map/ppermute | solution.py:22
  345.8 38.7 %collective-permute-start.27 = (bf16[432,640]{1,0:T(8,128)(2,1)}, bf16[432,640]{1,0:T(8,128)(2,1)S(1)}, u32[]{:S(2)}, u32[]{:S(2)}) collective-permute-start(bf16[432,640]{1,0:T(8,128)(2,1)} %collective-permute-done.25), channel_id=1, source_target_pairs={{0,8},{8,0},{16,24},{24,16},{1,9},{9,1},{17,25},{25,17},{2,10},{10... | collective-permute-start | bytes 1658888 | tf_op jit(solution)/shard_map/ppermute | solution.py:22
  351.7 34.0 %collective-permute-start.16 = (bf16[2,128,1280]{2,1,0:T(8,128)(2,1)S(1)}, bf16[2,128,1280]{2,1,0:T(8,128)(2,1)S(1)}, u32[]{:S(2)}, u32[]{:S(2)}) collective-permute-start(bf16[2,128,1280]{2,1,0:T(8,128)(2,1)S(1)} %get-tuple-element.216), channel_id=1, source_target_pairs={{0,4},{4,0},{1,5},{5,1},{2,6},{6,2},{3,7},{7,3},{8,12},{12,8},{9,1... | collective-permute-start | bytes 1966088 | tf_op jit(solution)/shard_map/ppermute | solution.py:22
  351.8 35.2 %collective-permute-start.18 = (bf16[2,128,1280]{2,1,0:T(8,128)(2,1)S(1)}, bf16[2,128,1280]{2,1,0:T(8,128)(2,1)S(1)}, u32[]{:S(2)}, u32[]{:S(2)}) collective-permute-start(bf16[2,128,1280]{2,1,0:T(8,128)(2,1)S(1)} %get-tuple-element.222), channel_id=1, source_target_pairs={{0,2},{1,3},{2,0},{3,1},{4,6},{5,7},{6,4},{7,5},{8,10},{9,11},{10,... | collective-permute-start | bytes 1966088 | tf_op jit(solution)/shard_map/ppermute | solution.py:22
  384.5 78.9 %collective-permute-start.62 = (bf16[2,2,128,2560]{3,2,0,1:T(8,128)(2,1)}, bf16[2,2,128,2560]{3,2,0,1:T(8,128)(2,1)}, u32[]{:S(2)}, u32[]{:S(2)}) collective-permute-start(bf16[2,2,128,2560]{3,2,0,1:T(8,128)(2,1)} %get-tuple-element.145), channel_id=1, source_target_pairs={{0,1},{1,0},{2,3},{3,2},{4,5},{5,4},{6,7},{7,6},{8,9},{9,8},{10,11... | collective-permute-start | bytes 7864328 | tf_op jit(solution)/shard_map/ppermute | solution.py:22
  385.7 41.3 %collective-permute-start.22 = (bf16[640,864]{0,1:T(8,128)(2,1)S(1)}, bf16[640,864]{0,1:T(8,128)(2,1)S(1)}, u32[]{:S(2)}, u32[]{:S(2)}) collective-permute-start(bf16[640,864]{0,1:T(8,128)(2,1)S(1)} %bitcast.546), channel_id=1, source_target_pairs={{0,8},{8,0},{16,24},{24,16},{1,9},{9,1},{17,25},{25,17},{2,10},{10... | collective-permute-start | bytes 3317768 | tf_op jit(solution)/shard_map/ppermute | solution.py:22
  385.8 38.8 %collective-permute-start.33 = (bf16[128,2560]{1,0:T(8,128)(2,1)S(1)}, bf16[128,2560]{1,0:T(8,128)(2,1)S(1)}, u32[]{:S(2)}, u32[]{:S(2)}) collective-permute-start(bf16[128,2560]{1,0:T(8,128)(2,1)S(1)} %copy-done.36), channel_id=1, source_target_pairs={{0,16},{8,24},{16,0},{24,8},{1,17},{9,25},{17,1},{25,9},{2,18},{10... | collective-permute-start | bytes 1966088 | tf_op jit(solution)/shard_map/ppermute | solution.py:22
  387.1 63.2 %collective-permute-start.23 = (bf16[640,864]{0,1:T(8,128)(2,1)S(1)}, bf16[640,864]{0,1:T(8,128)(2,1)S(1)}, u32[]{:S(2)}, u32[]{:S(2)}) collective-permute-start(bf16[640,864]{0,1:T(8,128)(2,1)S(1)} %collective-permute-done.21), channel_id=1, source_target_pairs={{0,8},{8,0},{16,24},{24,16},{1,9},{9,1},{17,25},{25,17},{2,10},{10... | collective-permute-start | bytes 3317768 | tf_op jit(solution)/shard_map/ppermute | solution.py:22
  424.5 54.5 %collective-permute-start.19 = (bf16[2,2,128,2560]{3,2,0,1:T(8,128)(2,1)}, bf16[2,2,128,2560]{3,2,0,1:T(8,128)(2,1)}, u32[]{:S(2)}, u32[]{:S(2)}) collective-permute-start(bf16[2,2,128,2560]{3,2,0,1:T(8,128)(2,1)} %get-tuple-element.151), channel_id=1, source_target_pairs={{0,1},{1,0},{2,3},{3,2},{4,5},{5,4},{6,7},{7,6},{8,9},{9,8},{10,11... | collective-permute-start | bytes 7864328 | tf_op jit(solution)/shard_map/ppermute | solution.py:22
  426.9 24.8 %collective-permute-start.34 = (bf16[128,1280]{1,0:T(8,128)(2,1)S(1)}, bf16[128,1280]{1,0:T(8,128)(2,1)S(1)}, u32[]{:S(2)}, u32[]{:S(2)}) collective-permute-start(bf16[128,1280]{1,0:T(8,128)(2,1)S(1)} %get-tuple-element.212), channel_id=1, source_target_pairs={{0,2},{1,3},{2,0},{3,1},{4,6},{5,7},{6,4},{7,5},{8,10},{9,11},{10,... | collective-permute-start | bytes 983048 | tf_op jit(solution)/shard_map/ppermute | solution.py:22
  478.9 48.5 %collective-permute-start.38 = (bf16[2,2,128,2560]{3,2,0,1:T(8,128)(2,1)}, bf16[2,2,128,2560]{3,2,0,1:T(8,128)(2,1)}, u32[]{:S(2)}, u32[]{:S(2)}) collective-permute-start(bf16[2,2,128,2560]{3,2,0,1:T(8,128)(2,1)} %get-tuple-element.147), channel_id=1, source_target_pairs={{0,1},{1,0},{2,3},{3,2},{4,5},{5,4},{6,7},{7,6},{8,9},{9,8},{10,11... | collective-permute-start | bytes 7864328 | tf_op jit(solution)/shard_map/ppermute | solution.py:22
  498.9 144.1 %collective-permute-start.28 = (bf16[2,2,128,2560]{3,2,0,1:T(8,128)(2,1)}, bf16[2,2,128,2560]{3,2,0,1:T(8,128)(2,1)}, u32[]{:S(2)}, u32[]{:S(2)}) collective-permute-start(bf16[2,2,128,2560]{3,2,0,1:T(8,128)(2,1)} %convolution_convert_fusion.5), channel_id=1, source_target_pairs={{0,1},{1,0},{2,3},{3,2},{4,5},{5,4},{6,7},{7,6},{8,9},{9,8},{10,11... | collective-permute-start | bytes 7864328 | tf_op jit(solution)/shard_map/ppermute | solution.py:22
  547.8 38.4 %collective-permute-start.95 = (bf16[432,640]{1,0:T(8,128)(2,1)}, bf16[432,640]{1,0:T(8,128)(2,1)}, u32[]{:S(2)}, u32[]{:S(2)}) collective-permute-start(bf16[432,640]{1,0:T(8,128)(2,1)} %get-tuple-element.134), channel_id=1, source_target_pairs={{0,8},{8,0},{16,24},{24,16},{1,9},{9,1},{17,25},{25,17},{2,10},{10... | collective-permute-start | bytes 1658888 | tf_op jit(solution)/shard_map/ppermute | solution.py:22
  548.5 37.7 %collective-permute-start.96 = (bf16[432,640]{1,0:T(8,128)(2,1)}, bf16[432,640]{1,0:T(8,128)(2,1)}, u32[]{:S(2)}, u32[]{:S(2)}) collective-permute-start(bf16[432,640]{1,0:T(8,128)(2,1)} %get-tuple-element.135), channel_id=1, source_target_pairs={{0,8},{8,0},{16,24},{24,16},{1,9},{9,1},{17,25},{25,17},{2,10},{10... | collective-permute-start | bytes 1658888 | tf_op jit(solution)/shard_map/ppermute | solution.py:22
  572.7 39.5 %collective-permute-start.85 = (bf16[640,864]{0,1:T(8,128)(2,1)}, bf16[640,864]{0,1:T(8,128)(2,1)}, u32[]{:S(2)}, u32[]{:S(2)}) collective-permute-start(bf16[640,864]{0,1:T(8,128)(2,1)} %get-tuple-element.112), channel_id=1, source_target_pairs={{0,8},{8,0},{16,24},{24,16},{1,9},{9,1},{17,25},{25,17},{2,10},{10... | collective-permute-start | bytes 3317768 | tf_op jit(solution)/shard_map/ppermute | solution.py:22
  573.4 60.9 %collective-permute-start.86 = (bf16[640,864]{0,1:T(8,128)(2,1)}, bf16[640,864]{0,1:T(8,128)(2,1)}, u32[]{:S(2)}, u32[]{:S(2)}) collective-permute-start(bf16[640,864]{0,1:T(8,128)(2,1)} %get-tuple-element.113), channel_id=1, source_target_pairs={{0,8},{8,0},{16,24},{24,16},{1,9},{9,1},{17,25},{25,17},{2,10},{10... | collective-permute-start | bytes 3317768 | tf_op jit(solution)/shard_map/ppermute | solution.py:22
  586.3 62.7 %collective-permute-start.52 = (bf16[2,2,128,2560]{3,2,0,1:T(8,128)(2,1)}, bf16[2,2,128,2560]{3,2,0,1:T(8,128)(2,1)}, u32[]{:S(2)}, u32[]{:S(2)}) collective-permute-start(bf16[2,2,128,2560]{3,2,0,1:T(8,128)(2,1)} %convolution_convert_fusion.3), channel_id=1, source_target_pairs={{0,1},{1,0},{2,3},{3,2},{4,5},{5,4},{6,7},{7,6},{8,9},{9,8},{10,11... | collective-permute-start | bytes 7864328 | tf_op jit(solution)/shard_map/ppermute | solution.py:22
  589.2 50.2 %collective-permute-start.97 = (bf16[432,640]{1,0:T(8,128)(2,1)}, bf16[432,640]{1,0:T(8,128)(2,1)}, u32[]{:S(2)}, u32[]{:S(2)}) collective-permute-start(bf16[432,640]{1,0:T(8,128)(2,1)} %get-tuple-element.133), channel_id=1, source_target_pairs={{0,16},{8,24},{16,0},{24,8},{1,17},{9,25},{17,1},{25,9},{2,18},{10... | collective-permute-start | bytes 1658888 | tf_op jit(solution)/shard_map/ppermute | solution.py:22
  612.2 55.6 %collective-permute-start.39 = (bf16[2,2,128,2560]{3,2,0,1:T(8,128)(2,1)}, bf16[2,2,128,2560]{3,2,0,1:T(8,128)(2,1)}, u32[]{:S(2)}, u32[]{:S(2)}) collective-permute-start(bf16[2,2,128,2560]{3,2,0,1:T(8,128)(2,1)} %convolution_convert_fusion.4), channel_id=1, source_target_pairs={{0,1},{1,0},{2,3},{3,2},{4,5},{5,4},{6,7},{7,6},{8,9},{9,8},{10,11... | collective-permute-start | bytes 7864328 | tf_op jit(solution)/shard_map/ppermute | solution.py:22
  634.3 37.7 %collective-permute-start.63 = (bf16[2,2,128,2560]{3,2,0,1:T(8,128)(2,1)}, bf16[2,2,128,2560]{3,2,0,1:T(8,128)(2,1)}, u32[]{:S(2)}, u32[]{:S(2)}) collective-permute-start(bf16[2,2,128,2560]{3,2,0,1:T(8,128)(2,1)} %convolution_convert_fusion.2), channel_id=1, source_target_pairs={{0,1},{1,0},{2,3},{3,2},{4,5},{5,4},{6,7},{7,6},{8,9},{9,8},{10,11... | collective-permute-start | bytes 7864328 | tf_op jit(solution)/shard_map/ppermute | solution.py:22
  639.3 172.5 %collective-permute-start.87 = (bf16[640,864]{0,1:T(8,128)(2,1)}, bf16[640,864]{0,1:T(8,128)(2,1)}, u32[]{:S(2)}, u32[]{:S(2)}) collective-permute-start(bf16[640,864]{0,1:T(8,128)(2,1)} %get-tuple-element.111), channel_id=1, source_target_pairs={{0,16},{8,24},{16,0},{24,8},{1,17},{9,25},{17,1},{25,9},{2,18},{10... | collective-permute-start | bytes 3317768 | tf_op jit(solution)/shard_map/ppermute | solution.py:22
  667.8 22.9 %collective-permute-start.30 = (bf16[128,1280]{1,0:T(8,128)(2,1)S(1)}, bf16[128,1280]{1,0:T(8,128)(2,1)S(1)}, u32[]{:S(2)}, u32[]{:S(2)}) collective-permute-start(bf16[128,1280]{1,0:T(8,128)(2,1)S(1)} %fusion.95), channel_id=1, source_target_pairs={{0,4},{4,0},{1,5},{5,1},{2,6},{6,2},{3,7},{7,3},{8,12},{12,8},{9,1... | collective-permute-start | bytes 983048 | tf_op jit(solution)/shard_map/ppermute | solution.py:22
  682.2 28.7 %collective-permute-start.40 = (bf16[2,128,1280]{2,1,0:T(8,128)(2,1)S(1)}, bf16[2,128,1280]{2,1,0:T(8,128)(2,1)S(1)}, u32[]{:S(2)}, u32[]{:S(2)}) collective-permute-start(bf16[2,128,1280]{2,1,0:T(8,128)(2,1)S(1)} %slice_bitcast_fusion.31), channel_id=1, source_target_pairs={{0,2},{1,3},{2,0},{3,1},{4,6},{5,7},{6,4},{7,5},{8,10},{9,11},{10,... | collective-permute-start | bytes 1966088 | tf_op jit(solution)/shard_map/ppermute | solution.py:22
  683.7 28.5 %collective-permute-start.42 = (bf16[2,128,1280]{2,1,0:T(8,128)(2,1)S(1)}, bf16[2,128,1280]{2,1,0:T(8,128)(2,1)S(1)}, u32[]{:S(2)}, u32[]{:S(2)}) collective-permute-start(bf16[2,128,1280]{2,1,0:T(8,128)(2,1)S(1)} %slice_bitcast_fusion.29), channel_id=1, source_target_pairs={{0,4},{4,0},{1,5},{5,1},{2,6},{6,2},{3,7},{7,3},{8,12},{12,8},{9,1... | collective-permute-start | bytes 1966088 | tf_op jit(solution)/shard_map/ppermute | solution.py:22
  692.2 58.3 %collective-permute-start.56 = (bf16[128,1280]{1,0:T(8,128)(2,1)S(1)}, bf16[128,1280]{1,0:T(8,128)(2,1)S(1)}, u32[]{:S(2)}, u32[]{:S(2)}) collective-permute-start(bf16[128,1280]{1,0:T(8,128)(2,1)S(1)} %fusion.100), channel_id=1, source_target_pairs={{0,2},{1,3},{2,0},{3,1},{4,6},{5,7},{6,4},{7,5},{8,10},{9,11},{10,... | collective-permute-start | bytes 983048 | tf_op jit(solution)/shard_map/ppermute | solution.py:22
  712.5 36.8 %collective-permute-start.41 = (bf16[128,1280]{1,0:T(8,128)(2,1)S(1)}, bf16[128,1280]{1,0:T(8,128)(2,1)S(1)}, u32[]{:S(2)}, u32[]{:S(2)}) collective-permute-start(bf16[128,1280]{1,0:T(8,128)(2,1)S(1)} %fusion.97), channel_id=1, source_target_pairs={{0,4},{4,0},{1,5},{5,1},{2,6},{6,2},{3,7},{7,3},{8,12},{12,8},{9,1... | collective-permute-start | bytes 983048 | tf_op jit(solution)/shard_map/ppermute | solution.py:22
  725.6 23.8 %collective-permute-start.43 = (bf16[128,1280]{1,0:T(8,128)(2,1)S(1)}, bf16[128,1280]{1,0:T(8,128)(2,1)S(1)}, u32[]{:S(2)}, u32[]{:S(2)}) collective-permute-start(bf16[128,1280]{1,0:T(8,128)(2,1)S(1)} %fusion.98), channel_id=1, source_target_pairs={{0,2},{1,3},{2,0},{3,1},{4,6},{5,7},{6,4},{7,5},{8,10},{9,11},{10,... | collective-permute-start | bytes 983048 | tf_op jit(solution)/shard_map/ppermute | solution.py:22
  747.2 41.1 %collective-permute-start.68 = (bf16[128,2560]{1,0:T(8,128)(2,1)S(1)}, bf16[128,2560]{1,0:T(8,128)(2,1)S(1)}, u32[]{:S(2)}, u32[]{:S(2)}) collective-permute-start(bf16[128,2560]{1,0:T(8,128)(2,1)S(1)} %pad_maximum_fusion.18), channel_id=1, source_target_pairs={{0,16},{8,24},{16,0},{24,8},{1,17},{9,25},{17,1},{25,9},{2,18},{10... | collective-permute-start | bytes 1966088 | tf_op jit(solution)/shard_map/ppermute | solution.py:22
  749.5 52.7 %collective-permute-start.44 = (bf16[128,2560]{1,0:T(8,128)(2,1)S(1)}, bf16[128,2560]{1,0:T(8,128)(2,1)S(1)}, u32[]{:S(2)}, u32[]{:S(2)}) collective-permute-start(bf16[128,2560]{1,0:T(8,128)(2,1)S(1)} %pad_maximum_fusion.13), channel_id=1, source_target_pairs={{0,16},{8,24},{16,0},{24,8},{1,17},{9,25},{17,1},{25,9},{2,18},{10... | collective-permute-start | bytes 1966088 | tf_op jit(solution)/shard_map/ppermute | solution.py:22
  808.5 31.7 %collective-permute-start.98 = (bf16[2,432,320]{1,2,0:T(8,128)(2,1)}, bf16[2,432,320]{1,2,0:T(8,128)(2,1)}, u32[]{:S(2)}, u32[]{:S(2)}) collective-permute-start(bf16[2,432,320]{1,2,0:T(8,128)(2,1)} %fusion.59), channel_id=1, source_target_pairs={{0,4},{4,0},{1,5},{5,1},{2,6},{6,2},{3,7},{7,3},{8,12},{12,8},{9,1... | collective-permute-start | bytes 1658888 | tf_op jit(solution)/shard_map/ppermute | solution.py:22
  819.9 31.4 %collective-permute-start.70 = (bf16[2,128,1280]{2,1,0:T(8,128)(2,1)}, bf16[2,128,1280]{2,1,0:T(8,128)(2,1)}, u32[]{:S(2)}, u32[]{:S(2)}) collective-permute-start(bf16[2,128,1280]{2,1,0:T(8,128)(2,1)} %get-tuple-element.184), channel_id=1, source_target_pairs={{0,4},{4,0},{1,5},{5,1},{2,6},{6,2},{3,7},{7,3},{8,12},{12,8},{9,1... | collective-permute-start | bytes 1966088 | tf_op jit(solution)/shard_map/ppermute | solution.py:22
  837.4 33.5 %collective-permute-start.88 = (bf16[2,320,864]{2,0,1:T(2,128)(2,1)}, bf16[2,320,864]{2,0,1:T(2,128)(2,1)}, u32[]{:S(2)}, u32[]{:S(2)}) collective-permute-start(bf16[2,320,864]{2,0,1:T(2,128)(2,1)} %copy.665), channel_id=1, source_target_pairs={{0,4},{4,0},{1,5},{5,1},{2,6},{6,2},{3,7},{7,3},{8,12},{12,8},{9,1... | collective-permute-start | bytes 3317768 | tf_op jit(solution)/shard_map/ppermute | solution.py:22
  855.1 44.4 %collective-permute-start.73 = (bf16[2,2,128,2560]{3,2,0,1:T(8,128)(2,1)}, bf16[2,2,128,2560]{3,2,0,1:T(8,128)(2,1)}, u32[]{:S(2)}, u32[]{:S(2)}) collective-permute-start(bf16[2,2,128,2560]{3,2,0,1:T(8,128)(2,1)} %get-tuple-element.141), channel_id=1, source_target_pairs={{0,1},{1,0},{2,3},{3,2},{4,5},{5,4},{6,7},{7,6},{8,9},{9,8},{10,11... | collective-permute-start | bytes 7864328 | tf_op jit(solution)/shard_map/ppermute | solution.py:22
  899.6 56.6 %collective-permute-start.46 = (bf16[2,128,2560]{2,1,0:T(8,128)(2,1)}, bf16[2,128,2560]{2,1,0:T(8,128)(2,1)}, u32[]{:S(2)}, u32[]{:S(2)}) collective-permute-start(bf16[2,128,2560]{2,1,0:T(8,128)(2,1)} %maximum_select_fusion.9), channel_id=1, source_target_pairs={{0,1},{1,0},{2,3},{3,2},{4,5},{5,4},{6,7},{7,6},{8,9},{9,8},{10,11... | collective-permute-start | bytes 3932168 | tf_op jit(solution)/shard_map/ppermute | solution.py:22
  907.7 39.9 %collective-permute-start.92 = (bf16[320,640]{1,0:T(8,128)(2,1)}, bf16[320,640]{1,0:T(8,128)(2,1)}, u32[]{:S(2)}, u32[]{:S(2)}) collective-permute-start(bf16[320,640]{1,0:T(8,128)(2,1)} %get-tuple-element.139), channel_id=1, source_target_pairs={{0,8},{8,0},{16,24},{24,16},{1,9},{9,1},{17,25},{25,17},{2,10},{10... | collective-permute-start | bytes 1228808 | tf_op jit(solution)/shard_map/ppermute | solution.py:22
  945.1 72.7 %collective-permute-start.74 = (bf16[2,2,128,2560]{3,2,0,1:T(8,128)(2,1)}, bf16[2,2,128,2560]{3,2,0,1:T(8,128)(2,1)}, u32[]{:S(2)}, u32[]{:S(2)}) collective-permute-start(bf16[2,2,128,2560]{3,2,0,1:T(8,128)(2,1)} %convolution_convert_fusion.1), channel_id=1, source_target_pairs={{0,1},{1,0},{2,3},{3,2},{4,5},{5,4},{6,7},{7,6},{8,9},{9,8},{10,11... | collective-permute-start | bytes 7864328 | tf_op jit(solution)/shard_map/ppermute | solution.py:22
  947.2 35.0 %collective-permute-start.91 = (bf16[320,640]{1,0:T(8,128)(2,1)S(1)}, bf16[320,640]{1,0:T(8,128)(2,1)S(1)}, u32[]{:S(2)}, u32[]{:S(2)}) collective-permute-start(bf16[320,640]{1,0:T(8,128)(2,1)S(1)} %copy-done.67), channel_id=1, source_target_pairs={{0,8},{8,0},{16,24},{24,16},{1,9},{9,1},{17,25},{25,17},{2,10},{10... | collective-permute-start | bytes 1228808 | tf_op jit(solution)/shard_map/ppermute | solution.py:22
  947.6 48.2 %collective-permute-start.81 = (bf16[640,512]{1,0:T(8,128)(2,1)}, bf16[640,512]{1,0:T(8,128)(2,1)S(1)}, u32[]{:S(2)}, u32[]{:S(2)}) collective-permute-start(bf16[640,512]{1,0:T(8,128)(2,1)} %get-tuple-element.118), channel_id=1, source_target_pairs={{0,8},{8,0},{16,24},{24,16},{1,9},{9,1},{17,25},{25,17},{2,10},{10... | collective-permute-start | bytes 1966088 | tf_op jit(solution)/shard_map/ppermute | solution.py:22
  954.3 31.2 %collective-permute-start.93 = (bf16[320,640]{1,0:T(8,128)(2,1)S(1)}, bf16[320,640]{1,0:T(8,128)(2,1)S(1)}, u32[]{:S(2)}, u32[]{:S(2)}) collective-permute-start(bf16[320,640]{1,0:T(8,128)(2,1)S(1)} %add_convert_fusion.3), channel_id=1, source_target_pairs={{0,16},{8,24},{16,0},{24,8},{1,17},{9,25},{17,1},{25,9},{2,18},{10... | collective-permute-start | bytes 1228808 | tf_op jit(solution)/shard_map/ppermute | solution.py:22
  956.2 46.8 %collective-permute-start.83 = (bf16[640,512]{1,0:T(8,128)(2,1)S(1)}, bf16[640,512]{1,0:T(8,128)(2,1)}, u32[]{:S(2)}, u32[]{:S(2)}) collective-permute-start(bf16[640,512]{1,0:T(8,128)(2,1)S(1)} %add_convert_fusion.1), channel_id=1, source_target_pairs={{0,16},{8,24},{16,0},{24,8},{1,17},{9,25},{17,1},{25,9},{2,18},{10... | collective-permute-start | bytes 1966088 | tf_op jit(solution)/shard_map/ppermute | solution.py:22
  1006.6 56.9 %collective-permute-start.94 = (bf16[320,320]{1,0:T(8,128)(2,1)S(1)}, bf16[320,320]{1,0:T(8,128)(2,1)S(1)}, u32[]{:S(2)}, u32[]{:S(2)}) collective-permute-start(bf16[320,320]{1,0:T(8,128)(2,1)S(1)} %bitcast.600), channel_id=1, source_target_pairs={{0,4},{4,0},{1,5},{5,1},{2,6},{6,2},{3,7},{7,3},{8,12},{12,8},{9,1... | collective-permute-start | bytes 614408 | tf_op jit(solution)/shard_map/ppermute | solution.py:22
  (132 other events, 1697.7 us)

commit v2 on v1

--- a/solution.py
+++ b/solution.py
@@ -36,34 +36,27 @@
     return lax.dynamic_index_in_dim(blocks, index, 0, keepdims=False)
 
 
-def attend_kernel(scale, block, qkv, cos, sin, seg_col, seg_row, sel, attn, rot, stats):
-    full_len = qkv.shape[0]
+def attend_rows(scale, block, i, rot, seg_col, seg_row, sel, attn, stats):
     n_q = rot.shape[1] // LANES - 2
-    cos_t, sin_t = cos[...], sin[...]
-    for h in range(n_q + 1):
-        u = qkv[:, h * LANES : (h + 1) * LANES]
-        rot[:, h * LANES : (h + 1) * LANES] = (u * cos_t + pltpu.roll(u, 64, 1) * sin_t).astype(BF16)
-    rot[:, (n_q + 1) * LANES :] = qkv[:, (n_q + 1) * LANES :].astype(BF16)
-    for i in range(full_len // block):
-        rows = slice(i * block, (i + 1) * block)
-        keys = (i + 1) * block
-        q_pos = i * block + lax.broadcasted_iota(jnp.int32, (block, keys), 0)
-        k_pos = lax.broadcasted_iota(jnp.int32, (block, keys), 1)
-        allowed = (seg_col[rows, :] == seg_row[:, :keys]) & (k_pos <= q_pos)
-        k = rot[:keys, n_q * LANES : (n_q + 1) * LANES]
-        v = rot[:keys, (n_q + 1) * LANES :]
-        outs, maxes, totals = [], [], []
-        for h in range(n_q):
-            s = dot(rot[rows, h * LANES : (h + 1) * LANES], k, ((1,), (1,))) * scale
-            s = jnp.where(allowed, s, MASK_FILL)
-            top = jnp.max(s, axis=1, keepdims=True)
-            e = jnp.exp(s - top)
-            total = jnp.sum(e, axis=1, keepdims=True)
-            outs.append(dot((e * (1.0 / total)).astype(BF16), v).astype(BF16))
-            maxes.append(top)
-            totals.append(total)
-        attn[rows, :] = dot(jnp.concatenate(outs, axis=1), sel[...]).astype(BF16)
-        stats[rows, :] = jnp.concatenate(maxes + totals, axis=1)
+    rows = slice(i * block, (i + 1) * block)
+    keys = (i + 1) * block
+    q_pos = i * block + lax.broadcasted_iota(jnp.int32, (block, keys), 0)
+    k_pos = lax.broadcasted_iota(jnp.int32, (block, keys), 1)
+    allowed = (seg_col[rows, :] == seg_row[:, :keys]) & (k_pos <= q_pos)
+    k = rot[:keys, n_q * LANES : (n_q + 1) * LANES]
+    v = rot[:keys, (n_q + 1) * LANES :]
+    outs, maxes, totals = [], [], []
+    for h in range(n_q):
+        s = dot(rot[rows, h * LANES : (h + 1) * LANES], k, ((1,), (1,))) * scale
+        s = jnp.where(allowed, s, MASK_FILL)
+        top = jnp.max(s, axis=1, keepdims=True)
+        e = jnp.exp(s - top)
+        total = jnp.sum(e, axis=1, keepdims=True)
+        outs.append(dot((e * (1.0 / total)).astype(BF16), v).astype(BF16))
+        maxes.append(top)
+        totals.append(total)
+    attn[rows, :] = dot(jnp.concatenate(outs, axis=1), sel[...]).astype(BF16)
+    stats[rows, :] = jnp.concatenate(maxes + totals, axis=1)
 
 
 def attend_back_kernel(
@@ -107,26 +100,6 @@
 VMEM_LIMIT = 56 * 1024 * 1024
 
 
-def attend(qkv, cos, sin, seg_col, seg_row, sel, scale):
-    full_len, width = qkv.shape
-    n_q = width // LANES - 2
-    return pl.pallas_call(
-        lambda *refs: attend_kernel(scale, min(256, full_len), *refs),
-        out_shape=(
-            jax.ShapeDtypeStruct((full_len, sel.shape[1]), BF16),
-            jax.ShapeDtypeStruct((full_len, width), BF16),
-            jax.ShapeDtypeStruct((full_len, 2 * n_q), F32),
-        ),
-        compiler_params=pltpu.CompilerParams(vmem_limit_bytes=VMEM_LIMIT),
-        cost_estimate=pl.CostEstimate(
-            flops=2 * n_q * full_len * full_len * LANES,
-            bytes_accessed=full_len * width * 6,
-            transcendentals=n_q * full_len * full_len // 2,
-        ),
-        name="attend",
-    )(qkv, cos, sin, seg_col, seg_row, sel)
-
-
 def attend_back(rot, d_attn, stats, cos, sin, seg_col, seg_row, sel, scale):
     full_len, width = rot.shape
     n_q = width // LANES - 2
@@ -231,6 +204,491 @@
     return {
         rel: lax.dynamic_slice_in_dim(value, (index ^ rel) * size, size, axis) for rel in range(n)
     }
+
+
+def flip(index, mask):
+    return index + mask * (1 - 2 * ((index // mask) % 2))
+
+
+def flip_all(index, bits):
+    mask = 1
+    while mask <= bits:
+        if bits & mask:
+            index = flip(index, mask)
+        mask *= 2
+    return index
+
+
+class Links:
+    def __init__(self, send_sems, recv_sems):
+        self.sems = (send_sems, recv_sems)
+        self.copies = []
+
+    def send(self, src, dst, peer):
+        k = len(self.copies)
+        copy = pltpu.make_async_remote_copy(
+            src_ref=src,
+            dst_ref=dst,
+            send_sem=self.sems[0].at[k],
+            recv_sem=self.sems[1].at[k],
+            device_id=peer,
+            device_id_type=pl.DeviceIdType.MESH,
+        )
+        copy.start()
+        self.copies.append(copy)
+        return copy
+
+    def finish(self):
+        for copy in self.copies:
+            copy.wait_send()
+
+
+def greet(peers):
+    barrier = pltpu.get_barrier_semaphore()
+    for peer in peers:
+        pl.semaphore_signal(barrier, inc=1, device_id=peer, device_id_type=pl.DeviceIdType.MESH)
+    pl.semaphore_wait(barrier, len(peers))
+
+
+class Place:
+    def __init__(self, n_z, n_tp):
+        self.n_z, self.n_tp = n_z, n_tp
+        self.z, self.y, self.t = (lax.axis_index(a) for a in ("fsdp", "ctx", "tp"))
+        self.me = self.y * n_tp + self.t
+        self.core = {"tp": flip(self.t, 1)}
+        self.x = {"tp": flip(self.t, 2)}
+        self.yy = {"ctx": 1 - self.y}
+        self.masks = below(n_z)
+
+    def zz(self, mask):
+        return {"fsdp": flip(self.z, mask)}
+
+    def peers(self):
+        return [self.core, self.x, self.yy] + [self.zz(m) for m in self.masks]
+
+
+class WeightFlow:
+    def __init__(self, links, at, out, cross, first, second):
+        self.links, self.at, self.out = links, at, out
+        self.first, self.second = first, second
+        self.got = {}
+        self.y_copy = links.send(cross, second(None), at.yy)
+
+    def own(self):
+        at = self.at
+        for m in at.masks:
+            dst = self.out.at[at.z, at.y]
+            self.got[m, 0] = self.links.send(self.first(m), dst, at.zz(m))
+
+    def crossed(self):
+        at = self.at
+        self.y_copy.wait_recv()
+        for m in at.masks:
+            dst = self.out.at[at.z, 1 - at.y]
+            self.got[m, 1] = self.links.send(self.second(m), dst, at.zz(m))
+
+    def take(self, rel, part):
+        at = self.at
+        self.got[rel, part].wait_recv()
+        low = rel & -rel
+        row = at.y if part == 0 else 1 - at.y
+        block = self.out.at[flip_all(at.z, rel), row]
+        for m in at.masks:
+            if m < low:
+                self.got[rel ^ m, part] = self.links.send(block, block, at.zz(m))
+
+    def order(self):
+        rels = [r for r in range(1, self.at.n_z)]
+        return sorted(rels, key=lambda r: (bin(r).count("1"), -(r & -r), r))
+
+
+def half_rows(ref, part, rows):
+    return ref.at[pl.ds(part * (rows // 2), rows // 2)]
+
+
+class LayerGather:
+    def __init__(self, links, at, out, rows, halves):
+        self.links, self.at, self.out, self.rows = links, at, out, rows
+        self.halves = halves
+        self.cores = []
+
+    def half(self, index, part):
+        return half_rows(self.out.at[index], part, self.rows)
+
+    def pass_on(self, index, part, peer):
+        block = self.half(index, part)
+        return self.links.send(block, block, peer)
+
+    def own(self, part, src=None):
+        at, me = self.at, self.at.me
+        a = self.half(me, part)
+        src = a if src is None else src
+        send = lambda peer: self.links.send(src, a, peer)
+        if part == 0:
+            self.xa, self.ya = send(at.x), send(at.yy)
+        else:
+            self.yb, self.xb = send(at.yy), send(at.x)
+        self.cores.append(send(at.core))
+
+    def to_core(self, index, part):
+        self.cores.append(self.pass_on(index, part, self.at.core))
+
+    def far_first(self):
+        at = self.at
+        self.x_of, self.y_of = flip(at.me, 2), flip(at.me, at.n_tp)
+        self.diag = flip(self.x_of, at.n_tp)
+        self.xa.wait_recv()
+        self.y_fwd = self.pass_on(self.x_of, 0, at.yy)
+        self.to_core(self.x_of, 0)
+        self.yb.wait_recv()
+        self.x_fwd = self.pass_on(self.y_of, 1, at.x)
+        self.to_core(self.y_of, 1)
+
+    def far_second(self):
+        self.ya.wait_recv()
+        self.to_core(self.y_of, 0)
+        self.xb.wait_recv()
+        self.to_core(self.x_of, 1)
+        self.y_fwd.wait_recv()
+        self.to_core(self.diag, 0)
+        self.x_fwd.wait_recv()
+        self.to_core(self.diag, 1)
+
+    def last(self):
+        for copy in self.cores:
+            copy.wait_recv()
+
+
+class LayerSum:
+    def __init__(self, links, at, rows, to_core, from_core, part, landed):
+        self.links, self.at, self.rows = links, at, rows
+        self.bufs = (to_core, from_core, part, landed)
+
+    def begin(self, product):
+        to_core, from_core, _, _ = self.bufs
+        self.core = {}
+        for k in (3, 1, 2, 0):
+            to_core[k] = product(2 * k + 1).astype(BF16)
+            self.core[k] = self.links.send(to_core.at[k], from_core.at[k], self.at.core)
+
+    def middle(self, product):
+        _, from_core, part, landed = self.bufs
+        at, rows, h = self.at, self.rows, self.rows // 2
+        a, b = slice(0, h), slice(h, rows)
+
+        def level(k):
+            value = product(2 * k)
+            self.core[k].wait_recv()
+            return value + from_core[k].astype(F32)
+
+        send = lambda k, i, peer: self.links.send(
+            part.at[k, pl.ds((i % 2) * h, h)], landed.at[i], peer
+        )
+        part[3] = level(3).astype(BF16)
+        x1 = send(3, 0, at.x)
+        y1 = send(3, 1, at.yy)
+        one = level(1)
+        part[1, a] = one[a].astype(BF16)
+        x2 = send(1, 2, at.x)
+        two = level(2)
+        part[2, b] = two[b].astype(BF16)
+        y2 = send(2, 3, at.yy)
+        zero = level(0)
+        x1.wait_recv()
+        part[2, a] = (two[a] + landed[0].astype(F32)).astype(BF16)
+        y3 = send(2, 4, at.yy)
+        y1.wait_recv()
+        part[1, b] = (one[b] + landed[1].astype(F32)).astype(BF16)
+        x3 = send(1, 5, at.x)
+        self.zero, self.tail = zero, (x2, y3, y2, x3)
+
+    def end(self):
+        _, _, _, landed = self.bufs
+        h = self.rows // 2
+        for copy in self.tail:
+            copy.wait_recv()
+        zero = self.zero
+        top = zero[:h] + landed[2].astype(F32) + landed[4].astype(F32)
+        low = zero[h:] + landed[3].astype(F32) + landed[5].astype(F32)
+        return top, low
+
+
+def sum_scratch(rows, width):
+    return [
+        pltpu.VMEM((4, rows, width), BF16),
+        pltpu.VMEM((4, rows, width), BF16),
+        pltpu.VMEM((4, rows, width), BF16),
+        pltpu.VMEM((6, rows // 2, width), BF16),
+    ]
+
+
+def front_kernel(
+    n_z, n_tp, scale, q_block,
+    x_here, dy_here, in_send, o_send, w3_send, cos, sin, seg_col, seg_row, spread, sel,
+    w_heads, w_o, w3, gains, norm_attn, dy_all, norm_all, attn, rot, stats, mid,
+    w_in, x_all, qkv, to_core, from_core, part, landed, in_cross, o_cross, w3_cross,
+    heads_v, norm_v, own_v, root_v, o_v, send_sems, recv_sems, sems,
+):
+    at = Place(n_z, n_tp)
+    links = Links(send_sems, recv_sems)
+    z, y, t, me = at.z, at.y, at.t, at.me
+    zb = z // (n_z // 2)
+    n_b, rows, width = 2 * n_tp, x_all.shape[0] // (2 * n_tp), x_all.shape[1]
+    depth = in_send.shape[1]
+    full_len = x_all.shape[0]
+    local = []
+
+    def move(src, dst):
+        copy = pltpu.make_async_copy(src, dst, sems.at[len(local)])
+        copy.start()
+        local.append(copy)
+        return copy
+
+    def block_of(ref, index):
+        return ref.at[pl.ds(pl.multiple_of(index * rows, rows), rows)]
+
+    greet(at.peers())
+    f_in = WeightFlow(
+        links, at, w_in, in_send.at[1 - y], lambda m: in_send.at[y], lambda m: in_cross
+    )
+    f_in.own()
+    own_in = move(in_send.at[y], w_in.at[z, y])
+    x_mine = block_of(x_here, t)
+    tok_y = links.send(x_mine, block_of(x_all, me), at.yy)
+    x_own = move(x_here, x_all.at[pl.ds(pl.multiple_of(y * (full_len // 2), full_len // 2), full_len // 2)])
+    dy_mine = block_of(dy_here, t)
+    dy_own = move(dy_here.reshape(n_tp, rows, width), dy_all.at[0, pl.ds(y * n_tp, n_tp)])
+
+    f_in.crossed()
+    cross_in = move(in_cross, w_in.at[z, 1 - y])
+    f_o = WeightFlow(
+        links, at, w_o, o_send.at[1 - y], lambda m: o_send.at[y], lambda m: o_cross
+    )
+    top = n_z // 2
+    f_3 = WeightFlow(
+        links, at, w3, w3_send.at[1 - y],
+        lambda m: w3_send.at[y, 1 - zb if m == top else zb],
+        lambda m: w3_cross if m is None else w3_cross.at[1 - zb if m == top else zb],
+    )
+    dy_y = links.send(dy_mine, dy_all.at[0, me], at.yy)
+    tok_y.wait_recv()
+    y_of, x_of = flip(me, n_tp), flip(me, 2)
+    y_block = block_of(x_all, y_of)
+    tok_x = links.send(y_block, y_block, at.x)
+    tok_c = [links.send(y_block, y_block, at.core)]
+    ins = [(rel, p) for rel in f_in.order() for p in (0, 1)]
+    for rel, p in ins:
+        if rel == top:
+            f_in.take(rel, p)
+    tok_x.wait_recv()
+    diag = block_of(x_all, flip(y_of, 2))
+    tok_c.append(links.send(diag, diag, at.core))
+    x_own.wait()
+
+    for copy in tok_c:
+        copy.wait_recv()
+
+    step = min(256, full_len)
+
+    def find_root(c, carry):
+        at_rows = pl.ds(pl.multiple_of(c * step, step), step)
+        value = x_all[at_rows, :].astype(F32)
+        root_v[at_rows, :] = lax.rsqrt(jnp.mean(value * value, axis=1, keepdims=True) + NORM_EPS)
+        return carry
+
+    lax.fori_loop(0, full_len // step, find_root, 0)
+    own_in.wait()
+    cross_in.wait()
+
+    pick_gain = (
+        lax.broadcasted_iota(jnp.int32, (8, w_in.shape[3]), 1)
+        == sel.shape[1] // HEAD_DIM * HEAD_DIM + 2 * HEAD_DIM + lax.broadcasted_iota(jnp.int32, (8, w_in.shape[3]), 0)
+    ).astype(F32).astype(BF16)
+
+    group = 1
+    while 2 * depth * group % LANES:
+        group *= 2
+    span = 2 * depth * group
+
+    def project(rel, first):
+        owner = flip_all(z, rel) // group
+        cols = pl.ds(pl.multiple_of(owner * span, span), span)
+        weights = w_in[pl.ds(owner * group, group)].reshape(span, w_in.shape[3])
+        gain = dot(pick_gain, weights, ((1,), (1,)))
+        gains[:, cols] = gain
+        heads = dot(weights, spread[...]).astype(BF16)
+        heads_v[cols, :] = heads
+
+        def some_rows(c, carry):
+            at_rows = pl.ds(pl.multiple_of(c * step, step), step)
+            value = (x_all[at_rows, cols].astype(F32) * root_v[at_rows, :] * gain[0:1, :]).astype(BF16)
+            norm_v[at_rows, cols] = value
+            term = dot(value, heads)
+            qkv[at_rows, :] = term if first else qkv[at_rows, :] + term
+            return carry
+
+        lax.fori_loop(0, full_len // step, some_rows, 0)
+
+    f_o.own()
+    f_o.crossed()
+    if group == 1:
+        project(0, True)
+    f_3.own()
+    f_3.crossed()
+    for rel in f_in.order():
+        for p in (0, 1):
+            if rel != top:
+                f_in.take(rel, p)
+        if group == 1:
+            project(rel, False)
+    if group > 1:
+        for rel in range(0, n_z, group):
+            project(rel, rel == 0)
+    heads_out = move(heads_v, w_heads)
+    norm_out = move(norm_v, norm_attn)
+    own_o = [move(o_send.at[y], w_o.at[z, y]), move(o_cross, w_o.at[z, 1 - y])]
+    own_3 = [move(w3_send.at[y, zb], w3.at[z, y]), move(w3_cross.at[zb], w3.at[z, 1 - y])]
+    dy_y.wait_recv()
+    dy_x = links.send(dy_all.at[0, y_of], dy_all.at[0, y_of], at.x)
+    dy_c = [links.send(dy_all.at[0, y_of], dy_all.at[0, y_of], at.core)]
+    dy_z = [
+        links.send(half_rows(dy_mine, p, rows), half_rows(dy_all.at[1, me], p, rows), at.zz(top))
+        for p in (0, 1)
+    ]
+    for p in (0, 1):
+        f_o.take(top, p)
+
+    n_q = rot.shape[1] // LANES - 2
+
+    def turn(c, carry):
+        r = pl.ds(pl.multiple_of(c * step, step), step)
+        for h in range(n_q + 1):
+            u = qkv[r, h * LANES : (h + 1) * LANES]
+            rot[r, h * LANES : (h + 1) * LANES] = (
+                u * cos[r, :] + pltpu.roll(u, 64, 1) * sin[r, :]
+            ).astype(BF16)
+        rot[r, (n_q + 1) * LANES :] = qkv[r, (n_q + 1) * LANES :].astype(BF16)
+        return carry
+
+    lax.fori_loop(0, full_len // step, turn, 0)
+    dy_far = LayerGather(links, at, dy_all.at[1], rows, True)
+    for i in range(full_len // q_block):
+        attend_rows(scale, q_block, i, rot, seg_col, seg_row, sel, attn, stats)
+        if i == 0:
+            dy_x.wait_recv()
+            d_of = flip(y_of, 2)
+            dy_c.append(links.send(dy_all.at[0, d_of], dy_all.at[0, d_of], at.core))
+    for rel in f_o.order():
+        for p in (0, 1):
+            if rel != top:
+                f_o.take(rel, p)
+    for copy in own_o:
+        copy.wait()
+    load_o = move(w_o, o_v)
+    load_o.wait()
+
+    layer = LayerSum(links, at, rows, to_core, from_core, part, landed)
+
+    def product(r):
+        lhs = attn[pl.ds(pl.multiple_of(flip_all(me, r) * rows, rows), rows), :]
+        return dot(lhs, o_v[...].reshape(width, o_v.shape[3]), ((1,), (1,)))
+
+    layer.begin(product)
+    layer.middle(product)
+    for p in (0, 1):
+        f_3.take(top, p)
+    norm_own = LayerGather(links, at, norm_all.at[0], rows, True)
+    norm_far = LayerGather(links, at, norm_all.at[1], rows, True)
+    far = []
+    h = rows // 2
+    load_x = move(x_mine, own_v)
+    load_x.wait()
+    for p, value in enumerate(layer.end()):
+        r = slice(p * h, (p + 1) * h)
+        value = value + own_v[r, :].astype(F32)
+        mid[r, :] = value
+        root = lax.rsqrt(jnp.mean(value * value, axis=1, keepdims=True) + NORM_EPS)
+        own_v[r, :] = (value * root * gains[1:2, :]).astype(BF16)
+        src = own_v.at[pl.ds(p * h, h)]
+        far.append(links.send(src, half_rows(norm_all.at[1, me], p, rows), at.zz(top)))
+        norm_own.own(p, src)
+    keep = move(own_v, norm_all.at[0, me])
+    for p in (0, 1):
+        dy_z[p].wait_recv()
+        dy_far.own(p)
+    norm_own.far_first()
+    for p in (0, 1):
+        far[p].wait_recv()
+        norm_far.own(p)
+    norm_own.far_second()
+    dy_far.far_first()
+    norm_far.far_first()
+    dy_far.far_second()
+    norm_far.far_second()
+    for rel in f_3.order():
+        for p in (0, 1):
+            if rel != top:
+                f_3.take(rel, p)
+    for gather in (norm_own, dy_far, norm_far):
+        gather.last()
+    for copy in dy_c:
+        copy.wait_recv()
+    for copy in [dy_own, heads_out, norm_out, keep] + own_3:
+        copy.wait()
+    links.finish()
+
+
+def front(n_z, n_tp, scale, x_here, dy_here, in_send, o_send, w3_send, cos, sin, seg_col, seg_row, spread, sel):
+    half_len, width = x_here.shape
+    full_len = 2 * half_len
+    rows = half_len // n_tp
+    depth, compact = in_send.shape[1:]
+    heads = spread.shape[1]
+    q_cols = sel.shape[1]
+    n_q = heads // LANES - 2
+    w3_cols = w3_send.shape[3]
+    any_, vmem = pl.BlockSpec(memory_space=pl.ANY), pl.BlockSpec(memory_space=pltpu.VMEM)
+    n_sems = 80 + 6 * n_z + 32
+    shape = jax.ShapeDtypeStruct
+    return pl.pallas_call(
+        lambda *refs: front_kernel(n_z, n_tp, scale, min(256, full_len), *refs),
+        out_shape=(
+            shape((width, heads), BF16),
+            shape((n_z, 2, depth, q_cols), BF16),
+            shape((n_z, 2, depth, w3_cols), BF16),
+            shape((8, width), F32),
+            shape((full_len, width), BF16),
+            shape((2, 2 * n_tp, rows, width), BF16),
+            shape((2, 2 * n_tp, rows, width), BF16),
+            shape((full_len, q_cols), BF16),
+            shape((full_len, heads), BF16),
+            shape((full_len, 2 * n_q), F32),
+            shape((rows, width), F32),
+        ),
+        in_specs=[any_] * 5 + [vmem] * 6,
+        out_specs=(any_, any_, any_, vmem, any_, any_, any_, vmem, vmem, vmem, vmem),
+        scratch_shapes=[
+            pltpu.VMEM((n_z, 2, depth, compact), BF16),
+            pltpu.VMEM((full_len, width), BF16),
+            pltpu.VMEM((full_len, heads), F32),
+            *sum_scratch(rows, width),
+            pltpu.VMEM((depth, compact), BF16),
+            pltpu.VMEM((depth, q_cols), BF16),
+            pltpu.VMEM((2, depth, w3_cols), BF16),
+            pltpu.VMEM((width, heads), BF16),
+            pltpu.VMEM((full_len, width), BF16),
+            pltpu.VMEM((rows, width), BF16),
+            pltpu.VMEM((full_len, 1), F32),
+            pltpu.VMEM((n_z, 2, depth, q_cols), BF16),
+            pltpu.SemaphoreType.DMA((n_sems,)),
+            pltpu.SemaphoreType.DMA((n_sems,)),
+            pltpu.SemaphoreType.DMA((16,)),
+        ],
+        compiler_params=pltpu.CompilerParams(
+            collective_id=1, has_side_effects=True, vmem_limit_bytes=VMEM_LIMIT
+        ),
+        name="front",
+    )(x_here, dy_here, in_send, o_send, w3_send, cos, sin, seg_col, seg_row, spread, sel)
 
 
 def body(
@@ -267,43 +725,24 @@
 
     extra = jnp.stack([attn_gain, ffn_gain], axis=1)
     extra = jnp.broadcast_to(jnp.pad(extra, ((0, 0), (0, 30)))[None], (2, depth, 32))
-    packed = jnp.concatenate([two(q_weight), two(k_weight), two(v_weight), extra], axis=2)
-    compact = packed.shape[2]
-    in_blk = in_order(y, pick(packed, y), pp(pick(packed, 1 - y), "ctx", 1)).reshape(2 * depth, -1)
-    w_in = place(gather_z({0: in_blk}, n_z), z, 0)
-
+    in_send = jnp.concatenate([two(q_weight), two(k_weight), two(v_weight), extra], axis=2)
+    compact = in_send.shape[2]
+    o_send = o_weight.reshape(2, q_cols, depth).transpose(0, 2, 1)
+
+    def four(w):
+        return w.reshape(depth, 2, 2, units).transpose(2, 1, 0, 3)
+
+    wide = -(-2 * units // LANES) * LANES
+    w3_send = jnp.concatenate(
+        [
+            four(gate_weight),
+            four(up_weight),
+            jnp.zeros((2, 2, depth, wide - 2 * units), BF16),
+            down_weight.reshape(2, 2, units, depth).transpose(1, 0, 3, 2),
+        ],
+        axis=3,
+    )
     x_here = tokens.reshape(half_len, width)
-    x_half = pp(pick(x_here.reshape(2, half_len // 2, width), t % 2), "ctx", 1)
-    x_other = in_order(t % 2, x_half, pp(x_half, "tp", 1)).reshape(half_len, width)
-    x_all = in_order(y, x_here, x_other).reshape(full_len, width)
-
-    o_two = o_weight.reshape(2, q_cols, depth)
-    o_blk = jnp.concatenate(
-        list(in_order(y, pick(o_two, y), pp(pick(o_two, 1 - y), "ctx", 1))), axis=1
-    )
-    w_o = place(gather_z({0: o_blk}, n_z), z, 1)
-
-    def four(w):
-        return w.reshape(depth, 2, 2, units).transpose(1, 2, 0, 3)
-
-    gu = jnp.concatenate([four(gate_weight), four(up_weight)], axis=3)
-    gu_y = gu.transpose(1, 0, 2, 3)
-    gu_blk = in_order(y, pick(gu_y, y), pp(pick(gu_y, 1 - y), "ctx", 1), axis=1).reshape(
-        2, 2 * depth, 2 * units
-    )
-    w_gu = place(
-        gather_z({0: pick(gu_blk, zb), n_z // 2: pp(pick(gu_blk, 1 - zb), "fsdp", n_z // 2)}, n_z // 2),
-        z,
-        0,
-    )
-    dn_y = down_weight.reshape(2, 2, units, depth).transpose(1, 0, 2, 3)
-    dn_pair = in_order(y, pick(dn_y, y), pp(pick(dn_y, 1 - y), "ctx", 1))
-    dn_blk = jnp.concatenate([dn_pair[0], dn_pair[1]], axis=2)
-    w_dn = place(
-        gather_z({0: pick(dn_blk, zb), n_z // 2: pp(pick(dn_blk, 1 - zb), "fsdp", n_z // 2)}, n_z // 2),
-        z,
-        1,
-    )
 
     seg = segments.reshape(full_len)
     start = jnp.sum((seg[None, :] < seg[:, None]).astype(jnp.int32), axis=1)
@@ -330,26 +769,18 @@
         == ((c320 // HEAD_DIM) * LANES + c320 % HEAD_DIM)[None, :]
     ).astype(BF16)
 
-    gain_one = w_in[:, compact - 32].astype(F32)[None, :]
-    gain_two = w_in[:, compact - 31].astype(F32)[None, :]
-    w_heads = dot(w_in, spread).astype(BF16)
-    x_f32 = x_all.astype(F32)
-    root_all = lax.rsqrt(jnp.mean(x_f32 * x_f32, axis=1, keepdims=True) + NORM_EPS)
-    norm_attn = (x_f32 * root_all * gain_one).astype(BF16)
-    qkv = dot(norm_attn, w_heads)
-    attn, rot, stats = attend(qkv, cos, sin, seg_col, seg_row, sel, scale)
+    w_heads, w_o, w3, gains, norm_attn, dy_all, norm_all, attn, rot, stats, mid = front(
+        n_z, n_tp, scale, x_here, cotangent.reshape(half_len, width), in_send, o_send, w3_send,
+        cos, sin, seg_col, seg_row, spread, sel,
+    )
+    gain_one, gain_two = gains[0:1], gains[1:2]
+    w_o = w_o.reshape(width, q_cols)
+    w3 = w3.reshape(width, -1)
+    w_gu, w_dn = w3[:, : 2 * units], w3[:, wide:]
+    x_mine = lax.dynamic_slice_in_dim(x_here, t * rows, rows, 0).astype(F32)
+    root_ffn = lax.rsqrt(jnp.mean(mid * mid, axis=1, keepdims=True) + NORM_EPS)
+    dy_mine = lax.dynamic_slice_in_dim(cotangent.reshape(half_len, width), t * rows, rows, 0)
     attn_rel = by_xor(attn, 2 * n_tp, me)
-    x_mine = lax.dynamic_slice_in_dim(x_here, t * rows, rows, 0).astype(F32)
-    mid = x_mine + scatter_layer(attn_rel.reshape(2, 2, 2, rows, q_cols), w_o)
-    root_ffn = lax.rsqrt(jnp.mean(mid * mid, axis=1, keepdims=True) + NORM_EPS)
-    norm_ffn = (mid * root_ffn * gain_two).astype(BF16)
-
-    def both(own):
-        return gather_layer(own), gather_layer(pp(own, "fsdp", n_z // 2))
-
-    dy_mine = lax.dynamic_slice_in_dim(cotangent.reshape(half_len, width), t * rows, rows, 0)
-    dy_pair = both(dy_mine)
-    norm_pair = both(norm_ffn)
 
     def mlp(norm, dy):
         norm = norm.reshape(full_len, width)
@@ -358,26 +789,26 @@
         gate, up = gate_up[:, :units], gate_up[:, units:]
         sig = jax.nn.sigmoid(gate)
         hidden = (gate * sig * up).astype(BF16)
-        d_hidden = dot(dy, w_dn, ((1,), (1,)))
+        d_hidden = dot(dy, w_dn)
         d_up = (d_hidden * gate * sig).astype(BF16)
         d_gate = (d_hidden * up * sig * (1.0 + gate * (1.0 - sig))).astype(BF16)
         return hidden, jnp.concatenate([d_gate, d_up], axis=1), norm, dy
 
-    own_mlp, far_mlp = mlp(norm_pair[0], dy_pair[0]), mlp(norm_pair[1], dy_pair[1])
+    own_mlp, far_mlp = mlp(norm_all[0], dy_all[0]), mlp(norm_all[1], dy_all[1])
 
     def shape8(v):
-        return v.reshape(2, 2, 2, rows, v.shape[-1])
+        return by_xor(v, 2 * n_tp, me).reshape(2, 2, 2, rows, v.shape[-1])
 
     def scatter_both(own, far, rhs, dims=((1,), (0,))):
         sent = pp(scatter_layer(shape8(far), rhs, dims).astype(BF16), "fsdp", n_z // 2)
         return scatter_layer(shape8(own), rhs, dims) + sent.astype(F32)
 
     d_norm = scatter_both(own_mlp[1], far_mlp[1], w_gu, ((1,), (1,)))
-    ffn = scatter_both(own_mlp[0], far_mlp[0], w_dn)
+    ffn = scatter_both(own_mlp[0], far_mlp[0], w_dn, ((1,), (1,)))
     output = gather_tp((mid + ffn).astype(BF16))
 
     gu_g = dot(own_mlp[2], own_mlp[1], ((0,), (0,))) + dot(far_mlp[2], far_mlp[1], ((0,), (0,)))
-    dn_g = dot(own_mlp[0], own_mlp[3], ((0,), (0,))) + dot(far_mlp[0], far_mlp[3], ((0,), (0,)))
+    dn_g = dot(own_mlp[3], own_mlp[0], ((0,), (0,))) + dot(far_mlp[3], far_mlp[0], ((0,), (0,)))
 
     def norm_back(inputs, root, gain, d_normed):
         scaled = d_normed * gain
@@ -387,12 +818,11 @@
 
     d_mid = dy_mine.astype(F32) + norm_back(mid, root_ffn, gain_two, d_norm)
     d_proj = gather_layer(d_mid.astype(BF16)).reshape(full_len, width)
-    o_g = dot(attn_rel.reshape(full_len, q_cols), d_proj, ((0,), (0,)))
-    d_attn = dot(d_proj, w_o, ((1,), (1,))).astype(BF16)
+    o_g = dot(d_proj, attn_rel.reshape(full_len, q_cols), ((0,), (0,)))
+    d_attn = dot(d_proj, w_o).astype(BF16)
     d_attn = by_xor(d_attn, 2 * n_tp, me).reshape(full_len, q_cols)
     d_qkv = attend_back(rot, d_attn, stats, cos, sin, seg_col, seg_row, sel, scale)
-    d_rel = by_xor(d_qkv, 2 * n_tp, me)
-    d_norm_attn = scatter_layer(shape8(d_rel), w_heads, ((1,), (1,)))
+    d_norm_attn = scatter_layer(shape8(d_qkv), w_heads, ((1,), (1,)))
     root_mine = lax.rsqrt(jnp.mean(x_mine * x_mine, axis=1, keepdims=True) + NORM_EPS)
     d_in = d_mid + norm_back(x_mine, root_mine, gain_one, d_norm_attn)
     input_grad = gather_tp(d_in.astype(BF16))
@@ -414,12 +844,12 @@
     gate_grad = gu_four[..., :units].reshape(depth, 4 * units)
     up_grad = gu_four[..., units:].reshape(depth, 4 * units)
 
-    dn_two = half_z(split_z(dn_g, n_z, z, 1))
-    dn_four = to_owner_y(dn_two.reshape(2, units, 2, depth).transpose(2, 0, 1, 3), 1)
-    down_grad = dn_four.transpose(1, 0, 2, 3).reshape(4 * units, depth)
-
-    o_one = scatter_z(split_z(o_g, n_z, z, 1), n_z)[0]
-    o_grad = to_owner_y(o_one.reshape(q_cols, 2, depth).transpose(1, 0, 2), 1).reshape(
+    dn_two = half_z(split_z(dn_g, n_z, z, 0))
+    dn_four = to_owner_y(dn_two.reshape(2, 2, depth, units).transpose(1, 0, 2, 3), 0)
+    down_grad = dn_four.transpose(1, 0, 3, 2).reshape(4 * units, depth)
+
+    o_one = scatter_z(split_z(o_g, n_z, z, 0), n_z)[0]
+    o_grad = to_owner_y(o_one.reshape(2, depth, q_cols), 0).transpose(0, 2, 1).reshape(
         2 * q_cols, depth
     )
 

time: 1080 us -> 895 us (0.83)
  waiting for transfers between devices: 500 us -> 220 us
  Pallas kernels: 27.6 us -> 283 us
  other arithmetic: 136 us -> 57.2 us
  starting transfers between devices: 94.5 us -> 60.6 us
  local copies, waits for them, and re-layouts: 192 us -> 163 us
  matrix products: 119 us -> 100 us
    ppermute x99 -> x54, waiting for transfers between devices: 500 us -> 220 us  [pp(): return lax.ppermute(value, axis, [(i, i ^ mask) for i in range(size)])]
    pallas_call x1, Pallas kernels: 12 us -> 267 us  [front(): pl.pallas_call(lambda *refs: front_kernel(n_z, n_tp, scale, min(256, full...]
    ppermute x99 -> x54, starting transfers between devices: 94.5 us -> 60.6 us  [pp(): return lax.ppermute(value, axis, [(i, i ^ mask) for i in range(size)])]
    select_n x15 -> x9, other arithmetic: 35.6 us -> 12.2 us  [in_order(): jnp.where(bit == 0, jnp.stack([mine, other], axis), jnp.stack([other, min...]
    another operation x10 -> x2, other arithmetic: 27.3 us -> 6.04 us  [gather_layer(): return jnp.stack([mine, pp(mine, 'tp', 1)], axis=2)]
    dot_general x25 -> x21, matrix products: 119 us -> 100 us  [dot(): return lax.dot_general(a, b, (dims, ((), ())), preferred_element_type=F32)]
    concatenate x3 -> x0, other arithmetic: 14 us -> none  [the longest x1 11.3 us: body(): gu = jnp.concatenate([four(gate_weight), four(up_weight)], axis=3)]
    reshape x10 -> x9, local copies, waits for them, and re-layouts: 39 us -> 26.5 us  [the longest x2 9.84 us: four(): return w.reshape(depth, 2, 2, units).transpose(2, 1, 0, 3)]
  transfers between devices with their start and end apart: 99 -> 54, of which waited for: 45 -> 29; matrix products, arithmetic and copies ran while one was open for 40% -> 23% of each run, Pallas kernels for 3% -> 2%
where the time goes in v2:
time: 895 us; the launch traced here: 887 us
  Pallas kernels  283 us (32%)
  waiting for transfers between devices  220 us (25%)
  local copies, waits for them, and re-layouts  163 us (18%)
  matrix products  100 us (11%)
  starting transfers between devices  60.6 us (7%)
  other arithmetic  57.2 us (6%)
    pallas_call x1, Pallas kernels, front(): pl.pallas_call(lambda *refs: front_kernel(n_z, n_tp, scale, min(256, full...  267 us
    ppermute x54, waiting for transfers between devices, pp(): return lax.ppermute(value, axis, [(i, i ^ mask) for i in range(size)])  220 us
    dot_general x21, matrix products, dot(): return lax.dot_general(a, b, (dims, ((), ())), preferred_element_type=F32)  100 us
    ppermute x54, starting transfers between devices, pp(): return lax.ppermute(value, axis, [(i, i ^ mask) for i in range(size)])  60.6 us
    unnamed x202, local copies, waits for them, and re-layouts  34 us
  transfers between devices with their start and end apart: 54, of which 29 were waited for; matrix products, arithmetic and copies ran while one was open for 23% of the time, Pallas kernels for 2%

profile of v2, /device:TPU:0, one launch (start us, length us, event | category | flops | bytes accessed | tf_op | source)
XLA Modules:
  0.0 886.9 jit_solution(656621080147267648)
XLA Ops:
  2.1 4.9 reshape.508
  7.0 4.9 reshape.509
  11.9 5.6 reshape.510
  31.1 3.1 fusion.103
  34.3 6.8 concatenate.74.refs_4_
  42.2 267.5 %front.1 = (bf16[2560,768]{1,0:T(8,128)(2,1)}, bf16[4,2,320,320]{3,2,1,0:T(8,128)(2,1)}, bf16[4,2,320,1328]{3,2,1,0:T(8,128)(2,1)}, f32[8,2560]{1,0:T(8,128)}, b...) custom-call(bf16[512,2560]{1,0:T(8,128)(2,1)} %bitcast.402, ...), custom_call_target="tpu_custom_call" | custom-call | tf_op jit(solution)/shard_map/front/pallas_call | solution.py:653
  309.7 8.8 fusion.145
  318.5 8.9 %fusion.144 = (bf16[1,8,128,2560]{3,2,1,0:T(8,128)(2,1)}, bf16[1,8,128,2560]{3,2,1,0:T(8,128)(2,1)}) fusion(bf16[2,8,128,2560]{3,2,1,0:T(8,128)(2,1)} %get-tuple-element.25), kind=kLoop, calls=%fused_computation.405 | loop fusion | bytes 20971520 | tf_op jit(solution)/shard_map/slice | solution.py:797
  327.4 8.2 fusion.40
  335.7 5.1 multiply_convert_fusion.3
  343.3 7.4 fusion.38
  350.7 6.3 multiply_convert_fusion.1
  357.9 4.6 convolution_add_fusion.1
  365.2 11.3 %collective-permute-start.50 = (bf16[640,432]{0,1:T(8,128)(2,1)}, bf16[640,432]{0,1:T(8,128)(2,1)}, u32[]{:S(2)}, u32[]{:S(2)}) collective-permute-start(bf16[640,432]{0,1:T(8,128)(2,1)} %get-tuple-element.130), channel_id=1, source_target_pairs={{0,8},{8,0},{16,24},{24,16},{1,9},{9,1},{17,25},{25,17},{2,10},{10... | collective-permute-start | bytes 1658888 | tf_op jit(solution)/shard_map/ppermute | solution.py:22
  381.0 4.9 convolution_convert_fusion.2
  386.2 4.7 fusion.68
  391.0 4.7 convolution_add_fusion
  395.7 3.5 copy-done.13
  412.6 3.7 constant_dynamic-slice_fusion.11
  418.6 3.7 constant_dynamic-slice_fusion.3
  425.2 7.2 fusion.13
  434.0 3.2 convolution_convert_fusion.1
  438.7 4.7 fusion.16
  444.0 2.9 convert_add_fusion.8
  446.9 4.9 collective-permute-done.41
  451.8 2.8 collective-permute-start.52
  454.6 3.2 convert_add_fusion.5
  458.1 3.3 convert_add_fusion.4
  466.8 3.0 convert_add_fusion.2
  472.1 4.7 convert_add_fusion.1
  477.0 3.4 collective-permute-done.1
  483.6 10.9 %collective-permute-done.6 = bf16[2,128,1280]{2,1,0:T(8,128)(2,1)S(1)} collective-permute-done((bf16[2,128,1280]{2,1,0:T(8,128)(2,1)S(1)}, bf16[2,128,1280]{2,1,0:T(8,128)(2,1)S(1)}, u32[]{:S(2)}, u32[]{:S(2)}) %collective-permute-start.6) | collective-permute-done | bytes 655392 | tf_op jit(solution)/shard_map/ppermute | solution.py:22
  497.6 10.9 %collective-permute-done.14 = bf16[2,128,1280]{2,1,0:T(8,128)(2,1)S(1)} collective-permute-done((bf16[2,128,1280]{2,1,0:T(8,128)(2,1)S(1)}, bf16[2,128,1280]{2,1,0:T(8,128)(2,1)S(1)}, u32[]{:S(2)}, u32[]{:S(2)}) %collective-permute-start.14) | collective-permute-done | bytes 655392 | tf_op jit(solution)/shard_map/ppermute | solution.py:22
  511.6 9.3 %collective-permute-done.19 = bf16[2,128,1280]{2,1,0:T(8,128)(2,1)S(1)} collective-permute-done((bf16[2,128,1280]{2,1,0:T(8,128)(2,1)S(1)}, bf16[2,128,1280]{2,1,0:T(8,128)(2,1)S(1)}, u32[]{:S(2)}, u32[]{:S(2)}) %collective-permute-start.19) | collective-permute-done | bytes 655392 | tf_op jit(solution)/shard_map/ppermute | solution.py:22
  522.2 4.0 collective-permute-done.21
  528.2 5.0 collective-permute-done.2
  535.4 4.8 collective-permute-done.7
  545.1 6.6 collective-permute-done.20
  552.4 6.3 collective-permute-done.22
  562.0 52.7 %collective-permute-done.23 = bf16[128,2560]{1,0:T(8,128)(2,1)S(1)} collective-permute-done((bf16[128,2560]{1,0:T(8,128)(2,1)S(1)}, bf16[128,2560]{1,0:T(8,128)(2,1)S(1)}, u32[]{:S(2)}, u32[]{:S(2)}) %collective-permute-start.23) | collective-permute-done | bytes 655392 | tf_op jit(solution)/shard_map/ppermute | solution.py:22
  615.2 2.9 fusion.143
  651.2 3.8 fusion.142
  658.7 6.5 collective-permute-done.53
  668.8 4.2 reshape.533
  674.8 12.2 %collective-permute-done.43 = bf16[2,320,864]{2,1,0:T(8,128)(2,1)} collective-permute-done((bf16[2,320,864]{2,1,0:T(8,128)(2,1)}, bf16[2,320,864]{2,1,0:T(8,128)(2,1)}, u32[]{:S(2)}, u32[]{:S(2)}) %collective-permute-start.43) | collective-permute-done | bytes 1105952 | tf_op jit(solution)/shard_map/ppermute | solution.py:22
  690.2 3.5 copy.436
  693.7 4.6 reshape.528
  698.3 3.5 copy.435
  701.8 5.1 reshape.527
  714.2 3.2 fusion.147
  724.8 15.6 %attend_back.1 = bf16[1024,768]{1,0:T(8,128)(2,1)} custom-call(bf16[1024,768]{1,0:T(8,128)(2,1)} %get-tuple-element.27.refs_0_, bf16[1024,320]{1,0:T(8,128)(2,1)} %bitcast.491, f32[1024,8]{1,0:T(8,128)} %get-tuple-element.29.refs_2_, f32[1024,128]{1,0:T(8,128)} %get-tuple-element.198.refs_5_.refs_3_, f32[1024,128]{1,0:T(8,128)} %get-tuple-element.197.refs_6_.refs_4_, ...), custom_call_target="tpu_custom_call" | custom-call | flops 2684354560 | bytes 4718592 | tf_op jit(solution)/shard_map/attend_back/pallas_call | solution.py:106
  740.5 9.1 %fusion.87 = f32[2560,512]{1,0:T(8,128)} fusion(bf16[1024,2560]{1,0:T(8,128)(2,1)} %get-tuple-element.31, bf16[1024,768]{1,0:T(8,128)(2,1)} %attend_back.1, s32[512]{0:T(512)S(1)} %copy-done.46), kind=kOutput, calls=%fused_computation.172 | convolution fusion | flops 3490578432 | bytes 12060672 | tf_op jit(solution)/shard_map/dot_general | solution.py:26
  749.6 2.8 dynamic-slice_convert_fusion.5
  756.1 3.7 convolution_convert_fusion
  765.4 4.6 collective-permute-done.37
  779.4 20.9 %collective-permute-done.46 = bf16[640,320]{0,1:T(8,128)(2,1)S(1)} collective-permute-done((bf16[640,320]{0,1:T(8,128)(2,1)}, bf16[640,320]{0,1:T(8,128)(2,1)S(1)}, u32[]{:S(2)}, u32[]{:S(2)}) %collective-permute-start.46) | collective-permute-done | bytes 409632 | tf_op jit(solution)/shard_map/ppermute | solution.py:22
  800.8 12.7 %collective-permute-done.36 = bf16[640,512]{1,0:T(8,128)(2,1)S(1)} collective-permute-done((bf16[640,512]{1,0:T(8,128)(2,1)}, bf16[640,512]{1,0:T(8,128)(2,1)S(1)}, u32[]{:S(2)}, u32[]{:S(2)}) %collective-permute-start.36) | collective-permute-done | bytes 655392 | tf_op jit(solution)/shard_map/ppermute | solution.py:22
  813.5 4.3 collective-permute-done.38
  823.8 4.9 collective-permute-done.39
  829.9 5.2 convert_add_fusion
  838.1 10.8 %collective-permute-done.30 = bf16[2,128,1280]{2,1,0:T(8,128)(2,1)S(1)} collective-permute-done((bf16[2,128,1280]{2,1,0:T(8,128)(2,1)S(1)}, bf16[2,128,1280]{2,1,0:T(8,128)(2,1)S(1)}, u32[]{:S(2)}, u32[]{:S(2)}) %collective-permute-start.30) | collective-permute-done | bytes 655392 | tf_op jit(solution)/shard_map/ppermute | solution.py:22
  853.7 5.0 collective-permute-done.31
  858.7 3.9 collective-permute-done.33
  866.5 7.8 collective-permute-done.34
  (446 shorter events, 190.8 us)
Async XLA Ops:
  0.7 19.5 %copy-start.45 = (s32[512]{0:T(512)}, s32[512]{0:T(512)S(1)}, u32[]{:S(2)}) copy-start(s32[512]{0:T(512)S(1)} %fusion.130) | copy-start | bytes 6148
  327.4 15.9 %slice-start.4 = ((s8[5242880]{0:T(1024)(128)(4,1)}), s8[4194304]{0:T(1024)(128)(4,1)S(1)}, s32[]{:S(2)}) async-start(s8[5242880]{0:T(1024)(128)(4,1)} %bitcast.405), calls=%async_computation.4 | async-start | bytes 8388608
  340.7 45.4 %copy-start.28 = (bf16[1024,432]{0,1:T(8,128)(2,1)}, bf16[1024,432]{0,1:T(8,128)(2,1)S(1)}, u32[]{:S(2)}) copy-start(bf16[1024,432]{0,1:T(8,128)(2,1)S(1)} %get-tuple-element.111) | copy-start | bytes 2654212
  357.0 34.0 %copy-start.30 = (bf16[1024,432]{0,1:T(8,128)(2,1)}, bf16[1024,432]{0,1:T(8,128)(2,1)S(1)}, u32[]{:S(2)}) copy-start(bf16[1024,432]{0,1:T(8,128)(2,1)S(1)} %get-tuple-element.112) | copy-start | bytes 2654212
  365.2 73.4 %collective-permute-start.50 = (bf16[640,432]{0,1:T(8,128)(2,1)}, bf16[640,432]{0,1:T(8,128)(2,1)}, u32[]{:S(2)}, u32[]{:S(2)}) collective-permute-start(bf16[640,432]{0,1:T(8,128)(2,1)} %get-tuple-element.130), channel_id=1, source_target_pairs={{0,8},{8,0},{16,24},{24,16},{1,9},{9,1},{17,25},{25,17},{2,10},{10... | collective-permute-start | bytes 1658888 | tf_op jit(solution)/shard_map/ppermute | solution.py:22
  376.6 66.8 %collective-permute-start.51 = (bf16[640,432]{0,1:T(8,128)(2,1)}, bf16[640,432]{0,1:T(8,128)(2,1)}, u32[]{:S(2)}, u32[]{:S(2)}) collective-permute-start(bf16[640,432]{0,1:T(8,128)(2,1)} %get-tuple-element.131), channel_id=1, source_target_pairs={{0,8},{8,0},{16,24},{24,16},{1,9},{9,1},{17,25},{25,17},{2,10},{10... | collective-permute-start | bytes 1658888 | tf_op jit(solution)/shard_map/ppermute | solution.py:22
  385.9 71.9 %collective-permute-start = (bf16[2,2,128,2560]{3,2,0,1:T(8,128)(2,1)}, bf16[2,2,128,2560]{3,2,0,1:T(8,128)(2,1)}, u32[]{:S(2)}, u32[]{:S(2)}) collective-permute-start(bf16[2,2,128,2560]{3,2,0,1:T(8,128)(2,1)} %convolution_convert_fusion.2), channel_id=1, source_target_pairs={{0,1},{1,0},{2,3},{3,2},{4,5},{5,4},{6,7},{7,6},{8,9},{9,8},{10,11... | collective-permute-start | bytes 7864328 | tf_op jit(solution)/shard_map/ppermute | solution.py:22
  400.9 45.9 %collective-permute-start.40 = (bf16[640,864]{0,1:T(8,128)(2,1)}, bf16[640,864]{0,1:T(8,128)(2,1)}, u32[]{:S(2)}, u32[]{:S(2)}) collective-permute-start(bf16[640,864]{0,1:T(8,128)(2,1)} %get-tuple-element.108), channel_id=1, source_target_pairs={{0,8},{8,0},{16,24},{24,16},{1,9},{9,1},{17,25},{25,17},{2,10},{10... | collective-permute-start | bytes 3317768 | tf_op jit(solution)/shard_map/ppermute | solution.py:22
  402.7 49.1 %collective-permute-start.41 = (bf16[640,864]{0,1:T(8,128)(2,1)}, bf16[640,864]{0,1:T(8,128)(2,1)}, u32[]{:S(2)}, u32[]{:S(2)}) collective-permute-start(bf16[640,864]{0,1:T(8,128)(2,1)} %get-tuple-element.109), channel_id=1, source_target_pairs={{0,8},{8,0},{16,24},{24,16},{1,9},{9,1},{17,25},{25,17},{2,10},{10... | collective-permute-start | bytes 3317768 | tf_op jit(solution)/shard_map/ppermute | solution.py:22
  438.7 23.8 %collective-permute-start.5 = (bf16[2,2,128,2560]{3,2,0,1:T(8,128)(2,1)}, bf16[2,2,128,2560]{3,2,0,1:T(8,128)(2,1)S(1)}, u32[]{:S(2)}, u32[]{:S(2)}) collective-permute-start(bf16[2,2,128,2560]{3,2,0,1:T(8,128)(2,1)} %convolution_convert_fusion.1), channel_id=1, source_target_pairs={{0,1},{1,0},{2,3},{3,2},{4,5},{5,4},{6,7},{7,6},{8,9},{9,8},{10,11... | collective-permute-start | bytes 7864328 | tf_op jit(solution)/shard_map/ppermute | solution.py:22
  438.7 15.9 %slice-start.10 = ((s8[8847360]{0:T(1024)(128)(4,1)}), s8[4194304]{0:T(1024)(128)(4,1)S(1)}, s32[]{:S(2)}) async-start(s8[8847360]{0:T(1024)(128)(4,1)} %bitcast.422), calls=%async_computation.10 | async-start | bytes 8388608
  438.7 15.9 %slice-start.11 = ((s8[8847360]{0:T(1024)(128)(4,1)}), s8[4194304]{0:T(1024)(128)(4,1)S(1)}, s32[]{:S(2)}) async-start(s8[8847360]{0:T(1024)(128)(4,1)} %bitcast.422), calls=%async_computation.11 | async-start | bytes 8388608
  438.7 15.9 %slice-start.12 = ((s8[8847360]{0:T(1024)(128)(4,1)}), s8[458752]{0:T(1024)(128)(4,1)S(1)}, s32[]{:S(2)}) async-start(s8[8847360]{0:T(1024)(128)(4,1)} %bitcast.422), calls=%async_computation.12 | async-start | bytes 917504
  443.4 22.4 %collective-permute-start.13 = (bf16[2,2,128,2560]{3,2,0,1:T(8,128)(2,1)}, bf16[2,2,128,2560]{3,2,0,1:T(8,128)(2,1)S(1)}, u32[]{:S(2)}, u32[]{:S(2)}) collective-permute-start(bf16[2,2,128,2560]{3,2,0,1:T(8,128)(2,1)} %fusion.13), channel_id=1, source_target_pairs={{0,1},{1,0},{2,3},{3,2},{4,5},{5,4},{6,7},{7,6},{8,9},{9,8},{10,11... | collective-permute-start | bytes 7864328 | tf_op jit(solution)/shard_map/ppermute | solution.py:22
  446.8 23.1 %collective-permute-start.18 = (bf16[2,2,128,2560]{3,2,0,1:T(8,128)(2,1)}, bf16[2,2,128,2560]{3,2,0,1:T(8,128)(2,1)}, u32[]{:S(2)}, u32[]{:S(2)}) collective-permute-start(bf16[2,2,128,2560]{3,2,0,1:T(8,128)(2,1)} %fusion.16), channel_id=1, source_target_pairs={{0,1},{1,0},{2,3},{3,2},{4,5},{5,4},{6,7},{7,6},{8,9},{9,8},{10,11... | collective-permute-start | bytes 7864328 | tf_op jit(solution)/shard_map/ppermute | solution.py:22
  451.8 176.7 %collective-permute-start.52 = (bf16[640,432]{0,1:T(8,128)(2,1)}, bf16[640,432]{0,1:T(8,128)(2,1)}, u32[]{:S(2)}, u32[]{:S(2)}) collective-permute-start(bf16[640,432]{0,1:T(8,128)(2,1)} %get-tuple-element.129), channel_id=1, source_target_pairs={{0,16},{8,24},{16,0},{24,8},{1,17},{9,25},{17,1},{25,9},{2,18},{10... | collective-permute-start | bytes 1658888 | tf_op jit(solution)/shard_map/ppermute | solution.py:22
  457.8 184.6 %collective-permute-start.42 = (bf16[640,864]{0,1:T(8,128)(2,1)}, bf16[640,864]{0,1:T(8,128)(2,1)}, u32[]{:S(2)}, u32[]{:S(2)}) collective-permute-start(bf16[640,864]{0,1:T(8,128)(2,1)} %get-tuple-element.107), channel_id=1, source_target_pairs={{0,16},{8,24},{16,0},{24,8},{1,17},{9,25},{17,1},{25,9},{2,18},{10... | collective-permute-start | bytes 3317768 | tf_op jit(solution)/shard_map/ppermute | solution.py:22
  462.5 17.9 %collective-permute-start.1 = (bf16[2,128,1280]{2,1,0:T(8,128)(2,1)}, bf16[2,128,1280]{2,1,0:T(8,128)(2,1)S(1)}, u32[]{:S(2)}, u32[]{:S(2)}) collective-permute-start(bf16[2,128,1280]{2,1,0:T(8,128)(2,1)} %slice_bitcast_fusion.35), channel_id=1, source_target_pairs={{0,2},{1,3},{2,0},{3,1},{4,6},{5,7},{6,4},{7,5},{8,10},{9,11},{10,... | collective-permute-start | bytes 1966088 | tf_op jit(solution)/shard_map/ppermute | solution.py:22
  465.8 17.1 %collective-permute-start.3 = (bf16[2,128,1280]{2,1,0:T(8,128)(2,1)S(1)}, bf16[2,128,1280]{2,1,0:T(8,128)(2,1)S(1)}, u32[]{:S(2)}, u32[]{:S(2)}) collective-permute-start(bf16[2,128,1280]{2,1,0:T(8,128)(2,1)S(1)} %slice_bitcast_fusion.33), channel_id=1, source_target_pairs={{0,4},{4,0},{1,5},{5,1},{2,6},{6,2},{3,7},{7,3},{8,12},{12,8},{9,1... | collective-permute-start | bytes 1966088 | tf_op jit(solution)/shard_map/ppermute | solution.py:22
  470.0 24.5 %collective-permute-start.6 = (bf16[2,128,1280]{2,1,0:T(8,128)(2,1)S(1)}, bf16[2,128,1280]{2,1,0:T(8,128)(2,1)S(1)}, u32[]{:S(2)}, u32[]{:S(2)}) collective-permute-start(bf16[2,128,1280]{2,1,0:T(8,128)(2,1)S(1)} %slice_bitcast_fusion.31), channel_id=1, source_target_pairs={{0,2},{1,3},{2,0},{3,1},{4,6},{5,7},{6,4},{7,5},{8,10},{9,11},{10,... | collective-permute-start | bytes 1966088 | tf_op jit(solution)/shard_map/ppermute | solution.py:22
  480.4 16.5 %collective-permute-start.8 = (bf16[2,128,1280]{2,1,0:T(8,128)(2,1)S(1)}, bf16[2,128,1280]{2,1,0:T(8,128)(2,1)S(1)}, u32[]{:S(2)}, u32[]{:S(2)}) collective-permute-start(bf16[2,128,1280]{2,1,0:T(8,128)(2,1)S(1)} %slice_bitcast_fusion.29), channel_id=1, source_target_pairs={{0,4},{4,0},{1,5},{5,1},{2,6},{6,2},{3,7},{7,3},{8,12},{12,8},{9,1... | collective-permute-start | bytes 1966088 | tf_op jit(solution)/shard_map/ppermute | solution.py:22
  482.9 25.6 %collective-permute-start.14 = (bf16[2,128,1280]{2,1,0:T(8,128)(2,1)S(1)}, bf16[2,128,1280]{2,1,0:T(8,128)(2,1)S(1)}, u32[]{:S(2)}, u32[]{:S(2)}) collective-permute-start(bf16[2,128,1280]{2,1,0:T(8,128)(2,1)S(1)} %slice_bitcast_fusion.27), channel_id=1, source_target_pairs={{0,2},{1,3},{2,0},{3,1},{4,6},{5,7},{6,4},{7,5},{8,10},{9,11},{10,... | collective-permute-start | bytes 1966088 | tf_op jit(solution)/shard_map/ppermute | solution.py:22
  483.2 28.0 %slice-start.17 = ((s8[5242880]{0:T(1024)(128)(4,1)}), s8[1048576]{0:T(1024)(128)(4,1)S(1)}, s32[]{:S(2)}) async-start(s8[5242880]{0:T(1024)(128)(4,1)} %bitcast.454), calls=%async_computation.17 | async-start | bytes 2097152
  483.6 27.6 %slice-start.18 = ((s8[5242880]{0:T(1024)(128)(4,1)}), s8[4194304]{0:T(1024)(128)(4,1)S(1)}, s32[]{:S(2)}) async-start(s8[5242880]{0:T(1024)(128)(4,1)} %bitcast.454), calls=%async_computation.18 | async-start | bytes 8388608
  494.5 16.5 %collective-permute-start.16 = (bf16[2,128,1280]{2,1,0:T(8,128)(2,1)S(1)}, bf16[2,128,1280]{2,1,0:T(8,128)(2,1)S(1)}, u32[]{:S(2)}, u32[]{:S(2)}) collective-permute-start(bf16[2,128,1280]{2,1,0:T(8,128)(2,1)S(1)} %slice_bitcast_fusion.25), channel_id=1, source_target_pairs={{0,4},{4,0},{1,5},{5,1},{2,6},{6,2},{3,7},{7,3},{8,12},{12,8},{9,1... | collective-permute-start | bytes 1966088 | tf_op jit(solution)/shard_map/ppermute | solution.py:22
  497.0 23.9 %collective-permute-start.19 = (bf16[2,128,1280]{2,1,0:T(8,128)(2,1)S(1)}, bf16[2,128,1280]{2,1,0:T(8,128)(2,1)S(1)}, u32[]{:S(2)}, u32[]{:S(2)}) collective-permute-start(bf16[2,128,1280]{2,1,0:T(8,128)(2,1)S(1)} %slice_bitcast_fusion.23), channel_id=1, source_target_pairs={{0,2},{1,3},{2,0},{3,1},{4,6},{5,7},{6,4},{7,5},{8,10},{9,11},{10,... | collective-permute-start | bytes 1966088 | tf_op jit(solution)/shard_map/ppermute | solution.py:22
  508.5 17.7 %collective-permute-start.21 = (bf16[2,128,1280]{2,1,0:T(8,128)(2,1)S(1)}, bf16[2,128,1280]{2,1,0:T(8,128)(2,1)S(1)}, u32[]{:S(2)}, u32[]{:S(2)}) collective-permute-start(bf16[2,128,1280]{2,1,0:T(8,128)(2,1)S(1)} %slice_bitcast_fusion.21), channel_id=1, source_target_pairs={{0,4},{4,0},{1,5},{5,1},{2,6},{6,2},{3,7},{7,3},{8,12},{12,8},{9,1... | collective-permute-start | bytes 1966088 | tf_op jit(solution)/shard_map/ppermute | solution.py:22
  511.0 22.2 %collective-permute-start.2 = (bf16[128,1280]{1,0:T(8,128)(2,1)S(1)}, bf16[128,1280]{1,0:T(8,128)(2,1)S(1)}, u32[]{:S(2)}, u32[]{:S(2)}) collective-permute-start(bf16[128,1280]{1,0:T(8,128)(2,1)S(1)} %fusion.108), channel_id=1, source_target_pairs={{0,4},{4,0},{1,5},{5,1},{2,6},{6,2},{3,7},{7,3},{8,12},{12,8},{9,1... | collective-permute-start | bytes 983048 | tf_op jit(solution)/shard_map/ppermute | solution.py:22
  520.9 13.9 %collective-permute-start.4 = (bf16[128,1280]{1,0:T(8,128)(2,1)S(1)}, bf16[128,1280]{1,0:T(8,128)(2,1)S(1)}, u32[]{:S(2)}, u32[]{:S(2)}) collective-permute-start(bf16[128,1280]{1,0:T(8,128)(2,1)S(1)} %fusion.109), channel_id=1, source_target_pairs={{0,2},{1,3},{2,0},{3,1},{4,6},{5,7},{6,4},{7,5},{8,10},{9,11},{10,... | collective-permute-start | bytes 983048 | tf_op jit(solution)/shard_map/ppermute | solution.py:22
  526.2 14.0 %collective-permute-start.7 = (bf16[128,1280]{1,0:T(8,128)(2,1)S(1)}, bf16[128,1280]{1,0:T(8,128)(2,1)S(1)}, u32[]{:S(2)}, u32[]{:S(2)}) collective-permute-start(bf16[128,1280]{1,0:T(8,128)(2,1)S(1)} %fusion.110), channel_id=1, source_target_pairs={{0,4},{4,0},{1,5},{5,1},{2,6},{6,2},{3,7},{7,3},{8,12},{12,8},{9,1... | collective-permute-start | bytes 983048 | tf_op jit(solution)/shard_map/ppermute | solution.py:22
  533.2 9.7 %collective-permute-start.9 = (bf16[128,1280]{1,0:T(8,128)(2,1)S(1)}, bf16[128,1280]{1,0:T(8,128)(2,1)S(1)}, u32[]{:S(2)}, u32[]{:S(2)}) collective-permute-start(bf16[128,1280]{1,0:T(8,128)(2,1)S(1)} %fusion.111), channel_id=1, source_target_pairs={{0,2},{1,3},{2,0},{3,1},{4,6},{5,7},{6,4},{7,5},{8,10},{9,11},{10,... | collective-permute-start | bytes 983048 | tf_op jit(solution)/shard_map/ppermute | solution.py:22
  534.8 26.5 %collective-permute-start.15 = (bf16[128,1280]{1,0:T(8,128)(2,1)S(1)}, bf16[128,1280]{1,0:T(8,128)(2,1)S(1)}, u32[]{:S(2)}, u32[]{:S(2)}) collective-permute-start(bf16[128,1280]{1,0:T(8,128)(2,1)S(1)} %fusion.112), channel_id=1, source_target_pairs={{0,4},{4,0},{1,5},{5,1},{2,6},{6,2},{3,7},{7,3},{8,12},{12,8},{9,1... | collective-permute-start | bytes 983048 | tf_op jit(solution)/shard_map/ppermute | solution.py:22
  540.2 21.7 %collective-permute-start.17 = (bf16[128,1280]{1,0:T(8,128)(2,1)S(1)}, bf16[128,1280]{1,0:T(8,128)(2,1)S(1)}, u32[]{:S(2)}, u32[]{:S(2)}) collective-permute-start(bf16[128,1280]{1,0:T(8,128)(2,1)S(1)} %fusion.113), channel_id=1, source_target_pairs={{0,2},{1,3},{2,0},{3,1},{4,6},{5,7},{6,4},{7,5},{8,10},{9,11},{10,... | collective-permute-start | bytes 983048 | tf_op jit(solution)/shard_map/ppermute | solution.py:22
  542.9 8.7 collective-permute-start.20
  551.6 7.1 collective-permute-start.22
  558.7 56.4 %collective-permute-start.10 = (bf16[128,2560]{1,0:T(8,128)(2,1)S(1)}, bf16[128,2560]{1,0:T(8,128)(2,1)S(1)}, u32[]{:S(2)}, u32[]{:S(2)}) collective-permute-start(bf16[128,2560]{1,0:T(8,128)(2,1)S(1)} %pad_maximum_fusion.7), channel_id=1, source_target_pairs={{0,16},{8,24},{16,0},{24,8},{1,17},{9,25},{17,1},{25,9},{2,18},{10... | collective-permute-start | bytes 1966088 | tf_op jit(solution)/shard_map/ppermute | solution.py:22
  561.3 53.4 %copy-start.8 = (f32[128,2560]{1,0:T(8,128)S(1)}, f32[128,2560]{1,0:T(8,128)}, u32[]{:S(2)}) copy-start(f32[128,2560]{1,0:T(8,128)} %get-tuple-element.22) | copy-start | bytes 3932164
  561.3 53.4 %collective-permute-start.23 = (bf16[128,2560]{1,0:T(8,128)(2,1)S(1)}, bf16[128,2560]{1,0:T(8,128)(2,1)S(1)}, u32[]{:S(2)}, u32[]{:S(2)}) collective-permute-start(bf16[128,2560]{1,0:T(8,128)(2,1)S(1)} %pad_maximum_fusion.8), channel_id=1, source_target_pairs={{0,16},{8,24},{16,0},{24,8},{1,17},{9,25},{17,1},{25,9},{2,18},{10... | collective-permute-start | bytes 1966088 | tf_op jit(solution)/shard_map/ppermute | solution.py:22
  619.1 11.7 %collective-permute-start.24 = (bf16[128,1280]{1,0:T(8,128)(2,1)}, bf16[128,1280]{1,0:T(8,128)(2,1)}, u32[]{:S(2)}, u32[]{:S(2)}) collective-permute-start(bf16[128,1280]{1,0:T(8,128)(2,1)} %get-tuple-element.194), channel_id=1, source_target_pairs={{0,2},{1,3},{2,0},{3,1},{4,6},{5,7},{6,4},{7,5},{8,10},{9,11},{10,... | collective-permute-start | bytes 983048 | tf_op jit(solution)/shard_map/ppermute | solution.py:22
  622.4 11.0 %collective-permute-start.26 = (bf16[128,1280]{1,0:T(8,128)(2,1)}, bf16[128,1280]{1,0:T(8,128)(2,1)}, u32[]{:S(2)}, u32[]{:S(2)}) collective-permute-start(bf16[128,1280]{1,0:T(8,128)(2,1)} %get-tuple-element.193), channel_id=1, source_target_pairs={{0,4},{4,0},{1,5},{5,1},{2,6},{6,2},{3,7},{7,3},{8,12},{12,8},{9,1... | collective-permute-start | bytes 983048 | tf_op jit(solution)/shard_map/ppermute | solution.py:22
  633.2 18.0 %collective-permute-start.25 = (bf16[2,128,1280]{2,1,0:T(8,128)(2,1)}, bf16[2,128,1280]{2,1,0:T(8,128)(2,1)}, u32[]{:S(2)}, u32[]{:S(2)}) collective-permute-start(bf16[2,128,1280]{2,1,0:T(8,128)(2,1)} %get-tuple-element.190), channel_id=1, source_target_pairs={{0,4},{4,0},{1,5},{5,1},{2,6},{6,2},{3,7},{7,3},{8,12},{12,8},{9,1... | collective-permute-start | bytes 1966088 | tf_op jit(solution)/shard_map/ppermute | solution.py:22
  635.6 15.6 %collective-permute-start.27 = (bf16[2,128,1280]{2,1,0:T(8,128)(2,1)}, bf16[2,128,1280]{2,1,0:T(8,128)(2,1)}, u32[]{:S(2)}, u32[]{:S(2)}) collective-permute-start(bf16[2,128,1280]{2,1,0:T(8,128)(2,1)} %get-tuple-element.196), channel_id=1, source_target_pairs={{0,2},{1,3},{2,0},{3,1},{4,6},{5,7},{6,4},{7,5},{8,10},{9,11},{10,... | collective-permute-start | bytes 1966088 | tf_op jit(solution)/shard_map/ppermute | solution.py:22
  640.0 25.2 %collective-permute-start.53 = (bf16[2,320,432]{2,1,0:T(8,128)(2,1)}, bf16[2,320,432]{2,1,0:T(8,128)(2,1)}, u32[]{:S(2)}, u32[]{:S(2)}) collective-permute-start(bf16[2,320,432]{2,1,0:T(8,128)(2,1)} %fusion.88), channel_id=1, source_target_pairs={{0,4},{4,0},{1,5},{5,1},{2,6},{6,2},{3,7},{7,3},{8,12},{12,8},{9,1... | collective-permute-start | bytes 1658888 | tf_op jit(solution)/shard_map/ppermute | solution.py:22
  648.2 38.9 %collective-permute-start.43 = (bf16[2,320,864]{2,1,0:T(8,128)(2,1)}, bf16[2,320,864]{2,1,0:T(8,128)(2,1)}, u32[]{:S(2)}, u32[]{:S(2)}) collective-permute-start(bf16[2,320,864]{2,1,0:T(8,128)(2,1)} %fusion.66), channel_id=1, source_target_pairs={{0,4},{4,0},{1,5},{5,1},{2,6},{6,2},{3,7},{7,3},{8,12},{12,8},{9,1... | collective-permute-start | bytes 3317768 | tf_op jit(solution)/shard_map/ppermute | solution.py:22
  655.0 56.2 %collective-permute-start.28 = (bf16[2,2,128,2560]{3,2,0,1:T(8,128)(2,1)}, bf16[2,2,128,2560]{3,2,0,1:T(8,128)(2,1)}, u32[]{:S(2)}, u32[]{:S(2)}) collective-permute-start(bf16[2,2,128,2560]{3,2,0,1:T(8,128)(2,1)} %get-tuple-element.137), channel_id=1, source_target_pairs={{0,1},{1,0},{2,3},{3,2},{4,5},{5,4},{6,7},{7,6},{8,9},{9,8},{10,11... | collective-permute-start | bytes 7864328 | tf_op jit(solution)/shard_map/ppermute | solution.py:22
  688.8 20.7 %collective-permute-start.11 = (bf16[128,2560]{1,0:T(8,128)(2,1)S(1)}, bf16[128,2560]{1,0:T(8,128)(2,1)}, u32[]{:S(2)}, u32[]{:S(2)}) collective-permute-start(bf16[128,2560]{1,0:T(8,128)(2,1)S(1)} %get-tuple-element.166), channel_id=1, source_target_pairs={{0,2},{1,3},{2,0},{3,1},{4,6},{5,7},{6,4},{7,5},{8,10},{9,11},{10,... | collective-permute-start | bytes 1966088 | tf_op jit(solution)/shard_map/ppermute | solution.py:22
  711.2 63.7 %collective-permute-start.12 = (bf16[2,128,2560]{2,1,0:T(8,128)(2,1)S(1)}, bf16[2,128,2560]{2,1,0:T(8,128)(2,1)}, u32[]{:S(2)}, u32[]{:S(2)}) collective-permute-start(bf16[2,128,2560]{2,1,0:T(8,128)(2,1)S(1)} %maximum_select_fusion.7), channel_id=1, source_target_pairs={{0,1},{1,0},{2,3},{3,2},{4,5},{5,4},{6,7},{7,6},{8,9},{9,8},{10,11... | collective-permute-start | bytes 3932168 | tf_op jit(solution)/shard_map/ppermute | solution.py:22
  718.6 43.9 %collective-permute-start.47 = (bf16[640,320]{0,1:T(8,128)(2,1)}, bf16[640,320]{0,1:T(8,128)(2,1)S(1)}, u32[]{:S(2)}, u32[]{:S(2)}) collective-permute-start(bf16[640,320]{0,1:T(8,128)(2,1)} %get-tuple-element.135), channel_id=1, source_target_pairs={{0,8},{8,0},{16,24},{24,16},{1,9},{9,1},{17,25},{25,17},{2,10},{10... | collective-permute-start | bytes 1228808 | tf_op jit(solution)/shard_map/ppermute | solution.py:22
  752.4 17.6 %collective-permute-start.37 = (bf16[640,512]{1,0:T(8,128)(2,1)S(1)}, bf16[640,512]{1,0:T(8,128)(2,1)S(1)}, u32[]{:S(2)}, u32[]{:S(2)}) collective-permute-start(bf16[640,512]{1,0:T(8,128)(2,1)S(1)} %get-tuple-element.115), channel_id=1, source_target_pairs={{0,8},{8,0},{16,24},{24,16},{1,9},{9,1},{17,25},{25,17},{2,10},{10... | collective-permute-start | bytes 1966088 | tf_op jit(solution)/shard_map/ppermute | solution.py:22
  759.9 69.1 %collective-permute-start.29 = (bf16[2,2,128,2560]{3,2,0,1:T(8,128)(2,1)}, bf16[2,2,128,2560]{3,2,0,1:T(8,128)(2,1)}, u32[]{:S(2)}, u32[]{:S(2)}) collective-permute-start(bf16[2,2,128,2560]{3,2,0,1:T(8,128)(2,1)} %convolution_convert_fusion), channel_id=1, source_target_pairs={{0,1},{1,0},{2,3},{3,2},{4,5},{5,4},{6,7},{7,6},{8,9},{9,8},{10,11... | collective-permute-start | bytes 7864328 | tf_op jit(solution)/shard_map/ppermute | solution.py:22
  761.4 38.8 %collective-permute-start.46 = (bf16[640,320]{0,1:T(8,128)(2,1)}, bf16[640,320]{0,1:T(8,128)(2,1)S(1)}, u32[]{:S(2)}, u32[]{:S(2)}) collective-permute-start(bf16[640,320]{0,1:T(8,128)(2,1)} %get-tuple-element.134), channel_id=1, source_target_pairs={{0,8},{8,0},{16,24},{24,16},{1,9},{9,1},{17,25},{25,17},{2,10},{10... | collective-permute-start | bytes 1228808 | tf_op jit(solution)/shard_map/ppermute | solution.py:22
  763.2 50.3 %collective-permute-start.36 = (bf16[640,512]{1,0:T(8,128)(2,1)}, bf16[640,512]{1,0:T(8,128)(2,1)S(1)}, u32[]{:S(2)}, u32[]{:S(2)}) collective-permute-start(bf16[640,512]{1,0:T(8,128)(2,1)} %get-tuple-element.114), channel_id=1, source_target_pairs={{0,8},{8,0},{16,24},{24,16},{1,9},{9,1},{17,25},{25,17},{2,10},{10... | collective-permute-start | bytes 1966088 | tf_op jit(solution)/shard_map/ppermute | solution.py:22
  770.0 30.3 %collective-permute-start.48 = (bf16[640,320]{0,1:T(8,128)(2,1)S(1)}, bf16[640,320]{0,1:T(8,128)(2,1)S(1)}, u32[]{:S(2)}, u32[]{:S(2)}) collective-permute-start(bf16[640,320]{0,1:T(8,128)(2,1)S(1)} %add_convert_fusion.3), channel_id=1, source_target_pairs={{0,16},{8,24},{16,0},{24,8},{1,17},{9,25},{17,1},{25,9},{2,18},{10... | collective-permute-start | bytes 1228808 | tf_op jit(solution)/shard_map/ppermute | solution.py:22
  774.9 42.9 %collective-permute-start.38 = (bf16[640,512]{1,0:T(8,128)(2,1)}, bf16[640,512]{1,0:T(8,128)(2,1)}, u32[]{:S(2)}, u32[]{:S(2)}) collective-permute-start(bf16[640,512]{1,0:T(8,128)(2,1)} %add_convert_fusion.1), channel_id=1, source_target_pairs={{0,16},{8,24},{16,0},{24,8},{1,17},{9,25},{17,1},{25,9},{2,18},{10... | collective-permute-start | bytes 1966088 | tf_op jit(solution)/shard_map/ppermute | solution.py:22
  819.9 8.8 collective-permute-start.39
  822.3 53.2 %collective-permute-start.49 = (bf16[320,320]{1,0:T(8,128)(2,1)}, bf16[320,320]{1,0:T(8,128)(2,1)}, u32[]{:S(2)}, u32[]{:S(2)}) collective-permute-start(bf16[320,320]{1,0:T(8,128)(2,1)} %fusion.118), channel_id=1, source_target_pairs={{0,4},{4,0},{1,5},{5,1},{2,6},{6,2},{3,7},{7,3},{8,12},{12,8},{9,1... | collective-permute-start | bytes 614408 | tf_op jit(solution)/shard_map/ppermute | solution.py:22
  835.2 13.7 %collective-permute-start.30 = (bf16[2,128,1280]{2,1,0:T(8,128)(2,1)S(1)}, bf16[2,128,1280]{2,1,0:T(8,128)(2,1)S(1)}, u32[]{:S(2)}, u32[]{:S(2)}) collective-permute-start(bf16[2,128,1280]{2,1,0:T(8,128)(2,1)S(1)} %slice_bitcast_fusion.19), channel_id=1, source_target_pairs={{0,2},{1,3},{2,0},{3,1},{4,6},{5,7},{6,4},{7,5},{8,10},{9,11},{10,... | collective-permute-start | bytes 1966088 | tf_op jit(solution)/shard_map/ppermute | solution.py:22
  837.0 14.1 %collective-permute-start.32 = (bf16[2,128,1280]{2,1,0:T(8,128)(2,1)S(1)}, bf16[2,128,1280]{2,1,0:T(8,128)(2,1)S(1)}, u32[]{:S(2)}, u32[]{:S(2)}) collective-permute-start(bf16[2,128,1280]{2,1,0:T(8,128)(2,1)S(1)} %slice_bitcast_fusion.17), channel_id=1, source_target_pairs={{0,4},{4,0},{1,5},{5,1},{2,6},{6,2},{3,7},{7,3},{8,12},{12,8},{9,1... | collective-permute-start | bytes 1966088 | tf_op jit(solution)/shard_map/ppermute | solution.py:22
  851.5 7.1 collective-permute-start.31
  851.9 10.7 %collective-permute-start.33 = (bf16[128,1280]{1,0:T(8,128)(2,1)S(1)}, bf16[128,1280]{1,0:T(8,128)(2,1)S(1)}, u32[]{:S(2)}, u32[]{:S(2)}) collective-permute-start(bf16[128,1280]{1,0:T(8,128)(2,1)S(1)} %fusion.117), channel_id=1, source_target_pairs={{0,2},{1,3},{2,0},{3,1},{4,6},{5,7},{6,4},{7,5},{8,10},{9,11},{10,... | collective-permute-start | bytes 983048 | tf_op jit(solution)/shard_map/ppermute | solution.py:22
  863.6 10.7 %collective-permute-start.34 = (bf16[128,2560]{1,0:T(8,128)(2,1)S(1)}, bf16[128,2560]{1,0:T(8,128)(2,1)S(1)}, u32[]{:S(2)}, u32[]{:S(2)}) collective-permute-start(bf16[128,2560]{1,0:T(8,128)(2,1)S(1)} %fusion.50), channel_id=1, source_target_pairs={{0,2},{1,3},{2,0},{3,1},{4,6},{5,7},{6,4},{7,5},{8,10},{9,11},{10,... | collective-permute-start | bytes 1966088 | tf_op jit(solution)/shard_map/ppermute | solution.py:22
  866.4 10.1 %collective-permute-start.44 = (f32[2,320]{1,0:T(2,128)S(1)}, f32[2,320]{1,0:T(2,128)S(1)}, u32[]{:S(2)}, u32[]{:S(2)}) collective-permute-start(f32[2,320]{1,0:T(2,128)S(1)} %pad_maximum_fusion.13), channel_id=1, source_target_pairs={{0,1},{1,0},{2,3},{3,2},{4,5},{5,4},{6,7},{7,6},{8,9},{9,8},{10,11... | collective-permute-start | bytes 7688 | tf_op jit(solution)/shard_map/ppermute | solution.py:22
  875.6 7.3 collective-permute-start.35
  876.6 5.4 collective-permute-start.45
  (62 other events, 331.9 us)

commit v3 on v2

--- a/solution.py
+++ b/solution.py
@@ -59,106 +59,50 @@
     stats[rows, :] = jnp.concatenate(maxes + totals, axis=1)
 
 
-def attend_back_kernel(
-    scale, block, rot, d_attn, stats, cos, sin, seg_col, seg_row, sel, d_qkv, dk_sum, dv_sum
+def turn_back(u, cos, sin, rows):
+    return (u * cos[rows, :] - pltpu.roll(u, 64, 1) * sin[rows, :]).astype(BF16)
+
+
+def attend_back_rows(
+    scale, block, i, rot, d_attn, stats, cos, sin, seg_col, seg_row, sel, d_qkv, dk_sum, dv_sum
 ):
-    full_len = rot.shape[0]
     n_q = rot.shape[1] // LANES - 2
-    dk_sum[...] = jnp.zeros_like(dk_sum)
-    dv_sum[...] = jnp.zeros_like(dv_sum)
-
-    def back(u, at):
-        return (u * cos[at, :] - pltpu.roll(u, 64, 1) * sin[at, :]).astype(BF16)
-
-    for i in range(full_len // block):
-        rows = slice(i * block, (i + 1) * block)
-        keys = (i + 1) * block
-        q_pos = i * block + lax.broadcasted_iota(jnp.int32, (block, keys), 0)
-        k_pos = lax.broadcasted_iota(jnp.int32, (block, keys), 1)
-        allowed = (seg_col[rows, :] == seg_row[:, :keys]) & (k_pos <= q_pos)
-        k = rot[:keys, n_q * LANES : (n_q + 1) * LANES]
-        v = rot[:keys, (n_q + 1) * LANES :]
-        d_out = dot(d_attn[rows, :], sel[...], ((1,), (1,))).astype(BF16)
-        stat = stats[rows, :]
-        for h in range(n_q):
-            q = rot[rows, h * LANES : (h + 1) * LANES]
-            d_h = d_out[:, h * LANES : (h + 1) * LANES]
-            s = dot(q, k, ((1,), (1,))) * scale
-            s = jnp.where(allowed, s, MASK_FILL)
-            p = jnp.exp(s - stat[:, h : h + 1]) * (1.0 / stat[:, n_q + h : n_q + h + 1])
-            dv_sum[:keys, :] += dot(p.astype(BF16), d_h, ((0,), (0,)))
-            d_p = dot(d_h, v, ((1,), (1,)))
-            d_s = (p * (d_p - jnp.sum(p * d_p, axis=1, keepdims=True))).astype(BF16)
-            d_q = (dot(d_s, k) * scale).astype(BF16).astype(F32)
-            d_qkv[rows, h * LANES : (h + 1) * LANES] = back(d_q, rows)
-            dk_sum[:keys, :] += dot(d_s, q, ((0,), (0,)))
+    rows = slice(i * block, (i + 1) * block)
+    keys = (i + 1) * block
+    q_pos = i * block + lax.broadcasted_iota(jnp.int32, (block, keys), 0)
+    k_pos = lax.broadcasted_iota(jnp.int32, (block, keys), 1)
+    allowed = (seg_col[rows, :] == seg_row[:, :keys]) & (k_pos <= q_pos)
+    k = rot[:keys, n_q * LANES : (n_q + 1) * LANES]
+    v = rot[:keys, (n_q + 1) * LANES :]
+    d_out = dot(d_attn[rows, :], sel[...], ((1,), (1,))).astype(BF16)
+    stat = stats[rows, :]
+    for h in range(n_q):
+        q = rot[rows, h * LANES : (h + 1) * LANES]
+        d_h = d_out[:, h * LANES : (h + 1) * LANES]
+        s = dot(q, k, ((1,), (1,))) * scale
+        s = jnp.where(allowed, s, MASK_FILL)
+        p = jnp.exp(s - stat[:, h : h + 1]) * (1.0 / stat[:, n_q + h : n_q + h + 1])
+        dv_sum[:keys, :] += dot(p.astype(BF16), d_h, ((0,), (0,)))
+        d_p = dot(d_h, v, ((1,), (1,)))
+        d_s = (p * (d_p - jnp.sum(p * d_p, axis=1, keepdims=True))).astype(BF16)
+        d_q = (dot(d_s, k) * scale).astype(BF16).astype(F32)
+        d_qkv[rows, h * LANES : (h + 1) * LANES] = turn_back(d_q, cos, sin, rows)
+        dk_sum[:keys, :] += dot(d_s, q, ((0,), (0,)))
+
+
+def attend_back_keys(scale, n_q, cos, sin, d_qkv, dk_sum, dv_sum):
     d_k = (dk_sum[...] * scale).astype(BF16).astype(F32)
-    d_qkv[:, n_q * LANES : (n_q + 1) * LANES] = back(d_k, slice(None))
+    d_qkv[:, n_q * LANES : (n_q + 1) * LANES] = turn_back(d_k, cos, sin, slice(None))
     d_qkv[:, (n_q + 1) * LANES :] = dv_sum[...].astype(BF16)
 
 
 VMEM_LIMIT = 56 * 1024 * 1024
-
-
-def attend_back(rot, d_attn, stats, cos, sin, seg_col, seg_row, sel, scale):
-    full_len, width = rot.shape
-    n_q = width // LANES - 2
-    return pl.pallas_call(
-        lambda *refs: attend_back_kernel(scale, min(256, full_len), *refs),
-        out_shape=jax.ShapeDtypeStruct((full_len, width), BF16),
-        scratch_shapes=[pltpu.VMEM((full_len, LANES), F32), pltpu.VMEM((full_len, LANES), F32)],
-        compiler_params=pltpu.CompilerParams(vmem_limit_bytes=VMEM_LIMIT),
-        cost_estimate=pl.CostEstimate(
-            flops=5 * n_q * full_len * full_len * LANES,
-            bytes_accessed=full_len * width * 6,
-            transcendentals=n_q * full_len * full_len // 2,
-        ),
-        name="attend_back",
-    )(rot, d_attn, stats, cos, sin, seg_col, seg_row, sel)
-
-
-def gather_layer(own):
-    half = own.shape[-1] // 2
-    a, b = own[:, :half], own[:, half:]
-    a1 = jnp.stack([a, pp(a, "tp", 2)])
-    b1 = jnp.stack([b, pp(b, "ctx", 1)])
-    a2 = jnp.stack([a1, pp(a1, "ctx", 1)])
-    b2 = jnp.stack([b1, pp(b1, "tp", 2)], axis=1)
-    mine = jnp.concatenate([a2, b2], axis=-1)
-    return jnp.stack([mine, pp(mine, "tp", 1)], axis=2)
-
-
-def scatter_layer(lhs, rhs, dims=((1,), (0,))):
-    rows, depth = lhs.shape[-2:]
-
-    def product(part):
-        return dot(part.reshape(4 * rows, depth), rhs, dims).reshape(2, 2, rows, -1)
-
-    sent = pp(product(lhs[:, :, 1]).astype(BF16), "tp", 1)
-    kept = product(lhs[:, :, 0]) + sent.astype(F32)
-    half = kept.shape[-1] // 2
-    a, b = kept[..., :half], kept[..., half:]
-    a1 = a[:, 0] + pp(a[:, 1].astype(BF16), "tp", 2).astype(F32)
-    b1 = b[0] + pp(b[1].astype(BF16), "ctx", 1).astype(F32)
-    a2 = a1[0] + pp(a1[1].astype(BF16), "ctx", 1).astype(F32)
-    b2 = b1[0] + pp(b1[1].astype(BF16), "tp", 2).astype(F32)
-    return jnp.concatenate([a2, b2], axis=-1)
-
-
-def gather_tp(own):
-    index = lax.axis_index("tp")
-    pair = in_order(index // 2, own, pp(own, "tp", 2))
-    return in_order(index % 2, pair, pp(pair, "tp", 1), axis=1).reshape(-1, own.shape[-1])
+BACK_LIMIT = 62 * 1024 * 1024
 
 
 def sum_tp(value):
     value = value + pp(value, "tp", 1)
     return value + pp(value, "tp", 2)
-
-
-def by_xor(value, parts, index):
-    blocks = value.reshape(parts, -1, value.shape[-1])
-    return jnp.stack([pick(blocks, index ^ r) for r in range(parts)])
 
 
 def below(top):
@@ -167,43 +111,6 @@
         top //= 2
         masks.append(top)
     return masks
-
-
-def gather_z(held, top):
-    held = dict(held)
-    for mask in below(top):
-        for rel in list(held):
-            held[rel ^ mask] = pp(held[rel], "fsdp", mask)
-    return held
-
-
-def place(held, index, axis):
-    shape = list(next(iter(held.values())).shape)
-    size = shape[axis]
-    shape[axis] = size * len(held)
-    out = jnp.zeros(shape, BF16)
-    for rel, block in held.items():
-        start = [0] * len(shape)
-        start[axis] = (index ^ rel) * size
-        out = lax.dynamic_update_slice(out, block, start)
-    return out
-
-
-def scatter_z(blocks, top):
-    blocks = dict(blocks)
-    for mask in reversed(below(top)):
-        for rel in [r for r in blocks if r & mask]:
-            blocks[rel ^ mask] = blocks[rel ^ mask] + pp(
-                blocks.pop(rel).astype(BF16), "fsdp", mask
-            ).astype(F32)
-    return blocks
-
-
-def split_z(value, n, index, axis):
-    size = value.shape[axis] // n
-    return {
-        rel: lax.dynamic_slice_in_dim(value, (index ^ rel) * size, size, axis) for rel in range(n)
-    }
 
 
 def flip(index, mask):
@@ -223,9 +130,11 @@
     def __init__(self, send_sems, recv_sems):
         self.sems = (send_sems, recv_sems)
         self.copies = []
-
-    def send(self, src, dst, peer):
-        k = len(self.copies)
+        self.count = 0
+
+    def send(self, src, dst, peer, kept=False):
+        k = self.count
+        self.count += 1
         copy = pltpu.make_async_remote_copy(
             src_ref=src,
             dst_ref=dst,
@@ -235,12 +144,15 @@
             device_id_type=pl.DeviceIdType.MESH,
         )
         copy.start()
-        self.copies.append(copy)
+        if not kept:
+            self.copies.append(copy)
         return copy
 
-    def finish(self):
+    def finish(self, *sums):
         for copy in self.copies:
             copy.wait_send()
+        for layer in sums:
+            layer.drain()
 
 
 def greet(peers):
@@ -259,6 +171,7 @@
         self.x = {"tp": flip(self.t, 2)}
         self.yy = {"ctx": 1 - self.y}
         self.masks = below(n_z)
+        self.zb = self.z // (n_z // 2)
 
     def zz(self, mask):
         return {"fsdp": flip(self.z, mask)}
@@ -307,23 +220,27 @@
 
 
 class LayerGather:
-    def __init__(self, links, at, out, rows, halves):
+    def __init__(self, links, at, out, rows):
         self.links, self.at, self.out, self.rows = links, at, out, rows
-        self.halves = halves
         self.cores = []
+        self.sent = []
 
     def half(self, index, part):
         return half_rows(self.out.at[index], part, self.rows)
 
+    def send(self, src, dst, peer):
+        self.sent.append(self.links.send(src, dst, peer, kept=True))
+        return self.sent[-1]
+
     def pass_on(self, index, part, peer):
         block = self.half(index, part)
-        return self.links.send(block, block, peer)
+        return self.send(block, block, peer)
 
     def own(self, part, src=None):
         at, me = self.at, self.at.me
         a = self.half(me, part)
         src = a if src is None else src
-        send = lambda peer: self.links.send(src, a, peer)
+        send = lambda peer: self.send(src, a, peer)
         if part == 0:
             self.xa, self.ya = send(at.x), send(at.yy)
         else:
@@ -358,67 +275,120 @@
         for copy in self.cores:
             copy.wait_recv()
 
+    def drain(self):
+        for copy in self.sent:
+            copy.wait_send()
+
 
 class LayerSum:
-    def __init__(self, links, at, rows, to_core, from_core, part, landed):
+    def __init__(self, links, at, rows, bufs, product, after=None):
         self.links, self.at, self.rows = links, at, rows
-        self.bufs = (to_core, from_core, part, landed)
-
-    def begin(self, product):
-        to_core, from_core, _, _ = self.bufs
+        self.to_core, self.held, self.landed, self.total, self.free = bufs
+        self.product = product
+        self.after = after
+
+    def peers(self):
+        return (self.at.core, self.at.x, self.at.yy)
+
+    def tiles(self, some):
+        width = self.total.shape[1]
+        tile = 512 if width % 512 == 0 else width
+
+        def body(c, carry):
+            some(pl.ds(pl.multiple_of(c * tile, tile), tile))
+            return carry
+
+        lax.fori_loop(0, width // tile, body, 0)
+
+    def drain(self):
+        for copy in self.sent:
+            copy.wait_send()
+        self.sent = []
+
+    def release(self):
+        self.drain()
+        for i, peer in enumerate(self.peers()):
+            pl.semaphore_signal(
+                self.free.at[i], inc=1, device_id=peer, device_id_type=pl.DeviceIdType.MESH
+            )
+
+    def begin(self):
         self.core = {}
-        for k in (3, 1, 2, 0):
-            to_core[k] = product(2 * k + 1).astype(BF16)
-            self.core[k] = self.links.send(to_core.at[k], from_core.at[k], self.at.core)
-
-    def middle(self, product):
-        _, from_core, part, landed = self.bufs
+        if self.after is not None:
+            self.after.drain()
+            for i in range(3):
+                pl.semaphore_wait(self.free.at[i], 1)
+        sent = []
+        for i, k in enumerate((3, 1, 2, 0)):
+            if i >= 2:
+                sent[i - 2].wait_send()
+
+
+            def some(cols, i=i, k=k):
+                self.to_core[i % 2, :, cols] = self.product(2 * k + 1, cols).astype(BF16)
+
+            self.tiles(some)
+            self.core[k] = self.links.send(
+                self.to_core.at[i % 2], self.held.at[k], self.at.core, kept=True
+            )
+            sent.append(self.core[k])
+        self.sent = sent[2:]
+
+    def middle(self):
         at, rows, h = self.at, self.rows, self.rows // 2
+        held, landed = self.held, self.landed
         a, b = slice(0, h), slice(h, rows)
 
         def level(k):
-            value = product(2 * k)
             self.core[k].wait_recv()
-            return value + from_core[k].astype(F32)
-
-        send = lambda k, i, peer: self.links.send(
-            part.at[k, pl.ds((i % 2) * h, h)], landed.at[i], peer
-        )
-        part[3] = level(3).astype(BF16)
+
+            def some(cols):
+                value = self.product(2 * k, cols) + held[k, :, cols].astype(F32)
+                if k == 0:
+                    self.total[:, cols] = value
+                else:
+                    held[k, :, cols] = value.astype(BF16)
+
+            self.tiles(some)
+
+        def send(k, i, peer):
+            copy = self.links.send(held.at[k, pl.ds((i % 2) * h, h)], landed.at[i], peer, kept=True)
+            self.sent.append(copy)
+            return copy
+
+        level(3)
         x1 = send(3, 0, at.x)
         y1 = send(3, 1, at.yy)
-        one = level(1)
-        part[1, a] = one[a].astype(BF16)
+        level(1)
         x2 = send(1, 2, at.x)
-        two = level(2)
-        part[2, b] = two[b].astype(BF16)
+        level(2)
         y2 = send(2, 3, at.yy)
-        zero = level(0)
+        level(0)
         x1.wait_recv()
-        part[2, a] = (two[a] + landed[0].astype(F32)).astype(BF16)
+        held[2, a] = (held[2, a].astype(F32) + landed[0].astype(F32)).astype(BF16)
         y3 = send(2, 4, at.yy)
         y1.wait_recv()
-        part[1, b] = (one[b] + landed[1].astype(F32)).astype(BF16)
+        held[1, b] = (held[1, b].astype(F32) + landed[1].astype(F32)).astype(BF16)
         x3 = send(1, 5, at.x)
-        self.zero, self.tail = zero, (x2, y3, y2, x3)
+        self.tail = (x2, y3, y2, x3)
 
     def end(self):
-        _, _, _, landed = self.bufs
         h = self.rows // 2
+        landed, total = self.landed, self.total
         for copy in self.tail:
             copy.wait_recv()
-        zero = self.zero
-        top = zero[:h] + landed[2].astype(F32) + landed[4].astype(F32)
-        low = zero[h:] + landed[3].astype(F32) + landed[5].astype(F32)
+        top = total[:h, :] + landed[2].astype(F32) + landed[4].astype(F32)
+        low = total[h:, :] + landed[3].astype(F32) + landed[5].astype(F32)
         return top, low
 
 
 def sum_scratch(rows, width):
     return [
-        pltpu.VMEM((4, rows, width), BF16),
-        pltpu.VMEM((4, rows, width), BF16),
+        pltpu.VMEM((2, rows, width), BF16),
         pltpu.VMEM((4, rows, width), BF16),
         pltpu.VMEM((6, rows // 2, width), BF16),
+        pltpu.VMEM((rows, width), F32),
+        pltpu.SemaphoreType.REGULAR((3,)),
     ]
 
 
@@ -426,7 +396,7 @@
     n_z, n_tp, scale, q_block,
     x_here, dy_here, in_send, o_send, w3_send, cos, sin, seg_col, seg_row, spread, sel,
     w_heads, w_o, w3, gains, norm_attn, dy_all, norm_all, attn, rot, stats, mid,
-    w_in, x_all, qkv, to_core, from_core, part, landed, in_cross, o_cross, w3_cross,
+    w_in, x_all, qkv, to_core, held, landed, total, free, in_cross, o_cross, w3_cross,
     heads_v, norm_v, own_v, root_v, o_v, send_sems, recv_sems, sems,
 ):
     at = Place(n_z, n_tp)
@@ -571,7 +541,7 @@
         return carry
 
     lax.fori_loop(0, full_len // step, turn, 0)
-    dy_far = LayerGather(links, at, dy_all.at[1], rows, True)
+    dy_far = LayerGather(links, at, dy_all.at[1], rows)
     for i in range(full_len // q_block):
         attend_rows(scale, q_block, i, rot, seg_col, seg_row, sel, attn, stats)
         if i == 0:
@@ -584,21 +554,20 @@
                 f_o.take(rel, p)
     for copy in own_o:
         copy.wait()
-    load_o = move(w_o, o_v)
+    load_o = move(w_o.reshape(width, o_v.shape[1]), o_v)
     load_o.wait()
 
-    layer = LayerSum(links, at, rows, to_core, from_core, part, landed)
-
-    def product(r):
+    def product(r, cols):
         lhs = attn[pl.ds(pl.multiple_of(flip_all(me, r) * rows, rows), rows), :]
-        return dot(lhs, o_v[...].reshape(width, o_v.shape[3]), ((1,), (1,)))
-
-    layer.begin(product)
-    layer.middle(product)
+        return dot(lhs, o_v[cols, :], ((1,), (1,)))
+
+    layer = LayerSum(links, at, rows, (to_core, held, landed, total, free), product)
+    layer.begin()
+    layer.middle()
     for p in (0, 1):
         f_3.take(top, p)
-    norm_own = LayerGather(links, at, norm_all.at[0], rows, True)
-    norm_far = LayerGather(links, at, norm_all.at[1], rows, True)
+    norm_own = LayerGather(links, at, norm_all.at[0], rows)
+    norm_far = LayerGather(links, at, norm_all.at[1], rows)
     far = []
     h = rows // 2
     load_x = move(x_mine, own_v)
@@ -631,11 +600,12 @@
                 f_3.take(rel, p)
     for gather in (norm_own, dy_far, norm_far):
         gather.last()
+        gather.drain()
     for copy in dy_c:
         copy.wait_recv()
     for copy in [dy_own, heads_out, norm_out, keep] + own_3:
         copy.wait()
-    links.finish()
+    links.finish(layer)
 
 
 def front(n_z, n_tp, scale, x_here, dy_here, in_send, o_send, w3_send, cos, sin, seg_col, seg_row, spread, sel):
@@ -679,7 +649,7 @@
             pltpu.VMEM((full_len, width), BF16),
             pltpu.VMEM((rows, width), BF16),
             pltpu.VMEM((full_len, 1), F32),
-            pltpu.VMEM((n_z, 2, depth, q_cols), BF16),
+            pltpu.VMEM((width, q_cols), BF16),
             pltpu.SemaphoreType.DMA((n_sems,)),
             pltpu.SemaphoreType.DMA((n_sems,)),
             pltpu.SemaphoreType.DMA((16,)),
@@ -689,6 +659,393 @@
         ),
         name="front",
     )(x_here, dy_here, in_send, o_send, w3_send, cos, sin, seg_col, seg_row, spread, sel)
+
+
+class TpGather:
+    def __init__(self, links, at, out):
+        self.links, self.at, self.out = links, at, out
+
+    def own(self, src):
+        at = self.at
+        dst = self.out.at[at.t]
+        self.x = self.links.send(src, dst, at.x)
+        self.cores = [self.links.send(src, dst, at.core)]
+
+    def second(self):
+        at = self.at
+        self.x.wait_recv()
+        block = self.out.at[flip(at.t, 2)]
+        self.cores.append(self.links.send(block, block, at.core))
+
+    def last(self):
+        for copy in self.cores:
+            copy.wait_recv()
+
+
+class GradFlow:
+    def __init__(self, links, at, src, land, swap, out, passing, fetch=None):
+        self.links, self.at, self.src, self.land = links, at, src, land
+        self.swap, self.out, self.passing, self.fetch = swap, out, passing, fetch
+        self.adds = [m for m in reversed(at.masks) if not (swap and m == at.n_z // 2)]
+        self.slot = {}
+        n = 0
+        for m in self.adds:
+            for rel in range(0, at.n_z, 2 * m):
+                self.slot[m, rel] = n
+                n += 1
+        self.got = {}
+        self.at_mask = {}
+
+    def row(self, part):
+        return self.at.y if part == 0 else 1 - self.at.y
+
+    def own(self, rel, part):
+        return self.src.at[flip_all(self.at.z, rel), self.row(part)]
+
+    def held(self, rel, part):
+        m = self.at_mask.get((rel, part))
+        if m is None:
+            return self.own(rel, part), True
+        return self.land.at[self.slot[m, rel], part], False
+
+    def send(self, m, rel, part):
+        block, _ = self.held(rel, part)
+        self.got[m, rel ^ m, part] = self.links.send(
+            block, self.land.at[self.slot[m, rel ^ m], part], self.at.zz(m)
+        )
+
+    def first(self, parts=(1, 0)):
+        m = self.adds[0]
+        rels = [r for r in range(self.at.n_z) if r & m]
+        for rel in sorted(rels, reverse=True):
+            for part in parts:
+                self.send(m, rel, part)
+
+    def add(self, m, rel, part):
+        block, is_first = self.held(rel, part)
+        if is_first and self.fetch is not None:
+            block = self.fetch(block)
+        self.got[m, rel, part].wait_recv()
+        slot = self.land.at[self.slot[m, rel], part]
+        slot[...] = (block[...].astype(F32) + slot[...].astype(F32)).astype(BF16)
+        self.at_mask[rel, part] = m
+
+    def spread(self):
+        at = self.at
+        for i, m in enumerate(self.adds):
+            left = range(0, at.n_z, 2 * m)
+            nxt = self.adds[i + 1] if i + 1 < len(self.adds) else (2 * m if self.swap else None)
+            for rel in sorted(left, key=lambda r: -(r & (nxt or 0))):
+                for part in (1, 0):
+                    self.add(m, rel, part)
+                    if nxt is not None and rel & nxt:
+                        if nxt in self.adds:
+                            self.send(nxt, rel, part)
+                        else:
+                            self.exchange(nxt, rel, part)
+
+    def column(self, mine):
+        return self.at.zb if mine else 1 - self.at.zb
+
+    def exchange(self, m, rel, part):
+        block, _ = self.held(rel, part)
+        if part == 0:
+            dst = self.out.at[self.at.zb, self.at.y]
+        else:
+            dst = self.passing
+        self.got[m, 0, part] = self.links.send(block, dst, self.at.zz(m))
+
+    def cross(self):
+        at = self.at
+        block, _ = self.held(0, 1)
+        dst = self.out.at[at.zb, at.y] if self.swap else self.out.at[at.y]
+        self.ends = [self.links.send(block, dst, at.yy)]
+
+    def cross_far(self):
+        at = self.at
+        self.got[at.n_z // 2, 0, 1].wait_recv()
+        self.ends.append(self.links.send(self.passing, self.out.at[1 - at.zb, at.y], at.yy))
+        self.ends.append(self.got[at.n_z // 2, 0, 0])
+
+    def mine(self):
+        at = self.at
+        dst = self.out.at[at.zb, at.y] if self.swap else self.out.at[at.y]
+        return self.held(0, 0)[0], dst
+
+    def last(self):
+        for copy in self.ends:
+            copy.wait_recv()
+
+
+def back_kernel(
+    n_z, n_tp, scale, q_block, units, wide,
+    x_here, dy_here, w3, d_gu, hidden, gu_src, dn_src, w_o, w_heads, norm_attn,
+    mid, gains, rot, attn, stats, cos, sin, seg_col, seg_row, sel, spread,
+    output, input_grad, gu_out, dn_out, o_out, in_out,
+    w3_v, gu_v, hid_v,
+    to_core_a, held_a, landed_a, total_a, free_a, to_core_b, held_b, landed_b, total_b, free_b,
+    far_v, far_in, d_mid, row_v, d_proj, d_attn, d_qkv, dk_sum, dv_sum, o_v,
+    gu_land, gu_pass, dn_land, dn_pass, fetch_gu, fetch_dn, o_land, in_land,
+    send_sems, recv_sems, sems,
+):
+    at = Place(n_z, n_tp)
+    links = Links(send_sems, recv_sems)
+    z, y, t, me = at.z, at.y, at.t, at.me
+    top = n_z // 2
+    n_b, rows, width = 2 * n_tp, mid.shape[0], mid.shape[1]
+    depth = gu_src.shape[2]
+    full_len = rot.shape[0]
+    h = rows // 2
+    n_q = rot.shape[1] // LANES - 2
+    local = []
+
+    def move(src, dst):
+        copy = pltpu.make_async_copy(src, dst, sems.at[len(local)])
+        copy.start()
+        local.append(copy)
+        return copy
+
+    load_w3 = move(w3, w3_v)
+    load_gu, load_hid = move(d_gu, gu_v), move(hidden, hid_v)
+    load_o = move(w_o, o_v)
+    load_x = move(x_here.at[pl.ds(pl.multiple_of(t * rows, rows), rows)], row_v.at[0])
+    load_dy = move(dy_here.at[pl.ds(pl.multiple_of(t * rows, rows), rows)], row_v.at[1])
+    greet(at.peers())
+
+    def fetch_with(buf):
+        def fetch(block):
+            move(block, buf).wait()
+            return buf
+
+        return fetch
+
+    f_gu = GradFlow(links, at, gu_src, gu_land, True, gu_out, gu_pass, fetch_with(fetch_gu))
+    f_dn = GradFlow(links, at, dn_src, dn_land, True, dn_out, dn_pass, fetch_with(fetch_dn))
+    f_gu.first()
+
+    def term(seq, lhs, lo, hi):
+        def product(r, cols):
+            return dot(lhs[seq, flip_all(me, r)], w3_v[cols, lo:hi], ((1,), (1,)))
+
+        return product
+
+    bufs_a = (to_core_a, held_a, landed_a, total_a, free_a)
+    bufs_b = (to_core_b, held_b, landed_b, total_b, free_b)
+    load_w3.wait()
+    load_gu.wait()
+    far = LayerSum(links, at, rows, bufs_a, term(1, gu_v, 0, 2 * units))
+    own = LayerSum(links, at, rows, bufs_b, term(0, gu_v, 0, 2 * units))
+    far.begin()
+    far.middle()
+    own.begin()
+
+    def send_far(layer, i):
+        sent = []
+        for p, value in enumerate(layer.end()):
+            far_v[i, pl.ds(p * h, h), :] = value.astype(BF16)
+            sent.append(
+                links.send(
+                    half_rows(far_v.at[i], p, rows), half_rows(far_in.at[i], p, rows), at.zz(top),
+                    kept=True,
+                )
+            )
+        layer.release()
+        return sent
+
+    sent_far = send_far(far, 0)
+    own.middle()
+    heads_v = w3_v.at[:, : w_heads.shape[1]]
+    load_heads = move(w_heads, heads_v)
+    f_dn.first()
+    load_hid.wait()
+    ffn_far = LayerSum(links, at, rows, bufs_a, term(1, hid_v, wide, wide + units), far)
+    ffn_own = LayerSum(links, at, rows, bufs_b, term(0, hid_v, wide, wide + units), own)
+    ffn_far.begin()
+
+    def norm_back(inputs, gain, d_normed):
+        root = lax.rsqrt(jnp.mean(inputs * inputs, axis=1, keepdims=True) + NORM_EPS)
+        scaled = d_normed * gain
+        return root * scaled - inputs * (root * root * root) * jnp.mean(
+            scaled * inputs, axis=1, keepdims=True
+        )
+
+    load_x.wait()
+    load_dy.wait()
+    gather = LayerGather(links, at, d_proj, rows)
+    for p, value in enumerate(own.end()):
+        r = slice(p * h, (p + 1) * h)
+        sent_far[p].wait_recv()
+        value = value + far_in[0, r, :].astype(F32)
+        value = row_v[1, r, :].astype(F32) + norm_back(mid[r, :], gains[1:2, :], value)
+        d_mid[r, :] = value
+        d_proj[me, r, :] = value.astype(BF16)
+        gather.own(p)
+    own.release()
+    gather.far_first()
+    ffn_own.begin()
+    f_gu.spread()
+    gather.far_second()
+    ffn_far.middle()
+    f_dn.spread()
+    gather.last()
+
+    load_o.wait()
+    w_o_all = o_v[...].reshape(width, o_v.shape[3])
+
+    def d_attn_rows(b, carry):
+        r = pl.ds(pl.multiple_of(b * rows, rows), rows)
+        d_attn[r, :] = dot(d_proj[b], w_o_all).astype(BF16)
+        return carry
+
+    lax.fori_loop(0, n_b, d_attn_rows, 0)
+
+    group = 1
+    while 2 * depth * group % LANES:
+        group *= 2
+    span = 2 * depth * group
+
+    def groups():
+        rels = sorted(range(0, n_z, group), key=lambda r: (-(r & 1), -r))
+        return [flip_all(z, r) // group for r in rels]
+
+    def span_of(owner):
+        return pl.ds(pl.multiple_of(owner * span, span), span)
+
+    o_src = o_v
+    f_o = GradFlow(links, at, o_src, o_land, False, o_out, None)
+    for owner in groups():
+        lhs = jnp.concatenate([d_proj[b, :, span_of(owner)] for b in range(n_b)], axis=0)
+        value = dot(lhs, attn[...], ((0,), (0,))).astype(BF16)
+        o_src[pl.ds(owner * group, group)] = value.reshape(group, 2, depth, value.shape[1])
+    f_o.first()
+    gather.drain()
+    load_norm = move(norm_attn, d_proj)
+    ffn_own.middle()
+    dk_sum[...] = jnp.zeros_like(dk_sum)
+    dv_sum[...] = jnp.zeros_like(dv_sum)
+    for i in range(full_len // q_block):
+        attend_back_rows(
+            scale, q_block, i, rot, d_attn, stats, cos, sin, seg_col, seg_row, sel, d_qkv, dk_sum, dv_sum
+        )
+        if i == 0:
+            f_gu.cross()
+            f_dn.cross()
+            sent_ffn = send_far(ffn_far, 1)
+        if i == 1:
+            f_o.spread()
+            f_o.cross()
+    attend_back_keys(scale, n_q, cos, sin, d_qkv, dk_sum, dv_sum)
+
+    load_heads.wait()
+
+    def d_term(r, cols):
+        value = d_qkv[pl.ds(pl.multiple_of(flip_all(me, r) * rows, rows), rows), :]
+        return dot(value, w3_v[cols, : w_heads.shape[1]], ((1,), (1,)))
+
+    d_in = LayerSum(links, at, rows, bufs_a, d_term, ffn_far)
+    d_in.begin()
+    d_in.middle()
+    in_cols = slice(w_heads.shape[1], w_heads.shape[1] + spread.shape[0])
+    in_src = w3_v.reshape(n_z, 2, depth, w3_v.shape[1]).at[:, :, :, in_cols]
+    f_in = GradFlow(links, at, in_src, in_land, False, in_out, None)
+    packed = dot(d_qkv[...], spread[...], ((1,), (1,))).astype(BF16)
+    load_norm.wait()
+    for owner in groups():
+        lhs = jnp.concatenate([d_proj[b, :, span_of(owner)] for b in range(n_b)], axis=0)
+        w3_v[span_of(owner), in_cols] = dot(lhs, packed, ((0,), (0,))).astype(BF16)
+    f_in.first()
+    out_g, in_g = TpGather(links, at, output), TpGather(links, at, input_grad)
+    stay = []
+    for p, value in enumerate(d_in.end()):
+        r = slice(p * h, (p + 1) * h)
+        value = d_mid[r, :] + norm_back(row_v[0, r, :].astype(F32), gains[0:1, :], value)
+        row_v[1, r, :] = value.astype(BF16)
+    in_g.own(row_v.at[1])
+    stay.append(move(row_v.at[1], input_grad.at[t]))
+    for copy in sent_far:
+        copy.wait_send()
+    for p, value in enumerate(ffn_own.end()):
+        r = slice(p * h, (p + 1) * h)
+        sent_ffn[p].wait_recv()
+        value = value + far_in[1, r, :].astype(F32)
+        far_v[0, r, :] = (mid[r, :] + value).astype(BF16)
+    out_g.own(far_v.at[0])
+    stay.append(move(far_v.at[0], output.at[t]))
+    f_in.spread()
+    f_in.cross()
+    f_gu.cross_far()
+    f_dn.cross_far()
+    for flow in (f_gu, f_dn, f_o, f_in):
+        stay.append(move(*flow.mine()))
+    in_g.second()
+    out_g.second()
+    for flow in (in_g, out_g, f_gu, f_dn, f_o, f_in):
+        flow.last()
+    for copy in stay:
+        copy.wait()
+    for copy in sent_ffn:
+        copy.wait_send()
+    links.finish(d_in, ffn_own)
+
+
+def back(n_z, n_tp, scale, units, wide, *args):
+    x_here, w_heads, spread, mid, sel = args[0], args[8], args[20], args[10], args[19]
+    d_gu, hidden, gu_src, dn_src, w3, w_o, rot = args[3], args[4], args[5], args[6], args[2], args[7], args[12]
+    half_len, width = x_here.shape
+    rows = mid.shape[0]
+    full_len = 2 * half_len
+    depth = gu_src.shape[2]
+    heads, compact = w_heads.shape[1], spread.shape[0]
+    q_cols = sel.shape[1]
+    any_, vmem = pl.BlockSpec(memory_space=pl.ANY), pl.BlockSpec(memory_space=pltpu.VMEM)
+    shape = jax.ShapeDtypeStruct
+    n_swap, n_add = max(1, n_z - 2), n_z - 1
+    n_sems = 120 + 8 * n_z
+    return pl.pallas_call(
+        lambda *refs: back_kernel(n_z, n_tp, scale, min(256, full_len), units, wide, *refs),
+        out_shape=(
+            shape((n_tp, rows, width), BF16),
+            shape((n_tp, rows, width), BF16),
+            shape((2, 2, depth, 2 * units), BF16),
+            shape((2, 2, depth, units), BF16),
+            shape((2, depth, q_cols), BF16),
+            shape((2, depth, compact), BF16),
+        ),
+        in_specs=[any_] * 10 + [vmem] * 11,
+        out_specs=(any_,) * 6,
+        scratch_shapes=[
+            pltpu.VMEM(w3.shape, BF16),
+            pltpu.VMEM(d_gu.shape, BF16),
+            pltpu.VMEM(hidden.shape, BF16),
+            *sum_scratch(rows, width),
+            *sum_scratch(rows, width),
+            pltpu.VMEM((2, rows, width), BF16),
+            pltpu.VMEM((2, rows, width), BF16),
+            pltpu.VMEM((rows, width), F32),
+            pltpu.VMEM((2, rows, width), BF16),
+            pltpu.VMEM((2 * n_tp, rows, width), BF16),
+            pltpu.VMEM((full_len, q_cols), BF16),
+            pltpu.VMEM((full_len, heads), BF16),
+            pltpu.VMEM((full_len, LANES), F32),
+            pltpu.VMEM((full_len, LANES), F32),
+            pltpu.VMEM(w_o.shape, BF16),
+            pltpu.VMEM((n_swap, 2, depth, 2 * units), BF16),
+            pltpu.VMEM((depth, 2 * units), BF16),
+            pltpu.VMEM((n_swap, 2, depth, units), BF16),
+            pltpu.VMEM((depth, units), BF16),
+            pltpu.VMEM((depth, 2 * units), BF16),
+            pltpu.VMEM((depth, units), BF16),
+            pltpu.VMEM((n_add, 2, depth, q_cols), BF16),
+            pltpu.VMEM((n_add, 2, depth, compact), BF16),
+            pltpu.SemaphoreType.DMA((n_sems,)),
+            pltpu.SemaphoreType.DMA((n_sems,)),
+            pltpu.SemaphoreType.DMA((24 + 6 * n_z,)),
+        ],
+        compiler_params=pltpu.CompilerParams(
+            collective_id=2, has_side_effects=True, vmem_limit_bytes=BACK_LIMIT
+        ),
+        name="back",
+    )(*args)
 
 
 def body(
@@ -773,14 +1130,8 @@
         n_z, n_tp, scale, x_here, cotangent.reshape(half_len, width), in_send, o_send, w3_send,
         cos, sin, seg_col, seg_row, spread, sel,
     )
-    gain_one, gain_two = gains[0:1], gains[1:2]
-    w_o = w_o.reshape(width, q_cols)
     w3 = w3.reshape(width, -1)
     w_gu, w_dn = w3[:, : 2 * units], w3[:, wide:]
-    x_mine = lax.dynamic_slice_in_dim(x_here, t * rows, rows, 0).astype(F32)
-    root_ffn = lax.rsqrt(jnp.mean(mid * mid, axis=1, keepdims=True) + NORM_EPS)
-    dy_mine = lax.dynamic_slice_in_dim(cotangent.reshape(half_len, width), t * rows, rows, 0)
-    attn_rel = by_xor(attn, 2 * n_tp, me)
 
     def mlp(norm, dy):
         norm = norm.reshape(full_len, width)
@@ -796,65 +1147,27 @@
 
     own_mlp, far_mlp = mlp(norm_all[0], dy_all[0]), mlp(norm_all[1], dy_all[1])
 
-    def shape8(v):
-        return by_xor(v, 2 * n_tp, me).reshape(2, 2, 2, rows, v.shape[-1])
-
-    def scatter_both(own, far, rhs, dims=((1,), (0,))):
-        sent = pp(scatter_layer(shape8(far), rhs, dims).astype(BF16), "fsdp", n_z // 2)
-        return scatter_layer(shape8(own), rhs, dims) + sent.astype(F32)
-
-    d_norm = scatter_both(own_mlp[1], far_mlp[1], w_gu, ((1,), (1,)))
-    ffn = scatter_both(own_mlp[0], far_mlp[0], w_dn, ((1,), (1,)))
-    output = gather_tp((mid + ffn).astype(BF16))
-
     gu_g = dot(own_mlp[2], own_mlp[1], ((0,), (0,))) + dot(far_mlp[2], far_mlp[1], ((0,), (0,)))
     dn_g = dot(own_mlp[3], own_mlp[0], ((0,), (0,))) + dot(far_mlp[3], far_mlp[0], ((0,), (0,)))
 
-    def norm_back(inputs, root, gain, d_normed):
-        scaled = d_normed * gain
-        return root * scaled - inputs * (root * root * root) * jnp.mean(
-            scaled * inputs, axis=1, keepdims=True
-        )
-
-    d_mid = dy_mine.astype(F32) + norm_back(mid, root_ffn, gain_two, d_norm)
-    d_proj = gather_layer(d_mid.astype(BF16)).reshape(full_len, width)
-    o_g = dot(d_proj, attn_rel.reshape(full_len, q_cols), ((0,), (0,)))
-    d_attn = dot(d_proj, w_o).astype(BF16)
-    d_attn = by_xor(d_attn, 2 * n_tp, me).reshape(full_len, q_cols)
-    d_qkv = attend_back(rot, d_attn, stats, cos, sin, seg_col, seg_row, sel, scale)
-    d_norm_attn = scatter_layer(shape8(d_qkv), w_heads, ((1,), (1,)))
-    root_mine = lax.rsqrt(jnp.mean(x_mine * x_mine, axis=1, keepdims=True) + NORM_EPS)
-    d_in = d_mid + norm_back(x_mine, root_mine, gain_one, d_norm_attn)
-    input_grad = gather_tp(d_in.astype(BF16))
-    d_packed = dot(d_qkv, spread, ((1,), (1,))).astype(BF16)
-    in_g = dot(norm_attn, d_packed, ((0,), (0,)))
-
-    def to_owner_y(blocks, rows_axis):
-        mine, theirs = pick(blocks, y), pick(blocks, 1 - y)
-        return in_order(y, mine, pp(theirs.astype(BF16), "ctx", 1).astype(F32))
-
-    def half_z(blocks):
-        top = n_z // 2
-        left = scatter_z(blocks, top)
-        return in_order(zb, left[0], pp(left[top].astype(BF16), "fsdp", top).astype(F32))
-
-    gu_two = half_z(split_z(gu_g, n_z, z, 0))
-    gu_four = to_owner_y(gu_two.reshape(2, 2, depth, 2 * units).transpose(1, 0, 2, 3), 0)
-    gu_four = gu_four.transpose(2, 1, 0, 3)
+    def blocks(own, far):
+        return jnp.stack([own, far]).reshape(2, 2 * n_tp, rows, own.shape[1])
+
+    output, input_grad, gu_four, dn_four, o_two, in_two = back(
+        n_z, n_tp, scale, units, wide,
+        x_here, cotangent.reshape(half_len, width), w3, blocks(own_mlp[1], far_mlp[1]),
+        blocks(own_mlp[0], far_mlp[0]),
+        gu_g.astype(BF16).reshape(n_z, 2, depth, 2 * units),
+        dn_g.astype(BF16).reshape(n_z, 2, depth, units),
+        w_o, w_heads, norm_attn.reshape(2 * n_tp, rows, width),
+        mid, gains, rot, attn, stats, cos, sin, seg_col, seg_row, sel, spread,
+    )
+    gu_four = gu_four.astype(F32).transpose(2, 0, 1, 3)
     gate_grad = gu_four[..., :units].reshape(depth, 4 * units)
     up_grad = gu_four[..., units:].reshape(depth, 4 * units)
-
-    dn_two = half_z(split_z(dn_g, n_z, z, 0))
-    dn_four = to_owner_y(dn_two.reshape(2, 2, depth, units).transpose(1, 0, 2, 3), 0)
-    down_grad = dn_four.transpose(1, 0, 3, 2).reshape(4 * units, depth)
-
-    o_one = scatter_z(split_z(o_g, n_z, z, 0), n_z)[0]
-    o_grad = to_owner_y(o_one.reshape(2, depth, q_cols), 0).transpose(0, 2, 1).reshape(
-        2 * q_cols, depth
-    )
-
-    in_one = scatter_z(split_z(in_g, n_z, z, 0), n_z)[0]
-    in_two = to_owner_y(in_one.reshape(2, depth, compact), 0)
+    down_grad = dn_four.astype(F32).transpose(0, 1, 3, 2).reshape(4 * units, depth)
+    o_grad = o_two.astype(F32).transpose(0, 2, 1).reshape(2 * q_cols, depth)
+    in_two = in_two.astype(F32)
 
     def columns(lo, hi):
         return jnp.concatenate([in_two[0, :, lo:hi], in_two[1, :, lo:hi]], axis=1)
@@ -876,8 +1189,8 @@
     ) / jnp.stack([attn_gain, ffn_gain]).astype(F32)
 
     return (
-        output[None],
-        input_grad[None],
+        output.reshape(tokens.shape),
+        input_grad.reshape(tokens.shape),
         gains[0],
         q_grad,
         k_grad,

time: 895 us -> 795 us (0.89)
  the two profiles are of different devices: /device:TPU:0 before, /device:TPU:18 now
where the time goes in v3:
time: 795 us; the launch traced here: 791 us
  Pallas kernels  583 us (73%)
  local copies, waits for them, and re-layouts  115 us (14%)
  matrix products  63.6 us (8%)
  other arithmetic  24.5 us (3%)
    pallas_call x1, Pallas kernels, back(): pl.pallas_call(lambda *refs: back_kernel(n_z, n_tp, scale, min(256, full_...  310 us
    pallas_call x1, Pallas kernels, front(): pl.pallas_call(lambda *refs: front_kernel(n_z, n_tp, scale, min(256, full...  273 us
    dot_general x8, matrix products, dot(): return lax.dot_general(a, b, (dims, ((), ())), preferred_element_type=F32)  63.6 us
  transfers between devices with their start and end apart: 2, of which 0 were waited for; matrix products, arithmetic and copies ran while one was open for 2% of the time, Pallas kernels for 0%

profile of v3, /device:TPU:18, one launch (start us, length us, event | category | flops | bytes accessed | tf_op | source)
XLA Modules:
  0.0 790.6 jit_solution(7068449844590006964)
XLA Ops:
  2.1 1.3 convert_reduce_fusion
  3.5 0.8 copy.81
  4.2 1.7 copy.74
  6.0 1.7 copy.59
  7.7 1.7 copy.73
  9.3 1.7 copy.58
  11.0 0.9 fusion.10.refs_10_.refs_19_
  11.9 1.4 reshape.206
  13.3 0.8 copy.88
  14.7 1.0 copy.65.refs_7_.refs_17_
  15.7 1.1 fusion.9.refs_9_.refs_20_
  16.8 5.2 reshape.209
  22.0 1.3 copy.87
  23.3 2.0 reshape.207
  25.2 4.9 reshape.208
  30.2 0.9 pad.4.clone
  31.1 2.0 copy_bitcast_fusion.1
  33.1 3.1 fusion.11
  36.2 1.1 pad_maximum_fusion.5.refs_2_
  37.4 6.4 concatenate.24.refs_4_
  43.8 273.1 %front.1 = (bf16[2560,768]{1,0:T(8,128)(2,1)}, bf16[4,2,320,320]{3,2,1,0:T(8,128)(2,1)}, bf16[4,2,320,1328]{3,2,1,0:T(8,128)(2,1)}, f32[8,2560]{1,0:T(8,128)}, b...) custom-call(bf16[512,2560]{1,0:T(8,128)(2,1)} %bitcast.73, ...), custom_call_target="tpu_custom_call" | custom-call | tf_op jit(solution)/shard_map/front/pallas_call | solution.py:623
  316.9 8.9 %fusion.33 = (bf16[1,8,128,2560]{3,2,1,0:T(8,128)(2,1)}, bf16[1,8,128,2560]{3,2,1,0:T(8,128)(2,1)}) fusion(bf16[2,8,128,2560]{3,2,1,0:T(8,128)(2,1)} %get-tuple-element.29), kind=kLoop, calls=%fused_computation.94 | loop fusion | bytes 20971520 | tf_op jit(solution)/shard_map/slice | solution.py:1148
  325.8 8.9 %fusion.32 = (bf16[1,8,128,2560]{3,2,1,0:T(8,128)(2,1)}, bf16[1,8,128,2560]{3,2,1,0:T(8,128)(2,1)}) fusion(bf16[2,8,128,2560]{3,2,1,0:T(8,128)(2,1)} %get-tuple-element.30), kind=kLoop, calls=%fused_computation.93 | loop fusion | bytes 20971520 | tf_op jit(solution)/shard_map/slice | solution.py:1148
  334.7 8.8 %fusion.3 = f32[1024,864]{0,1:T(8,128)S(1)} fusion(bf16[1024,2560]{1,0:T(8,128)(2,1)} %bitcast.94, bf16[2560,1328]{1,0:T(8,128)(2,1)} %bitcast.79), kind=kOutput, calls=%fused_computation.7 | convolution fusion | flops 4529848320 | bytes 13369344 | tf_op jit(solution)/shard_map/dot_general | solution.py:26
  343.5 6.1 multiply_convert_fusion.5
  349.7 0.9 copy-done.17
  350.6 4.5 fusion.35
  355.1 1.6 copy.68
  356.7 2.9 pad_maximum_fusion.2
  359.7 11.1 %fusion.31 = f32[2560,864]{0,1:T(8,128)} fusion(bf16[1024,2560]{1,0:T(8,128)(2,1)} %bitcast.95, bf16[1024,432]{0,1:T(8,128)(2,1)S(1)} %copy-done.16, bf16[1024,432]{0,1:T(8,128)(2,1)S(1)} %copy-done.15), kind=kOutput, calls=%fused_computation.92 | convolution fusion | flops 4533387264 | bytes 15859712 | tf_op jit(solution)/shard_map/dot_general | solution.py:26
  370.8 6.8 fusion.1
  377.6 6.1 multiply_convert_fusion.3
  383.8 2.8 copy.69
  386.6 1.3 pad_maximum_fusion.3
  387.9 3.0 copy.67
  391.0 7.9 fusion
  398.8 4.3 copy.71
  403.1 4.1 copy.66
  407.3 12.3 %add_convert_fusion = bf16[2560,864]{0,1:T(8,128)(2,1)} fusion(f32[2560,864]{0,1:T(8,128)} %fusion.31, bf16[1024,2560]{1,0:T(8,128)(2,1)} %bitcast.86, bf16[1024,432]{0,1:T(8,128)(2,1)} %copy-done.14, bf16[1024,432]{0,1:T(8,128)(2,1)} %copy-done.13), kind=kOutput, calls=%fused_computation | convolution fusion | flops 4537810944 | bytes 20283392 | tf_op jit(solution)/shard_map/dot_general | solution.py:26
  419.6 7.2 copy.70
  426.8 2.9 pad_maximum_fusion.1.refs_4_
  429.7 2.4 pad_maximum_fusion.refs_3_
  432.1 309.6 %back.1 = (bf16[4,128,2560]{2,1,0:T(8,128)(2,1)}, bf16[4,128,2560]{2,1,0:T(8,128)(2,1)}, bf16[2,2,320,864]{3,2,1,0:T(8,128)(2,1)}, bf16[2,2,320,432]{3,2,1,0:T(8...) custom-call(bf16[512,2560]{1,0:T(8,128)(2,1)} %bitcast.74, bf16[512,2560]{1,0:T(8,128)(2,1)} %bitcast.76, ...), custom_call_target="tpu_custom_call" | custom-call | tf_op jit(solution)/shard_map/back/pallas_call | solution.py:1004
  741.7 1.2 convert_element_type.91
  743.3 1.1 multiply_reduce_fusion.2
  744.4 0.9 pad_maximum_fusion.6
  745.3 0.9 pad_maximum_fusion.7
  746.5 1.0 fusion.34
  747.5 3.5 copy.76
  751.1 4.8 reshape.217
  755.9 2.3 multiply_reduce_fusion
  758.2 3.5 copy.75
  761.7 3.9 reshape.216
  766.1 0.9 copy-done
  768.2 2.6 collective-permute-start.1
  771.0 1.7 copy.77
  772.7 2.7 reshape.223
  775.4 0.8 copy.79
  776.2 0.8 copy.80
  777.1 3.5 copy.78
  780.6 4.7 reshape.225
  786.0 1.5 copy.92
  787.5 1.2 copy-done.6
  788.7 1.5 copy.93
  (99 shorter events, 5.0 us)
Async XLA Ops:
  0.6 13.5 %copy-start.9 = (bf16[320,640]{1,0:T(8,128)(2,1)S(1)}, bf16[320,640]{1,0:T(8,128)(2,1)}, u32[]{:S(2)}) copy-start(bf16[320,640]{1,0:T(8,128)(2,1)} %param.15) | copy-start | bytes 1228804
  4.2 10.4 %copy-start.23 = (s32[1,1024]{1,0:T(1,128)S(1)}, s32[1,1024]{1,0:T(1,128)}, u32[]{:S(2)}) copy-start(s32[1,1024]{1,0:T(1,128)} %refs_18_.1) | copy-start | bytes 12292
  16.8 6.5 copy-start.4
  31.1 5.1 copy-start.18
  31.1 5.1 copy-start.19
  33.1 4.3 copy-start.2
  33.1 4.3 copy-start.3
  325.8 17.7 %slice-start.6 = ((s8[5242880]{0:T(1024)(128)(4,1)}), s8[1048576]{0:T(1024)(128)(4,1)S(1)}, s32[]{:S(2)}) async-start(s8[5242880]{0:T(1024)(128)(4,1)} %bitcast.96), calls=%async_computation.6 | async-start | bytes 2097152
  334.7 8.8 %slice-start.7 = ((s8[5242880]{0:T(1024)(128)(4,1)}), s8[4194304]{0:T(1024)(128)(4,1)S(1)}, s32[]{:S(2)}) async-start(s8[5242880]{0:T(1024)(128)(4,1)} %bitcast.96), calls=%async_computation.7 | async-start | bytes 8388608
  349.7 0.9 copy-start.17
  355.1 4.6 copy-start.15
  355.1 4.6 copy-start.16
  356.7 14.1 %slice-start = ((s8[7208960]{0:T(1024)(128)(4,1)}), s8[4194304]{0:T(1024)(128)(4,1)S(1)}, s32[]{:S(2)}) async-start(s8[7208960]{0:T(1024)(128)(4,1)} %bitcast.82), calls=%async_computation | async-start | bytes 8388608
  356.7 14.1 %slice-start.2 = ((s8[5242880]{0:T(1024)(128)(4,1)}), s8[4194304]{0:T(1024)(128)(4,1)S(1)}, s32[]{:S(2)}) async-start(s8[5242880]{0:T(1024)(128)(4,1)} %bitcast.87), calls=%async_computation.2 | async-start | bytes 8388608
  359.6 11.2 %slice-start.1 = ((s8[7208960]{0:T(1024)(128)(4,1)}), s8[3014656]{0:T(1024)(128)(4,1)S(1)}, s32[]{:S(2)}) async-start(s8[7208960]{0:T(1024)(128)(4,1)} %bitcast.82), calls=%async_computation.1 | async-start | bytes 6029312
  359.6 11.2 %slice-start.3 = ((s8[5242880]{0:T(1024)(128)(4,1)}), s8[1048576]{0:T(1024)(128)(4,1)S(1)}, s32[]{:S(2)}) async-start(s8[5242880]{0:T(1024)(128)(4,1)} %bitcast.87), calls=%async_computation.3 | async-start | bytes 2097152
  359.6 18.0 %slice-start.4 = ((s8[5242880]{0:T(1024)(128)(4,1)}), s8[4194304]{0:T(1024)(128)(4,1)S(1)}, s32[]{:S(2)}) async-start(s8[5242880]{0:T(1024)(128)(4,1)} %bitcast.91), calls=%async_computation.4 | async-start | bytes 8388608
  370.8 6.8 slice-start.5
  383.8 2.8 copy-start.13
  383.8 2.8 copy-start.14
  426.8 2.9 copy-start.1
  743.0 1.5 copy-start.21
  743.2 2.1 copy-start.20
  743.2 3.0 copy-start.8
  761.7 4.0 copy-start.5
  765.6 1.4 copy-start
  765.6 2.1 copy-start.12
  766.0 4.8 copy-start.22
  766.0 2.1 collective-permute-start
  767.8 3.1 copy-start.24
  767.8 3.1 copy-start.25
  768.2 17.2 %collective-permute-start.1 = (f32[2,320]{1,0:T(2,128)S(1)}, f32[2,320]{1,0:T(2,128)S(1)}, u32[]{:S(2)}, u32[]{:S(2)}) collective-permute-start(f32[2,320]{1,0:T(2,128)S(1)} %fusion.30), channel_id=1, source_target_pairs={{0,2},{1,3},{2,0},{3,1},{4,6},{5,7},{6,4},{7,5},{8,10},{9,11},{10,... | collective-permute-start | bytes 7688 | tf_op jit(solution)/shard_map/ppermute | solution.py:22
  770.8 4.6 copy-start.10
  770.8 5.4 copy-start.11
  780.6 5.4 copy-start.7
  786.0 2.7 copy-start.6

commit v4 on v3

--- a/solution.py
+++ b/solution.py
@@ -392,12 +392,32 @@
     ]
 
 
+def eye(n):
+    shape = (n, n)
+    same = lax.broadcasted_iota(jnp.int32, shape, 0) == lax.broadcasted_iota(jnp.int32, shape, 1)
+    return same.astype(F32).astype(BF16)
+
+
+def head_spread(n_q, compact):
+    shape = (compact, (n_q + 2) * LANES)
+    col, lane = (lax.broadcasted_iota(jnp.int32, shape, d) for d in (0, 1))
+    at, head = col % HEAD_DIM, col // HEAD_DIM
+    spot = head * LANES + at + jnp.where((at >= HALF) & (head < n_q + 1), 64 - HALF, 0)
+    return ((spot == lane) & (head < n_q + 2)).astype(F32).astype(BF16)
+
+
+def head_select(n_q):
+    shape = (n_q * LANES, n_q * HEAD_DIM)
+    lane, col = (lax.broadcasted_iota(jnp.int32, shape, d) for d in (0, 1))
+    return ((col // HEAD_DIM) * LANES + col % HEAD_DIM == lane).astype(F32).astype(BF16)
+
+
 def front_kernel(
     n_z, n_tp, scale, q_block,
-    x_here, dy_here, in_send, o_send, w3_send, cos, sin, seg_col, seg_row, spread, sel,
-    w_heads, w_o, w3, gains, norm_attn, dy_all, norm_all, attn, rot, stats, mid,
+    x_here, dy_here, q_w, k_w, v_w, o_w, gate_w, up_w, down_w, extra, seg_col, seg_row,
+    w_heads, w_o, w3, gains, norm_attn, dy_all, norm_all, attn, rot, stats, mid, cos, sin, spread, sel,
     w_in, x_all, qkv, to_core, held, landed, total, free, in_cross, o_cross, w3_cross,
-    heads_v, norm_v, own_v, root_v, o_v, send_sems, recv_sems, sems,
+    heads_v, norm_v, own_v, root_v, o_v, in_send, o_send, w3_send, send_sems, recv_sems, sems,
 ):
     at = Place(n_z, n_tp)
     links = Links(send_sems, recv_sems)
@@ -417,6 +437,19 @@
     def block_of(ref, index):
         return ref.at[pl.ds(pl.multiple_of(index * rows, rows), rows)]
 
+    q_cols, kv_cols = q_w.shape[1] // 2, k_w.shape[1] // 2
+    units = gate_w.shape[1] // 4
+    wide = w3_send.shape[3] - units
+    for j in range(2):
+        in_send[j] = jnp.concatenate(
+            [
+                q_w[:, j * q_cols : (j + 1) * q_cols],
+                k_w[:, j * kv_cols : (j + 1) * kv_cols],
+                v_w[:, j * kv_cols : (j + 1) * kv_cols],
+                extra[...],
+            ],
+            axis=1,
+        )
     greet(at.peers())
     f_in = WeightFlow(
         links, at, w_in, in_send.at[1 - y], lambda m: in_send.at[y], lambda m: in_cross
@@ -429,6 +462,17 @@
     dy_mine = block_of(dy_here, t)
     dy_own = move(dy_here.reshape(n_tp, rows, width), dy_all.at[0, pl.ds(y * n_tp, n_tp)])
 
+    for j in range(2):
+        half = o_w[j * q_cols : (j + 1) * q_cols, :]
+        o_send[j] = dot(half, eye(q_cols), ((0,), (0,))).astype(BF16)
+    for j in range(4):
+        cols = slice(j * units, (j + 1) * units)
+        w3_send[j % 2, j // 2, :, : 2 * units] = jnp.concatenate(
+            [gate_w[:, cols], up_w[:, cols]], axis=1
+        )
+        w3_send[j % 2, j // 2, :, wide:] = dot(
+            down_w[cols, :], eye(units), ((0,), (0,))
+        ).astype(BF16)
     f_in.crossed()
     cross_in = move(in_cross, w_in.at[z, 1 - y])
     f_o = WeightFlow(
@@ -450,6 +494,28 @@
     for rel, p in ins:
         if rel == top:
             f_in.take(rel, p)
+    lane = lax.broadcasted_iota(jnp.int32, (1, LANES), 1)
+    within = lane % 64
+    frequency = jnp.where(
+        within < HALF, jnp.exp(within.astype(F32) * (-2.0 * math.log(ROPE_BASE) / HEAD_DIM)), 0.0
+    )
+    sign = jnp.where(lane < 64, -1.0, 1.0)
+    n_q = rot.shape[1] // LANES - 2
+    spread[...] = head_spread(n_q, w_in.shape[3])
+    sel[...] = head_select(n_q)
+    step = min(256, full_len)
+
+    def tables(c, carry):
+        at_rows = pl.ds(pl.multiple_of(c * step, step), step)
+        before = jnp.where(seg_row[...] < seg_col[at_rows, :], 1.0, 0.0)
+        start = jnp.sum(before, axis=1, keepdims=True)
+        position = (c * step + lax.broadcasted_iota(jnp.int32, (step, 1), 0)).astype(F32)
+        angles = (position - start) * frequency
+        cos[at_rows, :] = jnp.cos(angles)
+        sin[at_rows, :] = jnp.sin(angles) * sign
+        return carry
+
+    lax.fori_loop(0, full_len // step, tables, 0)
     tok_x.wait_recv()
     diag = block_of(x_all, flip(y_of, 2))
     tok_c.append(links.send(diag, diag, at.core))
@@ -457,8 +523,6 @@
 
     for copy in tok_c:
         copy.wait_recv()
-
-    step = min(256, full_len)
 
     def find_root(c, carry):
         at_rows = pl.ds(pl.multiple_of(c * step, step), step)
@@ -527,8 +591,6 @@
     ]
     for p in (0, 1):
         f_o.take(top, p)
-
-    n_q = rot.shape[1] // LANES - 2
 
     def turn(c, carry):
         r = pl.ds(pl.multiple_of(c * step, step), step)
@@ -608,15 +670,17 @@
     links.finish(layer)
 
 
-def front(n_z, n_tp, scale, x_here, dy_here, in_send, o_send, w3_send, cos, sin, seg_col, seg_row, spread, sel):
+def front(n_z, n_tp, scale, x_here, dy_here, weights, extra, seg_col, seg_row):
+    q_w, k_w, v_w, o_w, gate_w, up_w, down_w = weights
     half_len, width = x_here.shape
     full_len = 2 * half_len
     rows = half_len // n_tp
-    depth, compact = in_send.shape[1:]
-    heads = spread.shape[1]
-    q_cols = sel.shape[1]
-    n_q = heads // LANES - 2
-    w3_cols = w3_send.shape[3]
+    depth, q_cols = q_w.shape[0], q_w.shape[1] // 2
+    n_q = q_cols // HEAD_DIM
+    heads = (n_q + 2) * LANES
+    compact = q_cols + k_w.shape[1] + extra.shape[1]
+    units = gate_w.shape[1] // 4
+    w3_cols = wide_of(units) + units
     any_, vmem = pl.BlockSpec(memory_space=pl.ANY), pl.BlockSpec(memory_space=pltpu.VMEM)
     n_sems = 80 + 6 * n_z + 32
     shape = jax.ShapeDtypeStruct
@@ -634,9 +698,13 @@
             shape((full_len, heads), BF16),
             shape((full_len, 2 * n_q), F32),
             shape((rows, width), F32),
+            shape((full_len, LANES), F32),
+            shape((full_len, LANES), F32),
+            shape((compact, heads), BF16),
+            shape((n_q * LANES, q_cols), BF16),
         ),
-        in_specs=[any_] * 5 + [vmem] * 6,
-        out_specs=(any_, any_, any_, vmem, any_, any_, any_, vmem, vmem, vmem, vmem),
+        in_specs=[any_] * 2 + [vmem] * 10,
+        out_specs=(any_, any_, any_, vmem, any_, any_, any_) + (vmem,) * 8,
         scratch_shapes=[
             pltpu.VMEM((n_z, 2, depth, compact), BF16),
             pltpu.VMEM((full_len, width), BF16),
@@ -650,6 +718,9 @@
             pltpu.VMEM((rows, width), BF16),
             pltpu.VMEM((full_len, 1), F32),
             pltpu.VMEM((width, q_cols), BF16),
+            pltpu.VMEM((2, depth, compact), BF16),
+            pltpu.VMEM((2, depth, q_cols), BF16),
+            pltpu.VMEM((2, 2, depth, w3_cols), BF16),
             pltpu.SemaphoreType.DMA((n_sems,)),
             pltpu.SemaphoreType.DMA((n_sems,)),
             pltpu.SemaphoreType.DMA((16,)),
@@ -658,7 +729,123 @@
             collective_id=1, has_side_effects=True, vmem_limit_bytes=VMEM_LIMIT
         ),
         name="front",
-    )(x_here, dy_here, in_send, o_send, w3_send, cos, sin, seg_col, seg_row, spread, sel)
+    )(x_here, dy_here, *weights, extra, seg_col, seg_row)
+
+
+def wide_of(units):
+    return -(-2 * units // LANES) * LANES
+
+
+def act_kernel(norm, dy, w3, d_gu, hidden):
+    units = hidden.shape[2]
+    n = norm.shape[0] * norm.shape[1]
+    wide = w3.shape[1] - units
+    gate_up = dot(norm[...].reshape(n, norm.shape[2]), w3[:, : 2 * units])
+    d_hidden = dot(dy[...].reshape(n, dy.shape[2]), w3[:, wide:])
+    gate, up = gate_up[:, :units], gate_up[:, units:]
+    sig = 1.0 / (1.0 + jnp.exp(-gate))
+    silu = gate * sig
+    hidden[...] = (silu * up).astype(BF16).reshape(hidden.shape)
+    d_up = (d_hidden * silu).astype(BF16)
+    d_gate = (d_hidden * up * sig * (1.0 + gate * (1.0 - sig))).astype(BF16)
+    d_gu[...] = jnp.concatenate([d_gate, d_up], axis=1).reshape(d_gu.shape)
+
+
+def act(norm, dy, w3, units):
+    blocks, rows, width = norm.shape
+    per = max(1, 256 // rows)
+    one = lambda cols: pl.BlockSpec((per, rows, cols), lambda i: (i, 0, 0))
+    return pl.pallas_call(
+        act_kernel,
+        grid=(blocks // per,),
+        out_shape=(
+            jax.ShapeDtypeStruct((blocks, rows, 2 * units), BF16),
+            jax.ShapeDtypeStruct((blocks, rows, units), BF16),
+        ),
+        in_specs=[one(width), one(width), pl.BlockSpec(w3.shape, lambda i: (0, 0))],
+        out_specs=(one(2 * units), one(units)),
+        compiler_params=pltpu.CompilerParams(vmem_limit_bytes=VMEM_LIMIT),
+        name="act",
+    )(norm, dy, w3)
+
+
+def terms_kernel(norm, dy, d_gu, hidden, gu, dn):
+    def term(lhs, rhs, out):
+        n = lhs.shape[0] * lhs.shape[1]
+        value = dot(lhs[...].reshape(n, lhs.shape[2]), rhs[...].reshape(n, rhs.shape[2]), ((0,), (0,)))
+        out[...] = value.astype(BF16).reshape(out.shape)
+
+    term(norm, d_gu, gu)
+    term(dy, hidden, dn)
+
+
+def terms(norm, dy, d_gu, hidden, n_z):
+    blocks, rows, width = norm.shape
+    depth, units = width // n_z // 2, hidden.shape[2]
+    group = 1
+    while 2 * depth * group % LANES:
+        group *= 2
+    cols = pl.BlockSpec((blocks, rows, 2 * depth * group), lambda i: (0, 0, i))
+    whole = lambda a: pl.BlockSpec(a.shape, lambda i: (0, 0, 0))
+    out = lambda c: pl.BlockSpec((group, 2, depth, c), lambda i: (i, 0, 0, 0))
+    return pl.pallas_call(
+        terms_kernel,
+        grid=(n_z // group,),
+        out_shape=(
+            jax.ShapeDtypeStruct((n_z, 2, depth, 2 * units), BF16),
+            jax.ShapeDtypeStruct((n_z, 2, depth, units), BF16),
+        ),
+        in_specs=[cols, cols, whole(d_gu), whole(hidden)],
+        out_specs=(out(2 * units), out(units)),
+        compiler_params=pltpu.CompilerParams(vmem_limit_bytes=VMEM_LIMIT),
+        name="terms",
+    )(norm, dy, d_gu, hidden)
+
+
+def finish_kernel(
+    gu, dn, o, ins, q_w, k_w, v_w, gate_w, up_w,
+    q_grad, k_grad, v_grad, o_grad, gate_grad, up_grad, down_grad, sums,
+):
+    depth = q_w.shape[0]
+    units, q_cols, kv_cols = dn.shape[3], q_w.shape[1] // 2, k_w.shape[1] // 2
+    one = eye(depth)
+
+    def weighted(w, g):
+        return jnp.sum(w[...].astype(F32) * g[...], axis=1, keepdims=True)
+
+    gate_grad[...] = jnp.concatenate(
+        [gu[j // 2, j % 2, :, :units].astype(F32) for j in range(4)], axis=1
+    )
+    up_grad[...] = jnp.concatenate(
+        [gu[j // 2, j % 2, :, units:].astype(F32) for j in range(4)], axis=1
+    )
+    for j in range(4):
+        down_grad[j * units : (j + 1) * units, :] = dot(dn[j // 2, j % 2], one, ((0,), (0,)))
+    for j in range(2):
+        o_grad[j * q_cols : (j + 1) * q_cols, :] = dot(o[j], one, ((0,), (0,)))
+    lo = 0
+    for grad, cols in ((q_grad, q_cols), (k_grad, kv_cols), (v_grad, kv_cols)):
+        grad[...] = jnp.concatenate(
+            [ins[j, :, lo : lo + cols].astype(F32) for j in range(2)], axis=1
+        )
+        lo += cols
+    first = weighted(q_w, q_grad) + weighted(k_w, k_grad) + weighted(v_w, v_grad)
+    second = weighted(gate_w, gate_grad) + weighted(up_w, up_grad)
+    lane = lax.broadcasted_iota(jnp.int32, sums.shape, 1)
+    sums[...] = jnp.where(lane == 0, first, second)
+
+
+def finish(gu, dn, o, ins, q_w, k_w, v_w, gate_w, up_w, o_shape, down_shape):
+    shape = lambda dims: jax.ShapeDtypeStruct(dims, F32)
+    return pl.pallas_call(
+        finish_kernel,
+        out_shape=(
+            shape(q_w.shape), shape(k_w.shape), shape(v_w.shape), shape(o_shape),
+            shape(gate_w.shape), shape(up_w.shape), shape(down_shape), shape((q_w.shape[0], LANES)),
+        ),
+        compiler_params=pltpu.CompilerParams(vmem_limit_bytes=VMEM_LIMIT),
+        name="finish",
+    )(gu, dn, o, ins, q_w, k_w, v_w, gate_w, up_w)
 
 
 class TpGather:
@@ -1064,139 +1251,53 @@
 ):
     n_z = lax.axis_size("fsdp")
     n_tp = lax.axis_size("tp")
-    z, y, t = lax.axis_index("fsdp"), lax.axis_index("ctx"), lax.axis_index("tp")
-    zb = z // (n_z // 2)
     _, half_len, width = tokens.shape
     full_len = segments.shape[1]
     rows = half_len // n_tp
-    depth = q_weight.shape[0]
-    q_cols = q_weight.shape[1] // 2
-    kv_cols = k_weight.shape[1] // 2
     units = gate_weight.shape[1] // 4
-    n_q = q_cols // HEAD_DIM
     scale = HEAD_DIM ** (-0.5)
-    me = y * n_tp + t
-
-    def two(w):
-        return w.reshape(w.shape[0], 2, -1).transpose(1, 0, 2)
-
-    extra = jnp.stack([attn_gain, ffn_gain], axis=1)
-    extra = jnp.broadcast_to(jnp.pad(extra, ((0, 0), (0, 30)))[None], (2, depth, 32))
-    in_send = jnp.concatenate([two(q_weight), two(k_weight), two(v_weight), extra], axis=2)
-    compact = in_send.shape[2]
-    o_send = o_weight.reshape(2, q_cols, depth).transpose(0, 2, 1)
-
-    def four(w):
-        return w.reshape(depth, 2, 2, units).transpose(2, 1, 0, 3)
-
-    wide = -(-2 * units // LANES) * LANES
-    w3_send = jnp.concatenate(
-        [
-            four(gate_weight),
-            four(up_weight),
-            jnp.zeros((2, 2, depth, wide - 2 * units), BF16),
-            down_weight.reshape(2, 2, units, depth).transpose(1, 0, 3, 2),
-        ],
-        axis=3,
-    )
+
+    extra = jnp.pad(jnp.stack([attn_gain, ffn_gain], axis=1), ((0, 0), (0, 30)))
     x_here = tokens.reshape(half_len, width)
-
+    dy_here = cotangent.reshape(half_len, width)
     seg = segments.reshape(full_len)
-    start = jnp.sum((seg[None, :] < seg[:, None]).astype(jnp.int32), axis=1)
-    offset = (jnp.arange(full_len, dtype=jnp.int32) - start).astype(F32)
-    lane = jnp.arange(LANES)
-    within = lane % 64
-    frequency = jnp.where(
-        within < HALF, jnp.exp(within.astype(F32) * (-2.0 * math.log(ROPE_BASE) / HEAD_DIM)), 0.0
-    )
-    angles = offset[:, None] * frequency[None, :]
-    cos = jnp.cos(angles)
-    sin = jnp.sin(angles) * jnp.where(lane < 64, -1.0, 1.0)[None, :]
     seg_col, seg_row = seg[:, None], seg[None, :]
-
-    col = jnp.arange(compact)
-    at = col % HEAD_DIM
-    head = col // HEAD_DIM
-    spot = jnp.where(head < n_q + 1, at + jnp.where(at >= HALF, 64 - HALF, 0), at) + head * LANES
-    spot = jnp.where(head < n_q + 2, spot, -1)
-    spread = (spot[:, None] == jnp.arange((n_q + 2) * LANES)[None, :]).astype(BF16)
-    c320 = jnp.arange(q_cols)
-    sel = (
-        jnp.arange(n_q * LANES)[:, None]
-        == ((c320 // HEAD_DIM) * LANES + c320 % HEAD_DIM)[None, :]
-    ).astype(BF16)
-
-    w_heads, w_o, w3, gains, norm_attn, dy_all, norm_all, attn, rot, stats, mid = front(
-        n_z, n_tp, scale, x_here, cotangent.reshape(half_len, width), in_send, o_send, w3_send,
-        cos, sin, seg_col, seg_row, spread, sel,
+    (
+        w_heads, w_o, w3, gains, norm_attn, dy_all, norm_all, attn, rot, stats, mid, cos, sin, spread, sel,
+    ) = front(
+        n_z, n_tp, scale, x_here, dy_here,
+        (q_weight, k_weight, v_weight, o_weight, gate_weight, up_weight, down_weight),
+        extra, seg_col, seg_row,
     )
     w3 = w3.reshape(width, -1)
-    w_gu, w_dn = w3[:, : 2 * units], w3[:, wide:]
-
-    def mlp(norm, dy):
-        norm = norm.reshape(full_len, width)
-        dy = dy.reshape(full_len, width)
-        gate_up = dot(norm, w_gu)
-        gate, up = gate_up[:, :units], gate_up[:, units:]
-        sig = jax.nn.sigmoid(gate)
-        hidden = (gate * sig * up).astype(BF16)
-        d_hidden = dot(dy, w_dn)
-        d_up = (d_hidden * gate * sig).astype(BF16)
-        d_gate = (d_hidden * up * sig * (1.0 + gate * (1.0 - sig))).astype(BF16)
-        return hidden, jnp.concatenate([d_gate, d_up], axis=1), norm, dy
-
-    own_mlp, far_mlp = mlp(norm_all[0], dy_all[0]), mlp(norm_all[1], dy_all[1])
-
-    gu_g = dot(own_mlp[2], own_mlp[1], ((0,), (0,))) + dot(far_mlp[2], far_mlp[1], ((0,), (0,)))
-    dn_g = dot(own_mlp[3], own_mlp[0], ((0,), (0,))) + dot(far_mlp[3], far_mlp[0], ((0,), (0,)))
-
-    def blocks(own, far):
-        return jnp.stack([own, far]).reshape(2, 2 * n_tp, rows, own.shape[1])
-
+    norm_all = norm_all.reshape(4 * n_tp, rows, width)
+    dy_all = dy_all.reshape(4 * n_tp, rows, width)
+    d_gu, hidden = act(norm_all, dy_all, w3, units)
+    gu_src, dn_src = terms(norm_all, dy_all, d_gu, hidden, n_z)
     output, input_grad, gu_four, dn_four, o_two, in_two = back(
-        n_z, n_tp, scale, units, wide,
-        x_here, cotangent.reshape(half_len, width), w3, blocks(own_mlp[1], far_mlp[1]),
-        blocks(own_mlp[0], far_mlp[0]),
-        gu_g.astype(BF16).reshape(n_z, 2, depth, 2 * units),
-        dn_g.astype(BF16).reshape(n_z, 2, depth, units),
-        w_o, w_heads, norm_attn.reshape(2 * n_tp, rows, width),
+        n_z, n_tp, scale, units, wide_of(units),
+        x_here, dy_here, w3, d_gu.reshape(2, 2 * n_tp, rows, 2 * units),
+        hidden.reshape(2, 2 * n_tp, rows, units), gu_src, dn_src, w_o, w_heads,
+        norm_attn.reshape(2 * n_tp, rows, width),
         mid, gains, rot, attn, stats, cos, sin, seg_col, seg_row, sel, spread,
     )
-    gu_four = gu_four.astype(F32).transpose(2, 0, 1, 3)
-    gate_grad = gu_four[..., :units].reshape(depth, 4 * units)
-    up_grad = gu_four[..., units:].reshape(depth, 4 * units)
-    down_grad = dn_four.astype(F32).transpose(0, 1, 3, 2).reshape(4 * units, depth)
-    o_grad = o_two.astype(F32).transpose(0, 2, 1).reshape(2 * q_cols, depth)
-    in_two = in_two.astype(F32)
-
-    def columns(lo, hi):
-        return jnp.concatenate([in_two[0, :, lo:hi], in_two[1, :, lo:hi]], axis=1)
-
-    q_grad = columns(0, q_cols)
-    k_grad = columns(q_cols, q_cols + kv_cols)
-    v_grad = columns(q_cols + kv_cols, q_cols + 2 * kv_cols)
-
-    def gain_sum(pairs):
-        return sum(jnp.sum(w.astype(F32) * g, axis=1) for w, g in pairs)
-
-    gains = sum_tp(
-        jnp.stack(
-            [
-                gain_sum(((q_weight, q_grad), (k_weight, k_grad), (v_weight, v_grad))),
-                gain_sum(((gate_weight, gate_grad), (up_weight, up_grad))),
-            ]
-        )
-    ) / jnp.stack([attn_gain, ffn_gain]).astype(F32)
+    q_grad, k_grad, v_grad, o_grad, gate_grad, up_grad, down_grad, sums = finish(
+        gu_four, dn_four, o_two, in_two, q_weight, k_weight, v_weight, gate_weight, up_weight,
+        o_weight.shape, down_weight.shape,
+    )
+    gain_sums = sum_tp(sums[:, :2])
+    attn_gain_grad = gain_sums[:, 0] / attn_gain.astype(F32)
+    ffn_gain_grad = gain_sums[:, 1] / ffn_gain.astype(F32)
 
     return (
         output.reshape(tokens.shape),
         input_grad.reshape(tokens.shape),
-        gains[0],
+        attn_gain_grad,
         q_grad,
         k_grad,
         v_grad,
         o_grad,
-        gains[1],
+        ffn_gain_grad,
         gate_grad,
         up_grad,
         down_grad,

time: 795 us -> 678 us (0.85)
  the two profiles are of different devices: /device:TPU:18 before, /device:TPU:19 now
where the time goes in v4:
time: 678 us; the launch traced here: 671 us
  Pallas kernels  633 us (93%)
  local copies, waits for them, and re-layouts  24.3 us (4%)
  starting transfers between devices  10.1 us (1%)
    pallas_call x1, Pallas kernels, back(): pl.pallas_call(lambda *refs: back_kernel(n_z, n_tp, scale, min(256, full_...  304 us
    pallas_call x1, Pallas kernels, front(): pl.pallas_call(lambda *refs: front_kernel(n_z, n_tp, scale, min(256, full...  275 us
    pallas_call x1, Pallas kernels, act(): pl.pallas_call(act_kernel, grid=(blocks // per,), out_shape=(jax.ShapeDty...  23.4 us
    pallas_call x1, Pallas kernels, terms(): pl.pallas_call(terms_kernel, grid=(n_z // group,), out_shape=(jax.ShapeDt...  22.6 us
    unnamed x20, local copies, waits for them, and re-layouts  20.1 us
  transfers between devices with their start and end apart: 2, of which 1 were waited for; matrix products, arithmetic and copies ran while one was open for 1% of the time, Pallas kernels for 0%

profile of v4, /device:TPU:19, one launch (start us, length us, event | category | flops | bytes accessed | tf_op | source)
XLA Modules:
  0.0 671.4 jit_solution(6411231038878772809)
XLA Ops:
  0.6 0.0 copy-start.2
  0.7 0.8 stack.9
  1.4 0.7 stack.10
  2.1 0.2 copy.47
  2.3 1.7 copy.48.refs_3_.k_w
  4.0 1.7 copy.49.refs_4_.v_w
  5.7 2.0 copy.50.refs_5_
  7.7 1.7 copy.52.refs_10_.refs_17_
  9.4 0.0 copy-done.2
  9.4 1.5 copy.51.refs_8_
  10.9 0.7 pad.4.refs_9_
  11.5 275.0 %front.1 = (bf16[2560,768]{1,0:T(8,128)(2,1)}, bf16[4,2,320,320]{3,2,1,0:T(8,128)(2,1)}, bf16[4,2,320,1328]{3,2,1,0:T(8,128)(2,1)}, f32[8,2560]{1,0:T(8,128)}, b...) custom-call(bf16[512,2560]{1,0:T(8,128)(2,1)} %bitcast.19, ...), custom_call_target="tpu_custom_call" | custom-call | tf_op jit(solution)/shard_map/front/pallas_call | solution.py:687
  286.5 23.4 %act.1 = (bf16[16,128,864]{2,1,0:T(8,128)(2,1)}, bf16[16,128,432]{2,1,0:T(8,128)(2,1)}) custom-call(bf16[16,128,2560]{2,1,0:T(8,128)(2,1)} %bitcast.14, bf16[16,128,2560]{2,1,0:T(8,128)(2,1)} %bitcast.12, bf16[2560,1328]{1,0:T(8,128)(2,1)} %bitcast.16), custom_call_target="tpu_custom_call" | custom-call | tf_op jit(solution)/shard_map/act/pallas_call | solution.py:758
  309.9 22.6 %terms.1 = (bf16[4,2,320,864]{3,2,1,0:T(8,128)(2,1)}, bf16[4,2,320,432]{3,2,1,0:T(8,128)(2,1)}) custom-call(bf16[16,128,2560]{2,1,0:T(8,128)(2,1)} %bitcast.15, bf16[16,128,2560]{2,1,0:T(8,128)(2,1)} %bitcast.13, bf16[16,128,864]{2,1,0:T(8,128)(2,1)} %get-tuple-element.47.d_gu, bf16[16,128,432]{2,1,0:T(8,128)(2,1)} %get-tuple-element.48.hidden), custom_call_target="tpu_custom_call" | custom-call | tf_op jit(solution)/shard_map/terms/pallas_call | solution.py:791
  332.5 303.8 %back.1 = (bf16[4,128,2560]{2,1,0:T(8,128)(2,1)}, bf16[4,128,2560]{2,1,0:T(8,128)(2,1)}, bf16[2,2,320,864]{3,2,1,0:T(8,128)(2,1)}, bf16[2,2,320,432]{3,2,1,0:T(8...) custom-call(bf16[512,2560]{1,0:T(8,128)(2,1)} %bitcast.20, bf16[512,2560]{1,0:T(8,128)(2,1)} %bitcast.22, ...), custom_call_target="tpu_custom_call" | custom-call | tf_op jit(solution)/shard_map/back/pallas_call | solution.py:1191
  636.3 8.4 %finish.1 = (f32[320,640]{1,0:T(8,128)}, f32[320,160]{1,0:T(8,128)}, f32[320,160]{1,0:T(8,128)}, f32[640,320]{1,0:T(8,128)}, f32[320,1728]{1,0:T(8,128)}, /*inde...) custom-call(bf16[2,2,320,864]{3,2,1,0:T(8,128)(2,1)} %get-tuple-element.65.gu, ...), custom_call_target="tpu_custom_call" | custom-call | tf_op jit(solution)/shard_map/finish/pallas_call | solution.py:840
  644.7 0.0 copy-start
  644.7 7.7 %collective-permute-start = (f32[320,2]{1,0:T(8,128)}, f32[320,2]{1,0:T(8,128)S(1)}, u32[]{:S(2)}, u32[]{:S(2)}) collective-permute-start(f32[320,2]{1,0:T(8,128)} %bitcast.27), channel_id=1, source_target_pairs={{0,1},{1,0},{2,3},{3,2},{4,5},{5,4},{6,7},{7,6},{8,9},{9,8},{10,11... | collective-permute-start | bytes 7688 | tf_op jit(solution)/shard_map/ppermute | solution.py:22
  652.4 1.2 collective-permute-done
  653.6 0.9 slice_add_fusion
  654.5 2.5 collective-permute-start.1
  657.0 1.8 copy.56
  658.8 1.8 copy.57
  660.6 2.4 copy.58
  663.0 0.0 copy-done
  663.0 0.0 copy-start.3
  663.0 0.0 copy-start.4
  663.0 2.2 copy.59
  665.2 0.0 collective-permute-done.1
  665.2 0.3 slice_reduce_fusion
  665.5 0.0 copy-done.3
  665.5 0.0 copy-done.4
  665.5 0.6 convert_divide_fusion
  666.1 0.0 copy-start.1
  666.1 3.6 copy.62
  669.6 0.0 copy-done.1
  669.7 1.5 copy.63
  (2 shorter events, 0.0 us)
Async XLA Ops:
  0.6 8.7 %copy-start.2 = (bf16[1728,320]{0,1:T(8,128)(2,1)S(1)}, bf16[1728,320]{0,1:T(8,128)(2,1)}, u32[]{:S(2)}) copy-start(bf16[1728,320]{0,1:T(8,128)(2,1)} %param.22) | copy-start | bytes 3317764
  644.7 18.3 %copy-start = (f32[1728,320]{1,0:T(8,128)S(1)}, f32[1728,320]{1,0:T(8,128)}, u32[]{:S(2)}) copy-start(f32[1728,320]{1,0:T(8,128)} %get-tuple-element.109) | copy-start | bytes 6635524
  644.7 8.9 %collective-permute-start = (f32[320,2]{1,0:T(8,128)}, f32[320,2]{1,0:T(8,128)S(1)}, u32[]{:S(2)}, u32[]{:S(2)}) collective-permute-start(f32[320,2]{1,0:T(8,128)} %bitcast.27), channel_id=1, source_target_pairs={{0,1},{1,0},{2,3},{3,2},{4,5},{5,4},{6,7},{7,6},{8,9},{9,8},{10,11... | collective-permute-start | bytes 7688 | tf_op jit(solution)/shard_map/ppermute | solution.py:22
  654.5 10.6 %collective-permute-start.1 = (f32[320,2]{1,0:T(8,128)S(1)}, f32[320,2]{1,0:T(8,128)S(1)}, u32[]{:S(2)}, u32[]{:S(2)}) collective-permute-start(f32[320,2]{1,0:T(8,128)S(1)} %slice_add_fusion), channel_id=1, source_target_pairs={{0,2},{1,3},{2,0},{3,1},{4,6},{5,7},{6,4},{7,5},{8,10},{9,11},{10,... | collective-permute-start | bytes 7688 | tf_op jit(solution)/shard_map/ppermute | solution.py:22
  663.0 2.5 copy-start.3
  663.0 2.5 copy-start.4
  666.1 3.6 copy-start.1

commit v5 on v4

--- a/solution.py
+++ b/solution.py
@@ -101,8 +101,8 @@
 
 
 def sum_tp(value):
-    value = value + pp(value, "tp", 1)
-    return value + pp(value, "tp", 2)
+    others = [pp(value, "tp", mask) for mask in range(1, lax.axis_size("tp"))]
+    return value, others
 
 
 def below(top):
@@ -398,6 +398,12 @@
     return same.astype(F32).astype(BF16)
 
 
+def column(row):
+    n = row.shape[1]
+    same = lax.broadcasted_iota(jnp.int32, (n, n), 0) == lax.broadcasted_iota(jnp.int32, (n, n), 1)
+    return jnp.sum(jnp.where(same, row.astype(F32), 0.0), axis=1, keepdims=True)
+
+
 def head_spread(n_q, compact):
     shape = (compact, (n_q + 2) * LANES)
     col, lane = (lax.broadcasted_iota(jnp.int32, shape, d) for d in (0, 1))
@@ -414,8 +420,8 @@
 
 def front_kernel(
     n_z, n_tp, scale, q_block,
-    x_here, dy_here, q_w, k_w, v_w, o_w, gate_w, up_w, down_w, extra, seg_col, seg_row,
-    w_heads, w_o, w3, gains, norm_attn, dy_all, norm_all, attn, rot, stats, mid, cos, sin, spread, sel,
+    x_here, dy_here, q_w, k_t, v_t, o_t, gate_w, up_w, down_t, gain_rows, seg_row,
+    w_heads, w_o, w3, gains, norm_attn, dy_all, norm_all, attn, rot, stats, mid, cos, sin, spread, sel, seg_col,
     w_in, x_all, qkv, to_core, held, landed, total, free, in_cross, o_cross, w3_cross,
     heads_v, norm_v, own_v, root_v, o_v, in_send, o_send, w3_send, send_sems, recv_sems, sems,
 ):
@@ -437,18 +443,19 @@
     def block_of(ref, index):
         return ref.at[pl.ds(pl.multiple_of(index * rows, rows), rows)]
 
-    q_cols, kv_cols = q_w.shape[1] // 2, k_w.shape[1] // 2
+    q_cols, kv_cols = q_w.shape[1] // 2, k_t.shape[0] // 2
     units = gate_w.shape[1] // 4
     wide = w3_send.shape[3] - units
+    extra = jnp.concatenate(
+        [column(gain_rows[i : i + 1, :]) for i in range(2)]
+        + [jnp.zeros((depth, in_send.shape[2] - q_cols - 2 * kv_cols - 2), F32)],
+        axis=1,
+    ).astype(BF16)
     for j in range(2):
+        kv = slice(j * kv_cols, (j + 1) * kv_cols)
+        turned = [dot(w[kv, :], eye(kv_cols), ((0,), (0,))).astype(BF16) for w in (k_t, v_t)]
         in_send[j] = jnp.concatenate(
-            [
-                q_w[:, j * q_cols : (j + 1) * q_cols],
-                k_w[:, j * kv_cols : (j + 1) * kv_cols],
-                v_w[:, j * kv_cols : (j + 1) * kv_cols],
-                extra[...],
-            ],
-            axis=1,
+            [q_w[:, j * q_cols : (j + 1) * q_cols], *turned, extra], axis=1
         )
     greet(at.peers())
     f_in = WeightFlow(
@@ -463,29 +470,26 @@
     dy_own = move(dy_here.reshape(n_tp, rows, width), dy_all.at[0, pl.ds(y * n_tp, n_tp)])
 
     for j in range(2):
-        half = o_w[j * q_cols : (j + 1) * q_cols, :]
-        o_send[j] = dot(half, eye(q_cols), ((0,), (0,))).astype(BF16)
+        o_send[j] = o_t[:, j * q_cols : (j + 1) * q_cols]
     for j in range(4):
         cols = slice(j * units, (j + 1) * units)
         w3_send[j % 2, j // 2, :, : 2 * units] = jnp.concatenate(
             [gate_w[:, cols], up_w[:, cols]], axis=1
         )
-        w3_send[j % 2, j // 2, :, wide:] = dot(
-            down_w[cols, :], eye(units), ((0,), (0,))
-        ).astype(BF16)
+        w3_send[j % 2, j // 2, :, wide:] = down_t[:, cols]
     f_in.crossed()
     cross_in = move(in_cross, w_in.at[z, 1 - y])
     f_o = WeightFlow(
         links, at, w_o, o_send.at[1 - y], lambda m: o_send.at[y], lambda m: o_cross
     )
     top = n_z // 2
+    tok_y.wait_recv()
     f_3 = WeightFlow(
         links, at, w3, w3_send.at[1 - y],
         lambda m: w3_send.at[y, 1 - zb if m == top else zb],
         lambda m: w3_cross if m is None else w3_cross.at[1 - zb if m == top else zb],
     )
     dy_y = links.send(dy_mine, dy_all.at[0, me], at.yy)
-    tok_y.wait_recv()
     y_of, x_of = flip(me, n_tp), flip(me, 2)
     y_block = block_of(x_all, y_of)
     tok_x = links.send(y_block, y_block, at.x)
@@ -507,7 +511,15 @@
 
     def tables(c, carry):
         at_rows = pl.ds(pl.multiple_of(c * step, step), step)
-        before = jnp.where(seg_row[...] < seg_col[at_rows, :], 1.0, 0.0)
+        mine = jnp.concatenate(
+            [
+                column(seg_row[:, pl.ds(pl.multiple_of(c * step + i, LANES), LANES)])
+                for i in range(0, step, LANES)
+            ],
+            axis=0,
+        ).astype(jnp.int32)
+        seg_col[at_rows, :] = mine
+        before = jnp.where(seg_row[...] < mine, 1.0, 0.0)
         start = jnp.sum(before, axis=1, keepdims=True)
         position = (c * step + lax.broadcasted_iota(jnp.int32, (step, 1), 0)).astype(F32)
         angles = (position - start) * frequency
@@ -567,12 +579,13 @@
     f_o.crossed()
     if group == 1:
         project(0, True)
-    f_3.own()
-    f_3.crossed()
-    for rel in f_in.order():
-        for p in (0, 1):
-            if rel != top:
+    rest = [rel for rel in f_in.order() if rel != top]
+    for rel in [top] + rest:
+        if rel != top:
+            for p in (0, 1):
                 f_in.take(rel, p)
+        if rel == rest[-1]:
+            f_3.own()
         if group == 1:
             project(rel, False)
     if group > 1:
@@ -581,14 +594,9 @@
     heads_out = move(heads_v, w_heads)
     norm_out = move(norm_v, norm_attn)
     own_o = [move(o_send.at[y], w_o.at[z, y]), move(o_cross, w_o.at[z, 1 - y])]
-    own_3 = [move(w3_send.at[y, zb], w3.at[z, y]), move(w3_cross.at[zb], w3.at[z, 1 - y])]
     dy_y.wait_recv()
     dy_x = links.send(dy_all.at[0, y_of], dy_all.at[0, y_of], at.x)
     dy_c = [links.send(dy_all.at[0, y_of], dy_all.at[0, y_of], at.core)]
-    dy_z = [
-        links.send(half_rows(dy_mine, p, rows), half_rows(dy_all.at[1, me], p, rows), at.zz(top))
-        for p in (0, 1)
-    ]
     for p in (0, 1):
         f_o.take(top, p)
 
@@ -610,6 +618,15 @@
             dy_x.wait_recv()
             d_of = flip(y_of, 2)
             dy_c.append(links.send(dy_all.at[0, d_of], dy_all.at[0, d_of], at.core))
+        if i == 2:
+            f_3.crossed()
+            own_3 = [move(w3_send.at[y, zb], w3.at[z, y]), move(w3_cross.at[zb], w3.at[z, 1 - y])]
+            dy_z = [
+                links.send(
+                    half_rows(dy_mine, p, rows), half_rows(dy_all.at[1, me], p, rows), at.zz(top)
+                )
+                for p in (0, 1)
+            ]
     for rel in f_o.order():
         for p in (0, 1):
             if rel != top:
@@ -626,8 +643,6 @@
     layer = LayerSum(links, at, rows, (to_core, held, landed, total, free), product)
     layer.begin()
     layer.middle()
-    for p in (0, 1):
-        f_3.take(top, p)
     norm_own = LayerGather(links, at, norm_all.at[0], rows)
     norm_far = LayerGather(links, at, norm_all.at[1], rows)
     far = []
@@ -644,17 +659,19 @@
         far.append(links.send(src, half_rows(norm_all.at[1, me], p, rows), at.zz(top)))
         norm_own.own(p, src)
     keep = move(own_v, norm_all.at[0, me])
+    norm_own.far_first()
+    norm_own.far_second()
     for p in (0, 1):
         dy_z[p].wait_recv()
         dy_far.own(p)
-    norm_own.far_first()
+    dy_far.far_first()
+    for p in (0, 1):
+        f_3.take(top, p)
+    dy_far.far_second()
     for p in (0, 1):
         far[p].wait_recv()
         norm_far.own(p)
-    norm_own.far_second()
-    dy_far.far_first()
     norm_far.far_first()
-    dy_far.far_second()
     norm_far.far_second()
     for rel in f_3.order():
         for p in (0, 1):
@@ -670,15 +687,15 @@
     links.finish(layer)
 
 
-def front(n_z, n_tp, scale, x_here, dy_here, weights, extra, seg_col, seg_row):
-    q_w, k_w, v_w, o_w, gate_w, up_w, down_w = weights
+def front(n_z, n_tp, scale, x_here, dy_here, weights, gain_rows, seg_row):
+    q_w, k_t, _, _, gate_w, _, _ = weights
     half_len, width = x_here.shape
     full_len = 2 * half_len
     rows = half_len // n_tp
     depth, q_cols = q_w.shape[0], q_w.shape[1] // 2
     n_q = q_cols // HEAD_DIM
     heads = (n_q + 2) * LANES
-    compact = q_cols + k_w.shape[1] + extra.shape[1]
+    compact = q_cols + k_t.shape[0] + 32
     units = gate_w.shape[1] // 4
     w3_cols = wide_of(units) + units
     any_, vmem = pl.BlockSpec(memory_space=pl.ANY), pl.BlockSpec(memory_space=pltpu.VMEM)
@@ -702,9 +719,10 @@
             shape((full_len, LANES), F32),
             shape((compact, heads), BF16),
             shape((n_q * LANES, q_cols), BF16),
+            shape((full_len, 1), jnp.int32),
         ),
-        in_specs=[any_] * 2 + [vmem] * 10,
-        out_specs=(any_, any_, any_, vmem, any_, any_, any_) + (vmem,) * 8,
+        in_specs=[any_] * 2 + [vmem] * 9,
+        out_specs=(any_, any_, any_, vmem, any_, any_, any_) + (vmem,) * 9,
         scratch_shapes=[
             pltpu.VMEM((n_z, 2, depth, compact), BF16),
             pltpu.VMEM((full_len, width), BF16),
@@ -729,7 +747,7 @@
             collective_id=1, has_side_effects=True, vmem_limit_bytes=VMEM_LIMIT
         ),
         name="front",
-    )(x_here, dy_here, *weights, extra, seg_col, seg_row)
+    )(x_here, dy_here, *weights, gain_rows, seg_row)
 
 
 def wide_of(units):
@@ -753,7 +771,7 @@
 
 def act(norm, dy, w3, units):
     blocks, rows, width = norm.shape
-    per = max(1, 256 // rows)
+    per = max(1, 512 // rows)
     one = lambda cols: pl.BlockSpec((per, rows, cols), lambda i: (i, 0, 0))
     return pl.pallas_call(
         act_kernel,
@@ -802,50 +820,77 @@
     )(norm, dy, d_gu, hidden)
 
 
-def finish_kernel(
-    gu, dn, o, ins, q_w, k_w, v_w, gate_w, up_w,
-    q_grad, k_grad, v_grad, o_grad, gate_grad, up_grad, down_grad, sums,
-):
+def finish_in_kernel(gu, ins, q_w, k_t, v_t, gate_w, up_w, q_grad, k_grad, v_grad, sums):
     depth = q_w.shape[0]
-    units, q_cols, kv_cols = dn.shape[3], q_w.shape[1] // 2, k_w.shape[1] // 2
+    units, q_cols, kv_cols = gu.shape[3] // 2, q_w.shape[1] // 2, k_t.shape[0] // 2
     one = eye(depth)
-
-    def weighted(w, g):
-        return jnp.sum(w[...].astype(F32) * g[...], axis=1, keepdims=True)
-
-    gate_grad[...] = jnp.concatenate(
-        [gu[j // 2, j % 2, :, :units].astype(F32) for j in range(4)], axis=1
-    )
-    up_grad[...] = jnp.concatenate(
-        [gu[j // 2, j % 2, :, units:].astype(F32) for j in range(4)], axis=1
-    )
+    q_grad[...] = jnp.concatenate([ins[j, :, :q_cols].astype(F32) for j in range(2)], axis=1)
+    first = jnp.sum(q_w[...].astype(F32) * q_grad[...], axis=1, keepdims=True)
+    lo = q_cols
+    for w, grad in ((k_t, k_grad), (v_t, v_grad)):
+        for j in range(2):
+            grad[j * kv_cols : (j + 1) * kv_cols, :] = dot(
+                ins[j, :, lo : lo + kv_cols], one, ((0,), (0,))
+            )
+        lo += kv_cols
+        first += column(jnp.sum(w[...].astype(F32) * grad[...], axis=0, keepdims=True))
+    second = jnp.zeros((depth, 1), F32)
     for j in range(4):
-        down_grad[j * units : (j + 1) * units, :] = dot(dn[j // 2, j % 2], one, ((0,), (0,)))
-    for j in range(2):
-        o_grad[j * q_cols : (j + 1) * q_cols, :] = dot(o[j], one, ((0,), (0,)))
-    lo = 0
-    for grad, cols in ((q_grad, q_cols), (k_grad, kv_cols), (v_grad, kv_cols)):
-        grad[...] = jnp.concatenate(
-            [ins[j, :, lo : lo + cols].astype(F32) for j in range(2)], axis=1
-        )
-        lo += cols
-    first = weighted(q_w, q_grad) + weighted(k_w, k_grad) + weighted(v_w, v_grad)
-    second = weighted(gate_w, gate_grad) + weighted(up_w, up_grad)
+        cols = slice(j * units, (j + 1) * units)
+        weights = jnp.concatenate([gate_w[:, cols], up_w[:, cols]], axis=1).astype(F32)
+        second += jnp.sum(weights * gu[j // 2, j % 2].astype(F32), axis=1, keepdims=True)
     lane = lax.broadcasted_iota(jnp.int32, sums.shape, 1)
     sums[...] = jnp.where(lane == 0, first, second)
 
 
-def finish(gu, dn, o, ins, q_w, k_w, v_w, gate_w, up_w, o_shape, down_shape):
+def finish_in(gu, ins, q_w, k_t, v_t, gate_w, up_w):
     shape = lambda dims: jax.ShapeDtypeStruct(dims, F32)
+    return pl.pallas_call(
+        finish_in_kernel,
+        out_shape=(
+            shape(q_w.shape), shape(k_t.shape), shape(v_t.shape), shape((q_w.shape[0], LANES)),
+        ),
+        compiler_params=pltpu.CompilerParams(vmem_limit_bytes=VMEM_LIMIT),
+        name="finish_in",
+    )(gu, ins, q_w, k_t, v_t, gate_w, up_w)
+
+
+def finish_kernel(gu, dn, o, rows_a, rows_b, gate_grad, up_grad, down_grad, o_grad, out_a, out_b, sems):
+    copies = [
+        pltpu.make_async_copy(src, dst, sems.at[i])
+        for i, (src, dst) in enumerate(((rows_a, out_a), (rows_b, out_b)))
+    ]
+    for copy in copies:
+        copy.start()
+    units = dn.shape[3]
+    for grad, part in ((gate_grad, slice(0, units)), (up_grad, slice(units, 2 * units))):
+        grad[...] = jnp.concatenate(
+            [gu[j // 2, j % 2, :, part].astype(F32) for j in range(4)], axis=1
+        )
+    down_grad[...] = jnp.concatenate([dn[j // 2, j % 2].astype(F32) for j in range(4)], axis=1)
+    o_grad[...] = jnp.concatenate([o[j].astype(F32) for j in range(2)], axis=1)
+    for copy in copies:
+        copy.wait()
+
+
+def finish(gu, dn, o, rows_a, rows_b):
+    depth, units, q_cols = dn.shape[2], dn.shape[3], o.shape[2]
+    shape = lambda cols: jax.ShapeDtypeStruct((depth, cols), F32)
+    like = lambda a: jax.ShapeDtypeStruct(a.shape, a.dtype)
+    any_, vmem = pl.BlockSpec(memory_space=pl.ANY), pl.BlockSpec(memory_space=pltpu.VMEM)
     return pl.pallas_call(
         finish_kernel,
         out_shape=(
-            shape(q_w.shape), shape(k_w.shape), shape(v_w.shape), shape(o_shape),
-            shape(gate_w.shape), shape(up_w.shape), shape(down_shape), shape((q_w.shape[0], LANES)),
+            shape(4 * units), shape(4 * units), shape(4 * units), shape(2 * q_cols),
+            like(rows_a), like(rows_b),
         ),
+        in_specs=[vmem] * 3 + [any_] * 2,
+        out_specs=(vmem,) * 4 + (any_,) * 2,
+        scratch_shapes=[pltpu.SemaphoreType.DMA((2,))],
         compiler_params=pltpu.CompilerParams(vmem_limit_bytes=VMEM_LIMIT),
+        cost_estimate=pl.CostEstimate(flops=0, bytes_accessed=20 * 2**20, transcendentals=0),
         name="finish",
-    )(gu, dn, o, ins, q_w, k_w, v_w, gate_w, up_w)
+    )(gu, dn, o, rows_a, rows_b)
 
 
 class TpGather:
@@ -1009,6 +1054,7 @@
     f_gu = GradFlow(links, at, gu_src, gu_land, True, gu_out, gu_pass, fetch_with(fetch_gu))
     f_dn = GradFlow(links, at, dn_src, dn_land, True, dn_out, dn_pass, fetch_with(fetch_dn))
     f_gu.first()
+    f_dn.first()
 
     def term(seq, lhs, lo, hi):
         def product(r, cols):
@@ -1043,7 +1089,6 @@
     own.middle()
     heads_v = w3_v.at[:, : w_heads.shape[1]]
     load_heads = move(w_heads, heads_v)
-    f_dn.first()
     load_hid.wait()
     ffn_far = LayerSum(links, at, rows, bufs_a, term(1, hid_v, wide, wide + units), far)
     ffn_own = LayerSum(links, at, rows, bufs_b, term(0, hid_v, wide, wide + units), own)
@@ -1073,7 +1118,6 @@
     f_gu.spread()
     gather.far_second()
     ffn_far.middle()
-    f_dn.spread()
     gather.last()
 
     load_o.wait()
@@ -1107,6 +1151,7 @@
     f_o.first()
     gather.drain()
     load_norm = move(norm_attn, d_proj)
+    f_dn.spread()
     ffn_own.middle()
     dk_sum[...] = jnp.zeros_like(dk_sum)
     dv_sum[...] = jnp.zeros_like(dv_sum)
@@ -1118,9 +1163,6 @@
             f_gu.cross()
             f_dn.cross()
             sent_ffn = send_far(ffn_far, 1)
-        if i == 1:
-            f_o.spread()
-            f_o.cross()
     attend_back_keys(scale, n_q, cos, sin, d_qkv, dk_sum, dv_sum)
 
     load_heads.wait()
@@ -1129,9 +1171,6 @@
         value = d_qkv[pl.ds(pl.multiple_of(flip_all(me, r) * rows, rows), rows), :]
         return dot(value, w3_v[cols, : w_heads.shape[1]], ((1,), (1,)))
 
-    d_in = LayerSum(links, at, rows, bufs_a, d_term, ffn_far)
-    d_in.begin()
-    d_in.middle()
     in_cols = slice(w_heads.shape[1], w_heads.shape[1] + spread.shape[0])
     in_src = w3_v.reshape(n_z, 2, depth, w3_v.shape[1]).at[:, :, :, in_cols]
     f_in = GradFlow(links, at, in_src, in_land, False, in_out, None)
@@ -1141,6 +1180,11 @@
         lhs = jnp.concatenate([d_proj[b, :, span_of(owner)] for b in range(n_b)], axis=0)
         w3_v[span_of(owner), in_cols] = dot(lhs, packed, ((0,), (0,))).astype(BF16)
     f_in.first()
+    d_in = LayerSum(links, at, rows, bufs_a, d_term, ffn_far)
+    d_in.begin()
+    d_in.middle()
+    f_o.spread()
+    f_o.cross()
     out_g, in_g = TpGather(links, at, output), TpGather(links, at, input_grad)
     stay = []
     for p, value in enumerate(d_in.end()):
@@ -1257,17 +1301,16 @@
     units = gate_weight.shape[1] // 4
     scale = HEAD_DIM ** (-0.5)
 
-    extra = jnp.pad(jnp.stack([attn_gain, ffn_gain], axis=1), ((0, 0), (0, 30)))
     x_here = tokens.reshape(half_len, width)
     dy_here = cotangent.reshape(half_len, width)
-    seg = segments.reshape(full_len)
-    seg_col, seg_row = seg[:, None], seg[None, :]
+    k_t, v_t, o_t, down_t = k_weight.T, v_weight.T, o_weight.T, down_weight.T
     (
         w_heads, w_o, w3, gains, norm_attn, dy_all, norm_all, attn, rot, stats, mid, cos, sin, spread, sel,
+        seg_col,
     ) = front(
         n_z, n_tp, scale, x_here, dy_here,
-        (q_weight, k_weight, v_weight, o_weight, gate_weight, up_weight, down_weight),
-        extra, seg_col, seg_row,
+        (q_weight, k_t, v_t, o_t, gate_weight, up_weight, down_t),
+        jnp.stack([attn_gain, ffn_gain]), segments,
     )
     w3 = w3.reshape(width, -1)
     norm_all = norm_all.reshape(4 * n_tp, rows, width)
@@ -1279,28 +1322,31 @@
         x_here, dy_here, w3, d_gu.reshape(2, 2 * n_tp, rows, 2 * units),
         hidden.reshape(2, 2 * n_tp, rows, units), gu_src, dn_src, w_o, w_heads,
         norm_attn.reshape(2 * n_tp, rows, width),
-        mid, gains, rot, attn, stats, cos, sin, seg_col, seg_row, sel, spread,
+        mid, gains, rot, attn, stats, cos, sin, seg_col, segments, sel, spread,
     )
-    q_grad, k_grad, v_grad, o_grad, gate_grad, up_grad, down_grad, sums = finish(
-        gu_four, dn_four, o_two, in_two, q_weight, k_weight, v_weight, gate_weight, up_weight,
-        o_weight.shape, down_weight.shape,
+    q_grad, k_grad, v_grad, sums = finish_in(
+        gu_four, in_two, q_weight, k_t, v_t, gate_weight, up_weight
     )
-    gain_sums = sum_tp(sums[:, :2])
-    attn_gain_grad = gain_sums[:, 0] / attn_gain.astype(F32)
-    ffn_gain_grad = gain_sums[:, 1] / ffn_gain.astype(F32)
+    here, others = sum_tp(sums[:, :2].T)
+    gate_grad, up_grad, down_grad, o_grad, output, input_grad = finish(
+        gu_four, dn_four, o_two, output, input_grad
+    )
+    gain_sums = sum(others, here)
+    attn_gain_grad = gain_sums[0] / attn_gain.astype(F32)
+    ffn_gain_grad = gain_sums[1] / ffn_gain.astype(F32)
 
     return (
         output.reshape(tokens.shape),
         input_grad.reshape(tokens.shape),
         attn_gain_grad,
         q_grad,
-        k_grad,
-        v_grad,
-        o_grad,
+        k_grad.T,
+        v_grad.T,
+        o_grad.T,
         ffn_gain_grad,
         gate_grad,
         up_grad,
-        down_grad,
+        down_grad.T,
     )
 
 

time: 678 us -> 763 us (1.13)
  the two profiles are of different devices: /device:TPU:19 before, /device:TPU:0 now
where the time goes in v5:
time: 763 us; the launch traced here: 757 us
  Pallas kernels  750 us (98%)
    pallas_call x1, Pallas kernels, back(): pl.pallas_call(lambda *refs: back_kernel(n_z, n_tp, scale, min(256, full_...  285 us
    pallas_call x1, Pallas kernels, front(): pl.pallas_call(lambda *refs: front_kernel(n_z, n_tp, scale, min(256, full...  249 us
    pallas_call x1, Pallas kernels, finish(): pl.pallas_call(finish_kernel, out_shape=(shape(4 * units), shape(4 * unit...  165 us
    pallas_call x1, Pallas kernels, act(): pl.pallas_call(act_kernel, grid=(blocks // per,), out_shape=(jax.ShapeDty...  23.7 us
    pallas_call x1, Pallas kernels, terms(): pl.pallas_call(terms_kernel, grid=(n_z // group,), out_shape=(jax.ShapeDt...  22.2 us
  transfers between devices with their start and end apart: 3, of which 0 were waited for; matrix products, arithmetic and copies ran while one was open for 0% of the time, Pallas kernels for 22%

profile of v5, /device:TPU:0, one launch (start us, length us, event | category | flops | bytes accessed | tf_op | source)
XLA Modules:
  0.0 757.3 jit_solution(8060472419240892729)
XLA Ops:
  0.6 0.7 stack.9
  1.3 0.7 stack.10
  2.0 0.6 pad_maximum_fusion.refs_9_
  2.6 248.9 %front.1 = (bf16[2560,768]{1,0:T(8,128)(2,1)}, bf16[4,2,320,320]{3,2,1,0:T(8,128)(2,1)}, bf16[4,2,320,1328]{3,2,1,0:T(8,128)(2,1)}, f32[8,2560]{1,0:T(8,128)}, b...) custom-call(bf16[512,2560]{1,0:T(8,128)(2,1)} %bitcast.29, ...), custom_call_target="tpu_custom_call" | custom-call | tf_op jit(solution)/shard_map/front/pallas_call | solution.py:704
  251.5 23.7 %act.1 = (bf16[16,128,864]{2,1,0:T(8,128)(2,1)}, bf16[16,128,432]{2,1,0:T(8,128)(2,1)}) custom-call(bf16[16,128,2560]{2,1,0:T(8,128)(2,1)} %bitcast.24, bf16[16,128,2560]{2,1,0:T(8,128)(2,1)} %bitcast.22, bf16[2560,1328]{1,0:T(8,128)(2,1)} %bitcast.26), custom_call_target="tpu_custom_call" | custom-call | tf_op jit(solution)/shard_map/act/pallas_call | solution.py:776
  275.2 22.2 %terms.1 = (bf16[4,2,320,864]{3,2,1,0:T(8,128)(2,1)}, bf16[4,2,320,432]{3,2,1,0:T(8,128)(2,1)}) custom-call(bf16[16,128,2560]{2,1,0:T(8,128)(2,1)} %bitcast.25, bf16[16,128,2560]{2,1,0:T(8,128)(2,1)} %bitcast.23, bf16[16,128,864]{2,1,0:T(8,128)(2,1)} %get-tuple-element.50.d_gu, bf16[16,128,432]{2,1,0:T(8,128)(2,1)} %get-tuple-element.51.hidden), custom_call_target="tpu_custom_call" | custom-call | tf_op jit(solution)/shard_map/terms/pallas_call | solution.py:809
  297.3 284.8 %back.1 = (bf16[4,128,2560]{2,1,0:T(8,128)(2,1)}, bf16[4,128,2560]{2,1,0:T(8,128)(2,1)}, bf16[2,2,320,864]{3,2,1,0:T(8,128)(2,1)}, bf16[2,2,320,432]{3,2,1,0:T(8...) custom-call(bf16[512,2560]{1,0:T(8,128)(2,1)} %bitcast.30, bf16[512,2560]{1,0:T(8,128)(2,1)} %bitcast.32, ...), custom_call_target="tpu_custom_call" | custom-call | tf_op jit(solution)/shard_map/back/pallas_call | solution.py:1235
  582.1 5.7 finish_in.1
  587.8 0.9 slice_bitcast_fusion
  588.7 0.6 collective-permute-start.1
  589.3 0.3 collective-permute-start.2
  589.6 1.3 collective-permute-start
  590.9 0.0 copy-start
  590.9 0.0 copy-start.1
  590.9 0.0 copy-start.2
  590.9 165.2 %finish.1 = (f32[320,1728]{1,0:T(8,128)}, f32[320,1728]{1,0:T(8,128)}, f32[320,1728]{1,0:T(8,128)}, f32[320,640]{1,0:T(8,128)}, bf16[4,128,2560]{2,1,0:T(8,128)(2,1)}, /*index=5*/bf16[4,128,2560]{2,1,0:T(8,128)(2,1)}) custom-call(bf16[2,2,320,864]{3,2,1,0:T(8,128)(2,1)} %get-tuple-element.67.gu, bf16[2,2,320,432]{3,2,1,0:T(8,128)(2,1)} %get-tuple-element.68.dn, ...), custom_call_target="tpu_custom_call" | custom-call | bytes 20971520 | tf_op jit(solution)/shard_map/finish/pallas_call | solution.py:881
  756.1 0.0 collective-permute-done.1
  756.1 0.0 collective-permute-done.2
  756.1 0.0 collective-permute-done
  756.2 0.0 copy-done
  756.2 0.3 slice_reduce_fusion
  756.5 0.0 copy-done.1
  756.5 0.0 copy-done.2
  756.5 0.6 convert_divide_fusion
  (1 shorter events, 0.0 us)
Async XLA Ops:
  588.7 167.4 %collective-permute-start.1 = (f32[2,320]{0,1:T(8,128)S(1)}, f32[2,320]{0,1:T(8,128)S(1)}, u32[]{:S(2)}, u32[]{:S(2)}) collective-permute-start(f32[2,320]{0,1:T(8,128)S(1)} %slice_bitcast_fusion), channel_id=1, source_target_pairs={{0,2},{1,3},{2,0},{3,1},{4,6},{5,7},{6,4},{7,5},{8,10},{9,11},{10,... | collective-permute-start | bytes 7688 | tf_op jit(solution)/shard_map/ppermute | solution.py:22
  589.3 166.8 %collective-permute-start.2 = (f32[2,320]{0,1:T(8,128)S(1)}, f32[2,320]{0,1:T(8,128)S(1)}, u32[]{:S(2)}, u32[]{:S(2)}) collective-permute-start(f32[2,320]{0,1:T(8,128)S(1)} %slice_bitcast_fusion), channel_id=1, source_target_pairs={{0,3},{1,2},{2,1},{3,0},{4,7},{5,6},{6,5},{7,4},{8,11},{9,10},{10,... | collective-permute-start | bytes 7688 | tf_op jit(solution)/shard_map/ppermute | solution.py:22
  589.6 166.5 %collective-permute-start = (f32[2,320]{0,1:T(8,128)S(1)}, f32[2,320]{0,1:T(8,128)S(1)}, u32[]{:S(2)}, u32[]{:S(2)}) collective-permute-start(f32[2,320]{0,1:T(8,128)S(1)} %slice_bitcast_fusion), channel_id=1, source_target_pairs={{0,1},{1,0},{2,3},{3,2},{4,5},{5,4},{6,7},{7,6},{8,9},{9,8},{10,11... | collective-permute-start | bytes 7688 | tf_op jit(solution)/shard_map/ppermute | solution.py:22
  590.9 165.2 %copy-start = (f32[320,128]{1,0:T(8,128)S(1)}, f32[320,128]{1,0:T(8,128)}, u32[]{:S(2)}) copy-start(f32[320,128]{1,0:T(8,128)} %get-tuple-element.75) | copy-start | bytes 491524
  590.9 165.5 %copy-start.1 = (bf16[320]{0:T(512)(128)(2,1)S(1)}, bf16[320]{0:T(512)(128)(2,1)}, u32[]{:S(2)}) copy-start(bf16[320]{0:T(512)(128)(2,1)} %param.19) | copy-start | bytes 1924
  590.9 165.5 %copy-start.2 = (bf16[320]{0:T(512)(128)(2,1)S(1)}, bf16[320]{0:T(512)(128)(2,1)}, u32[]{:S(2)}) copy-start(bf16[320]{0:T(512)(128)(2,1)} %param.14) | copy-start | bytes 1924

commit v6 on v5

--- a/solution.py
+++ b/solution.py
@@ -187,16 +187,18 @@
         self.got = {}
         self.y_copy = links.send(cross, second(None), at.yy)
 
-    def own(self):
+    def own(self, masks=None):
         at = self.at
-        for m in at.masks:
+        for m in at.masks if masks is None else masks:
             dst = self.out.at[at.z, at.y]
             self.got[m, 0] = self.links.send(self.first(m), dst, at.zz(m))
 
-    def crossed(self):
+    def arrived(self):
+        self.y_copy.wait_recv()
+
+    def crossed(self, masks=None):
         at = self.at
-        self.y_copy.wait_recv()
-        for m in at.masks:
+        for m in at.masks if masks is None else masks:
             dst = self.out.at[at.z, 1 - at.y]
             self.got[m, 1] = self.links.send(self.second(m), dst, at.zz(m))
 
@@ -357,20 +359,26 @@
             return copy
 
         level(3)
-        x1 = send(3, 0, at.x)
-        y1 = send(3, 1, at.yy)
+        self.x1 = send(3, 0, at.x)
+        self.y1 = send(3, 1, at.yy)
         level(1)
         x2 = send(1, 2, at.x)
         level(2)
         y2 = send(2, 3, at.yy)
         level(0)
-        x1.wait_recv()
+        self.send, self.tail = send, (x2, y2)
+
+    def second(self):
+        at, h = self.at, self.rows // 2
+        held, landed = self.held, self.landed
+        a, b = slice(0, h), slice(h, self.rows)
+        self.x1.wait_recv()
         held[2, a] = (held[2, a].astype(F32) + landed[0].astype(F32)).astype(BF16)
-        y3 = send(2, 4, at.yy)
-        y1.wait_recv()
+        y3 = self.send(2, 4, at.yy)
+        self.y1.wait_recv()
         held[1, b] = (held[1, b].astype(F32) + landed[1].astype(F32)).astype(BF16)
-        x3 = send(1, 5, at.x)
-        self.tail = (x2, y3, y2, x3)
+        x3 = self.send(1, 5, at.x)
+        self.tail += (y3, x3)
 
     def end(self):
         h = self.rows // 2
@@ -467,7 +475,7 @@
     tok_y = links.send(x_mine, block_of(x_all, me), at.yy)
     x_own = move(x_here, x_all.at[pl.ds(pl.multiple_of(y * (full_len // 2), full_len // 2), full_len // 2)])
     dy_mine = block_of(dy_here, t)
-    dy_own = move(dy_here.reshape(n_tp, rows, width), dy_all.at[0, pl.ds(y * n_tp, n_tp)])
+    dy_in = move(dy_here, norm_v.at[pl.ds(0, full_len // 2)])
 
     for j in range(2):
         o_send[j] = o_t[:, j * q_cols : (j + 1) * q_cols]
@@ -477,6 +485,7 @@
             [gate_w[:, cols], up_w[:, cols]], axis=1
         )
         w3_send[j % 2, j // 2, :, wide:] = down_t[:, cols]
+    f_in.arrived()
     f_in.crossed()
     cross_in = move(in_cross, w_in.at[z, 1 - y])
     f_o = WeightFlow(
@@ -490,6 +499,11 @@
         lambda m: w3_cross if m is None else w3_cross.at[1 - zb if m == top else zb],
     )
     dy_y = links.send(dy_mine, dy_all.at[0, me], at.yy)
+    dy_in.wait()
+    dy_own = move(
+        norm_v.at[pl.ds(0, full_len // 2)].reshape(n_tp, rows, width),
+        dy_all.at[0, pl.ds(y * n_tp, n_tp)],
+    )
     y_of, x_of = flip(me, n_tp), flip(me, 2)
     y_block = block_of(x_all, y_of)
     tok_x = links.send(y_block, y_block, at.x)
@@ -545,6 +559,7 @@
     lax.fori_loop(0, full_len // step, find_root, 0)
     own_in.wait()
     cross_in.wait()
+    dy_own.wait()
 
     pick_gain = (
         lax.broadcasted_iota(jnp.int32, (8, w_in.shape[3]), 1)
@@ -576,6 +591,7 @@
         lax.fori_loop(0, full_len // step, some_rows, 0)
 
     f_o.own()
+    f_o.arrived()
     f_o.crossed()
     if group == 1:
         project(0, True)
@@ -584,8 +600,6 @@
         if rel != top:
             for p in (0, 1):
                 f_in.take(rel, p)
-        if rel == rest[-1]:
-            f_3.own()
         if group == 1:
             project(rel, False)
     if group > 1:
@@ -597,8 +611,15 @@
     dy_y.wait_recv()
     dy_x = links.send(dy_all.at[0, y_of], dy_all.at[0, y_of], at.x)
     dy_c = [links.send(dy_all.at[0, y_of], dy_all.at[0, y_of], at.core)]
+    lower = at.masks[1:]
+    dy_z = [
+        links.send(half_rows(dy_mine, p, rows), half_rows(dy_all.at[1, me], p, rows), at.zz(top))
+        for p in (0, 1)
+    ]
+    f_3.own([top])
     for p in (0, 1):
         f_o.take(top, p)
+    f_3.own(lower)
 
     def turn(c, carry):
         r = pl.ds(pl.multiple_of(c * step, step), step)
@@ -619,14 +640,9 @@
             d_of = flip(y_of, 2)
             dy_c.append(links.send(dy_all.at[0, d_of], dy_all.at[0, d_of], at.core))
         if i == 2:
+            f_3.arrived()
             f_3.crossed()
             own_3 = [move(w3_send.at[y, zb], w3.at[z, y]), move(w3_cross.at[zb], w3.at[z, 1 - y])]
-            dy_z = [
-                links.send(
-                    half_rows(dy_mine, p, rows), half_rows(dy_all.at[1, me], p, rows), at.zz(top)
-                )
-                for p in (0, 1)
-            ]
     for rel in f_o.order():
         for p in (0, 1):
             if rel != top:
@@ -643,6 +659,7 @@
     layer = LayerSum(links, at, rows, (to_core, held, landed, total, free), product)
     layer.begin()
     layer.middle()
+    layer.second()
     norm_own = LayerGather(links, at, norm_all.at[0], rows)
     norm_far = LayerGather(links, at, norm_all.at[1], rows)
     far = []
@@ -659,18 +676,18 @@
         far.append(links.send(src, half_rows(norm_all.at[1, me], p, rows), at.zz(top)))
         norm_own.own(p, src)
     keep = move(own_v, norm_all.at[0, me])
+    f_3.take(top, 0)
     norm_own.far_first()
-    norm_own.far_second()
     for p in (0, 1):
         dy_z[p].wait_recv()
         dy_far.own(p)
+    norm_own.far_second()
     dy_far.far_first()
-    for p in (0, 1):
-        f_3.take(top, p)
-    dy_far.far_second()
     for p in (0, 1):
         far[p].wait_recv()
         norm_far.own(p)
+    dy_far.far_second()
+    f_3.take(top, 1)
     norm_far.far_first()
     norm_far.far_second()
     for rel in f_3.order():
@@ -682,7 +699,7 @@
         gather.drain()
     for copy in dy_c:
         copy.wait_recv()
-    for copy in [dy_own, heads_out, norm_out, keep] + own_3:
+    for copy in [heads_out, norm_out, keep] + own_3:
         copy.wait()
     links.finish(layer)
 
@@ -855,13 +872,9 @@
     )(gu, ins, q_w, k_t, v_t, gate_w, up_w)
 
 
-def finish_kernel(gu, dn, o, rows_a, rows_b, gate_grad, up_grad, down_grad, o_grad, out_a, out_b, sems):
-    copies = [
-        pltpu.make_async_copy(src, dst, sems.at[i])
-        for i, (src, dst) in enumerate(((rows_a, out_a), (rows_b, out_b)))
-    ]
-    for copy in copies:
-        copy.start()
+def finish_kernel(gu, dn, o, rows_a, rows_b, gate_grad, up_grad, down_grad, o_grad, out_a, out_b):
+    out_a[...] = rows_a[...]
+    out_b[...] = rows_b[...]
     units = dn.shape[3]
     for grad, part in ((gate_grad, slice(0, units)), (up_grad, slice(units, 2 * units))):
         grad[...] = jnp.concatenate(
@@ -869,24 +882,18 @@
         )
     down_grad[...] = jnp.concatenate([dn[j // 2, j % 2].astype(F32) for j in range(4)], axis=1)
     o_grad[...] = jnp.concatenate([o[j].astype(F32) for j in range(2)], axis=1)
-    for copy in copies:
-        copy.wait()
 
 
 def finish(gu, dn, o, rows_a, rows_b):
     depth, units, q_cols = dn.shape[2], dn.shape[3], o.shape[2]
     shape = lambda cols: jax.ShapeDtypeStruct((depth, cols), F32)
     like = lambda a: jax.ShapeDtypeStruct(a.shape, a.dtype)
-    any_, vmem = pl.BlockSpec(memory_space=pl.ANY), pl.BlockSpec(memory_space=pltpu.VMEM)
     return pl.pallas_call(
         finish_kernel,
         out_shape=(
             shape(4 * units), shape(4 * units), shape(4 * units), shape(2 * q_cols),
             like(rows_a), like(rows_b),
         ),
-        in_specs=[vmem] * 3 + [any_] * 2,
-        out_specs=(vmem,) * 4 + (any_,) * 2,
-        scratch_shapes=[pltpu.SemaphoreType.DMA((2,))],
         compiler_params=pltpu.CompilerParams(vmem_limit_bytes=VMEM_LIMIT),
         cost_estimate=pl.CostEstimate(flops=0, bytes_accessed=20 * 2**20, transcendentals=0),
         name="finish",
@@ -927,6 +934,7 @@
                 n += 1
         self.got = {}
         self.at_mask = {}
+        self.steps = None
 
     def row(self, part):
         return self.at.y if part == 0 else 1 - self.at.y
@@ -946,11 +954,11 @@
             block, self.land.at[self.slot[m, rel ^ m], part], self.at.zz(m)
         )
 
-    def first(self, parts=(1, 0)):
+    def first(self, rel=None):
         m = self.adds[0]
-        rels = [r for r in range(self.at.n_z) if r & m]
+        rels = [r for r in range(self.at.n_z) if r & m] if rel is None else [rel] if rel & m else []
         for rel in sorted(rels, reverse=True):
-            for part in parts:
+            for part in (1, 0):
                 self.send(m, rel, part)
 
     def add(self, m, rel, part):
@@ -962,22 +970,27 @@
         slot[...] = (block[...].astype(F32) + slot[...].astype(F32)).astype(BF16)
         self.at_mask[rel, part] = m
 
-    def spread(self):
-        at = self.at
+    def plan(self):
+        steps = []
         for i, m in enumerate(self.adds):
-            left = range(0, at.n_z, 2 * m)
+            left = range(0, self.at.n_z, 2 * m)
             nxt = self.adds[i + 1] if i + 1 < len(self.adds) else (2 * m if self.swap else None)
             for rel in sorted(left, key=lambda r: -(r & (nxt or 0))):
-                for part in (1, 0):
-                    self.add(m, rel, part)
-                    if nxt is not None and rel & nxt:
-                        if nxt in self.adds:
-                            self.send(nxt, rel, part)
-                        else:
-                            self.exchange(nxt, rel, part)
-
-    def column(self, mine):
-        return self.at.zb if mine else 1 - self.at.zb
+                steps += [(m, nxt, rel, part) for part in (1, 0)]
+        return steps
+
+    def go(self, count=None):
+        if self.steps is None:
+            self.steps = self.plan()
+        count = len(self.steps) if count is None else count
+        for m, nxt, rel, part in self.steps[:count]:
+            self.add(m, rel, part)
+            if nxt is not None and rel & nxt:
+                if nxt in self.adds:
+                    self.send(nxt, rel, part)
+                else:
+                    self.exchange(nxt, rel, part)
+        self.steps = self.steps[count:]
 
     def exchange(self, m, rel, part):
         block, _ = self.held(rel, part)
@@ -1071,6 +1084,8 @@
     far.begin()
     far.middle()
     own.begin()
+    far.second()
+    f_gu.go(1)
 
     def send_far(layer, i):
         sent = []
@@ -1085,8 +1100,10 @@
         layer.release()
         return sent
 
+    own.middle()
     sent_far = send_far(far, 0)
-    own.middle()
+    own.second()
+    f_gu.go(1)
     heads_v = w3_v.at[:, : w_heads.shape[1]]
     load_heads = move(w_heads, heads_v)
     load_hid.wait()
@@ -1113,22 +1130,27 @@
         d_proj[me, r, :] = value.astype(BF16)
         gather.own(p)
     own.release()
+    f_dn.go(2)
     gather.far_first()
     ffn_own.begin()
-    f_gu.spread()
+    f_gu.go()
     gather.far_second()
-    ffn_far.middle()
+    f_dn.go()
     gather.last()
 
     load_o.wait()
     w_o_all = o_v[...].reshape(width, o_v.shape[3])
 
-    def d_attn_rows(b, carry):
-        r = pl.ds(pl.multiple_of(b * rows, rows), rows)
-        d_attn[r, :] = dot(d_proj[b], w_o_all).astype(BF16)
+    n_part = 4
+
+    def d_attn_rows(c, carry):
+        per = n_b // n_part
+        r = pl.ds(pl.multiple_of(c * (per * rows), per * rows), per * rows)
+        value = d_proj[pl.ds(c * per, per)].reshape(per * rows, width)
+        d_attn[r, :] = dot(value, w_o_all).astype(BF16)
         return carry
 
-    lax.fori_loop(0, n_b, d_attn_rows, 0)
+    lax.fori_loop(0, n_part, d_attn_rows, 0)
 
     group = 1
     while 2 * depth * group % LANES:
@@ -1137,22 +1159,22 @@
 
     def groups():
         rels = sorted(range(0, n_z, group), key=lambda r: (-(r & 1), -r))
-        return [flip_all(z, r) // group for r in rels]
+        return [(r, flip_all(z, r) // group) for r in rels]
 
     def span_of(owner):
         return pl.ds(pl.multiple_of(owner * span, span), span)
 
     o_src = o_v
     f_o = GradFlow(links, at, o_src, o_land, False, o_out, None)
-    for owner in groups():
+    for rel, owner in groups():
         lhs = jnp.concatenate([d_proj[b, :, span_of(owner)] for b in range(n_b)], axis=0)
         value = dot(lhs, attn[...], ((0,), (0,))).astype(BF16)
         o_src[pl.ds(owner * group, group)] = value.reshape(group, 2, depth, value.shape[1])
     f_o.first()
+    ffn_far.middle()
+    ffn_own.middle()
     gather.drain()
     load_norm = move(norm_attn, d_proj)
-    f_dn.spread()
-    ffn_own.middle()
     dk_sum[...] = jnp.zeros_like(dk_sum)
     dv_sum[...] = jnp.zeros_like(dv_sum)
     for i in range(full_len // q_block):
@@ -1160,10 +1182,12 @@
             scale, q_block, i, rot, d_attn, stats, cos, sin, seg_col, seg_row, sel, d_qkv, dk_sum, dv_sum
         )
         if i == 0:
+            ffn_far.second()
+            ffn_own.second()
             f_gu.cross()
             f_dn.cross()
-            sent_ffn = send_far(ffn_far, 1)
     attend_back_keys(scale, n_q, cos, sin, d_qkv, dk_sum, dv_sum)
+    sent_ffn = send_far(ffn_far, 1)
 
     load_heads.wait()
 
@@ -1176,14 +1200,21 @@
     f_in = GradFlow(links, at, in_src, in_land, False, in_out, None)
     packed = dot(d_qkv[...], spread[...], ((1,), (1,))).astype(BF16)
     load_norm.wait()
-    for owner in groups():
+    for rel, owner in groups():
         lhs = jnp.concatenate([d_proj[b, :, span_of(owner)] for b in range(n_b)], axis=0)
         w3_v[span_of(owner), in_cols] = dot(lhs, packed, ((0,), (0,))).astype(BF16)
-    f_in.first()
+        if group == 1:
+            f_in.first(rel)
+    if group > 1:
+        f_in.first()
     d_in = LayerSum(links, at, rows, bufs_a, d_term, ffn_far)
     d_in.begin()
+    f_o.go(2)
     d_in.middle()
-    f_o.spread()
+    f_in.go(2)
+    d_in.second()
+    f_in.go(2)
+    f_o.go()
     f_o.cross()
     out_g, in_g = TpGather(links, at, output), TpGather(links, at, input_grad)
     stay = []
@@ -1202,7 +1233,7 @@
         far_v[0, r, :] = (mid[r, :] + value).astype(BF16)
     out_g.own(far_v.at[0])
     stay.append(move(far_v.at[0], output.at[t]))
-    f_in.spread()
+    f_in.go()
     f_in.cross()
     f_gu.cross_far()
     f_dn.cross_far()

time: 763 us -> 610 us (0.80)
  Pallas kernels: 750 us -> 597 us
    pallas_call x1, Pallas kernels: 165 us -> 9.27 us  [finish(): pl.pallas_call(finish_kernel, out_shape=(shape(4 * units), shape(4 * unit...]
  transfers between devices with their start and end apart: 3 -> 3, of which waited for: 0 -> 0; matrix products, arithmetic and copies ran while one was open for 0% -> 0% of each run, Pallas kernels for 22% -> 2%
where the time goes in v6:
time: 610 us; the launch traced here: 604 us
  Pallas kernels  597 us (98%)
    pallas_call x1, Pallas kernels, back(): pl.pallas_call(lambda *refs: back_kernel(n_z, n_tp, scale, min(256, full_...  286 us
    pallas_call x1, Pallas kernels, front(): pl.pallas_call(lambda *refs: front_kernel(n_z, n_tp, scale, min(256, full...  250 us
    pallas_call x1, Pallas kernels, act(): pl.pallas_call(act_kernel, grid=(blocks // per,), out_shape=(jax.ShapeDty...  23.7 us
    pallas_call x1, Pallas kernels, terms(): pl.pallas_call(terms_kernel, grid=(n_z // group,), out_shape=(jax.ShapeDt...  22.2 us
  transfers between devices with their start and end apart: 3, of which 0 were waited for; matrix products, arithmetic and copies ran while one was open for 0% of the time, Pallas kernels for 2%

profile of v6, /device:TPU:0, one launch (start us, length us, event | category | flops | bytes accessed | tf_op | source)
XLA Modules:
  0.0 603.9 jit_solution(11864821292747487458)
XLA Ops:
  0.6 0.7 stack.9
  1.3 0.7 stack.10
  2.0 0.6 pad_maximum_fusion.refs_9_
  2.6 249.8 %front.1 = (bf16[2560,768]{1,0:T(8,128)(2,1)}, bf16[4,2,320,320]{3,2,1,0:T(8,128)(2,1)}, bf16[4,2,320,1328]{3,2,1,0:T(8,128)(2,1)}, f32[8,2560]{1,0:T(8,128)}, b...) custom-call(bf16[512,2560]{1,0:T(8,128)(2,1)} %bitcast.29, ...), custom_call_target="tpu_custom_call" | custom-call | tf_op jit(solution)/shard_map/front/pallas_call | solution.py:721
  252.4 23.7 %act.1 = (bf16[16,128,864]{2,1,0:T(8,128)(2,1)}, bf16[16,128,432]{2,1,0:T(8,128)(2,1)}) custom-call(bf16[16,128,2560]{2,1,0:T(8,128)(2,1)} %bitcast.24, bf16[16,128,2560]{2,1,0:T(8,128)(2,1)} %bitcast.22, bf16[2560,1328]{1,0:T(8,128)(2,1)} %bitcast.26), custom_call_target="tpu_custom_call" | custom-call | tf_op jit(solution)/shard_map/act/pallas_call | solution.py:793
  276.1 22.2 %terms.1 = (bf16[4,2,320,864]{3,2,1,0:T(8,128)(2,1)}, bf16[4,2,320,432]{3,2,1,0:T(8,128)(2,1)}) custom-call(bf16[16,128,2560]{2,1,0:T(8,128)(2,1)} %bitcast.25, bf16[16,128,2560]{2,1,0:T(8,128)(2,1)} %bitcast.23, bf16[16,128,864]{2,1,0:T(8,128)(2,1)} %get-tuple-element.50.d_gu, bf16[16,128,432]{2,1,0:T(8,128)(2,1)} %get-tuple-element.51.hidden), custom_call_target="tpu_custom_call" | custom-call | tf_op jit(solution)/shard_map/terms/pallas_call | solution.py:826
  298.3 286.4 %back.1 = (bf16[4,128,2560]{2,1,0:T(8,128)(2,1)}, bf16[4,128,2560]{2,1,0:T(8,128)(2,1)}, bf16[2,2,320,864]{3,2,1,0:T(8,128)(2,1)}, bf16[2,2,320,432]{3,2,1,0:T(8...) custom-call(bf16[512,2560]{1,0:T(8,128)(2,1)} %bitcast.30, bf16[512,2560]{1,0:T(8,128)(2,1)} %bitcast.32, ...), custom_call_target="tpu_custom_call" | custom-call | tf_op jit(solution)/shard_map/back/pallas_call | solution.py:1266
  584.7 5.7 finish_in.1
  590.4 0.9 slice_bitcast_fusion
  591.3 0.6 collective-permute-start.1
  591.9 0.7 collective-permute-start.2
  592.6 0.9 collective-permute-start
  593.5 0.0 copy-start
  593.5 0.0 copy-start.1
  593.5 0.0 copy-start.2
  593.5 9.3 %finish.1 = (f32[320,1728]{1,0:T(8,128)}, f32[320,1728]{1,0:T(8,128)}, f32[320,1728]{1,0:T(8,128)}, f32[320,640]{1,0:T(8,128)}, bf16[4,128,2560]{2,1,0:T(8,128)(2,1)}, /*index=5*/bf16[4,128,2560]{2,1,0:T(8,128)(2,1)}) custom-call(bf16[2,2,320,864]{3,2,1,0:T(8,128)(2,1)} %get-tuple-element.67.gu, bf16[2,2,320,432]{3,2,1,0:T(8,128)(2,1)} %get-tuple-element.68.dn, ...), custom_call_target="tpu_custom_call" | custom-call | bytes 20971520 | tf_op jit(solution)/shard_map/finish/pallas_call | solution.py:891
  602.8 0.0 collective-permute-done.1
  602.8 0.0 collective-permute-done.2
  602.8 0.0 collective-permute-done
  602.8 0.0 copy-done
  602.8 0.3 slice_reduce_fusion
  603.1 0.0 copy-done.1
  603.1 0.0 copy-done.2
  603.1 0.6 convert_divide_fusion
  (1 shorter events, 0.0 us)
Async XLA Ops:
  591.3 11.5 %collective-permute-start.1 = (f32[2,320]{0,1:T(8,128)S(1)}, f32[2,320]{0,1:T(8,128)S(1)}, u32[]{:S(2)}, u32[]{:S(2)}) collective-permute-start(f32[2,320]{0,1:T(8,128)S(1)} %slice_bitcast_fusion), channel_id=1, source_target_pairs={{0,2},{1,3},{2,0},{3,1},{4,6},{5,7},{6,4},{7,5},{8,10},{9,11},{10,... | collective-permute-start | bytes 7688 | tf_op jit(solution)/shard_map/ppermute | solution.py:22
  591.9 10.9 %collective-permute-start.2 = (f32[2,320]{0,1:T(8,128)S(1)}, f32[2,320]{0,1:T(8,128)S(1)}, u32[]{:S(2)}, u32[]{:S(2)}) collective-permute-start(f32[2,320]{0,1:T(8,128)S(1)} %slice_bitcast_fusion), channel_id=1, source_target_pairs={{0,3},{1,2},{2,1},{3,0},{4,7},{5,6},{6,5},{7,4},{8,11},{9,10},{10,... | collective-permute-start | bytes 7688 | tf_op jit(solution)/shard_map/ppermute | solution.py:22
  592.6 10.2 %collective-permute-start = (f32[2,320]{0,1:T(8,128)S(1)}, f32[2,320]{0,1:T(8,128)S(1)}, u32[]{:S(2)}, u32[]{:S(2)}) collective-permute-start(f32[2,320]{0,1:T(8,128)S(1)} %slice_bitcast_fusion), channel_id=1, source_target_pairs={{0,1},{1,0},{2,3},{3,2},{4,5},{5,4},{6,7},{7,6},{8,9},{9,8},{10,11... | collective-permute-start | bytes 7688 | tf_op jit(solution)/shard_map/ppermute | solution.py:22
  593.5 9.3 %copy-start = (f32[320,128]{1,0:T(8,128)S(1)}, f32[320,128]{1,0:T(8,128)}, u32[]{:S(2)}) copy-start(f32[320,128]{1,0:T(8,128)} %get-tuple-element.75) | copy-start | bytes 491524
  593.5 9.6 %copy-start.1 = (bf16[320]{0:T(512)(128)(2,1)S(1)}, bf16[320]{0:T(512)(128)(2,1)}, u32[]{:S(2)}) copy-start(bf16[320]{0:T(512)(128)(2,1)} %param.19) | copy-start | bytes 1924
  593.5 9.6 %copy-start.2 = (bf16[320]{0:T(512)(128)(2,1)S(1)}, bf16[320]{0:T(512)(128)(2,1)}, u32[]{:S(2)}) copy-start(bf16[320]{0:T(512)(128)(2,1)} %param.14) | copy-start | bytes 1924

commit v7 on v6

--- a/solution.py
+++ b/solution.py
@@ -97,7 +97,7 @@
 
 
 VMEM_LIMIT = 56 * 1024 * 1024
-BACK_LIMIT = 62 * 1024 * 1024
+BACK_LIMIT = 63 * 1024 * 1024
 
 
 def sum_tp(value):
@@ -1066,8 +1066,9 @@
 
     f_gu = GradFlow(links, at, gu_src, gu_land, True, gu_out, gu_pass, fetch_with(fetch_gu))
     f_dn = GradFlow(links, at, dn_src, dn_land, True, dn_out, dn_pass, fetch_with(fetch_dn))
-    f_gu.first()
-    f_dn.first()
+    for rel in reversed(range(1, n_z, 2)):
+        f_gu.first(rel)
+        f_dn.first(rel)
 
     def term(seq, lhs, lo, hi):
         def product(r, cols):
@@ -1110,6 +1111,7 @@
     ffn_far = LayerSum(links, at, rows, bufs_a, term(1, hid_v, wide, wide + units), far)
     ffn_own = LayerSum(links, at, rows, bufs_b, term(0, hid_v, wide, wide + units), own)
     ffn_far.begin()
+    ffn_far.middle()
 
     def norm_back(inputs, gain, d_normed):
         root = lax.rsqrt(jnp.mean(inputs * inputs, axis=1, keepdims=True) + NORM_EPS)
@@ -1132,10 +1134,10 @@
     own.release()
     f_dn.go(2)
     gather.far_first()
+    ffn_far.second()
     ffn_own.begin()
-    f_gu.go()
     gather.far_second()
-    f_dn.go()
+    sent_ffn = send_far(ffn_far, 1)
     gather.last()
 
     load_o.wait()
@@ -1171,7 +1173,6 @@
         value = dot(lhs, attn[...], ((0,), (0,))).astype(BF16)
         o_src[pl.ds(owner * group, group)] = value.reshape(group, 2, depth, value.shape[1])
     f_o.first()
-    ffn_far.middle()
     ffn_own.middle()
     gather.drain()
     load_norm = move(norm_attn, d_proj)
@@ -1182,12 +1183,13 @@
             scale, q_block, i, rot, d_attn, stats, cos, sin, seg_col, seg_row, sel, d_qkv, dk_sum, dv_sum
         )
         if i == 0:
-            ffn_far.second()
             ffn_own.second()
+            f_gu.go()
             f_gu.cross()
+        if i == 2:
+            f_dn.go()
             f_dn.cross()
     attend_back_keys(scale, n_q, cos, sin, d_qkv, dk_sum, dv_sum)
-    sent_ffn = send_far(ffn_far, 1)
 
     load_heads.wait()
 
@@ -1211,11 +1213,10 @@
     d_in.begin()
     f_o.go(2)
     d_in.middle()
-    f_in.go(2)
+    f_gu.cross_far()
     d_in.second()
     f_in.go(2)
-    f_o.go()
-    f_o.cross()
+    f_dn.cross_far()
     out_g, in_g = TpGather(links, at, output), TpGather(links, at, input_grad)
     stay = []
     for p, value in enumerate(d_in.end()):
@@ -1232,11 +1233,12 @@
         value = value + far_in[1, r, :].astype(F32)
         far_v[0, r, :] = (mid[r, :] + value).astype(BF16)
     out_g.own(far_v.at[0])
+    f_in.go(2)
+    f_o.go()
+    f_o.cross()
     stay.append(move(far_v.at[0], output.at[t]))
     f_in.go()
     f_in.cross()
-    f_gu.cross_far()
-    f_dn.cross_far()
     for flow in (f_gu, f_dn, f_o, f_in):
         stay.append(move(*flow.mine()))
     in_g.second()

time: 610 us -> 587 us (0.962)
  Pallas kernels: 597 us -> 574 us
    pallas_call x1, Pallas kernels: 286 us -> 264 us  [back(): pl.pallas_call(lambda *refs: back_kernel(n_z, n_tp, scale, min(256, full_...]
where the time goes in v7:
time: 587 us; the launch traced here: 581 us
  Pallas kernels  574 us (98%)
    pallas_call x1, Pallas kernels, back(): pl.pallas_call(lambda *refs: back_kernel(n_z, n_tp, scale, min(256, full_...  264 us
    pallas_call x1, Pallas kernels, front(): pl.pallas_call(lambda *refs: front_kernel(n_z, n_tp, scale, min(256, full...  250 us
    pallas_call x1, Pallas kernels, act(): pl.pallas_call(act_kernel, grid=(blocks // per,), out_shape=(jax.ShapeDty...  23.7 us
    pallas_call x1, Pallas kernels, terms(): pl.pallas_call(terms_kernel, grid=(n_z // group,), out_shape=(jax.ShapeDt...  22.2 us
  transfers between devices with their start and end apart: 3, of which 0 were waited for; matrix products, arithmetic and copies ran while one was open for 0% of the time, Pallas kernels for 2%

profile of v7, /device:TPU:0, one launch (start us, length us, event | category | flops | bytes accessed | tf_op | source)
XLA Modules:
  0.0 581.3 jit_solution(13031452781090885097)
XLA Ops:
  0.6 0.7 stack.9
  1.3 0.7 stack.10
  2.0 0.6 pad_maximum_fusion.refs_9_
  2.6 249.8 %front.1 = (bf16[2560,768]{1,0:T(8,128)(2,1)}, bf16[4,2,320,320]{3,2,1,0:T(8,128)(2,1)}, bf16[4,2,320,1328]{3,2,1,0:T(8,128)(2,1)}, f32[8,2560]{1,0:T(8,128)}, b...) custom-call(bf16[512,2560]{1,0:T(8,128)(2,1)} %bitcast.29, ...), custom_call_target="tpu_custom_call" | custom-call | tf_op jit(solution)/shard_map/front/pallas_call | solution.py:721
  252.4 23.7 %act.1 = (bf16[16,128,864]{2,1,0:T(8,128)(2,1)}, bf16[16,128,432]{2,1,0:T(8,128)(2,1)}) custom-call(bf16[16,128,2560]{2,1,0:T(8,128)(2,1)} %bitcast.24, bf16[16,128,2560]{2,1,0:T(8,128)(2,1)} %bitcast.22, bf16[2560,1328]{1,0:T(8,128)(2,1)} %bitcast.26), custom_call_target="tpu_custom_call" | custom-call | tf_op jit(solution)/shard_map/act/pallas_call | solution.py:793
  276.1 22.2 %terms.1 = (bf16[4,2,320,864]{3,2,1,0:T(8,128)(2,1)}, bf16[4,2,320,432]{3,2,1,0:T(8,128)(2,1)}) custom-call(bf16[16,128,2560]{2,1,0:T(8,128)(2,1)} %bitcast.25, bf16[16,128,2560]{2,1,0:T(8,128)(2,1)} %bitcast.23, bf16[16,128,864]{2,1,0:T(8,128)(2,1)} %get-tuple-element.50.d_gu, bf16[16,128,432]{2,1,0:T(8,128)(2,1)} %get-tuple-element.51.hidden), custom_call_target="tpu_custom_call" | custom-call | tf_op jit(solution)/shard_map/terms/pallas_call | solution.py:826
  298.3 263.8 %back.1 = (bf16[4,128,2560]{2,1,0:T(8,128)(2,1)}, bf16[4,128,2560]{2,1,0:T(8,128)(2,1)}, bf16[2,2,320,864]{3,2,1,0:T(8,128)(2,1)}, bf16[2,2,320,432]{3,2,1,0:T(8...) custom-call(bf16[512,2560]{1,0:T(8,128)(2,1)} %bitcast.30, bf16[512,2560]{1,0:T(8,128)(2,1)} %bitcast.32, ...), custom_call_target="tpu_custom_call" | custom-call | tf_op jit(solution)/shard_map/back/pallas_call | solution.py:1268
  562.0 5.7 finish_in.1
  567.7 0.9 slice_bitcast_fusion
  568.6 0.1 collective-permute-start.1
  568.7 1.8 collective-permute-start.2
  570.5 0.3 collective-permute-start
  570.8 0.0 copy-start
  570.8 0.0 copy-start.1
  570.8 0.0 copy-start.2
  570.8 9.3 %finish.1 = (f32[320,1728]{1,0:T(8,128)}, f32[320,1728]{1,0:T(8,128)}, f32[320,1728]{1,0:T(8,128)}, f32[320,640]{1,0:T(8,128)}, bf16[4,128,2560]{2,1,0:T(8,128)(2,1)}, /*index=5*/bf16[4,128,2560]{2,1,0:T(8,128)(2,1)}) custom-call(bf16[2,2,320,864]{3,2,1,0:T(8,128)(2,1)} %get-tuple-element.67.gu, bf16[2,2,320,432]{3,2,1,0:T(8,128)(2,1)} %get-tuple-element.68.dn, ...), custom_call_target="tpu_custom_call" | custom-call | bytes 20971520 | tf_op jit(solution)/shard_map/finish/pallas_call | solution.py:891
  580.1 0.0 collective-permute-done.1
  580.1 0.0 collective-permute-done.2
  580.1 0.0 collective-permute-done
  580.1 0.0 copy-done
  580.2 0.3 slice_reduce_fusion
  580.4 0.0 copy-done.1
  580.4 0.0 copy-done.2
  580.5 0.6 convert_divide_fusion
  (1 shorter events, 0.0 us)
Async XLA Ops:
  568.6 11.5 %collective-permute-start.1 = (f32[2,320]{0,1:T(8,128)S(1)}, f32[2,320]{0,1:T(8,128)S(1)}, u32[]{:S(2)}, u32[]{:S(2)}) collective-permute-start(f32[2,320]{0,1:T(8,128)S(1)} %slice_bitcast_fusion), channel_id=1, source_target_pairs={{0,2},{1,3},{2,0},{3,1},{4,6},{5,7},{6,4},{7,5},{8,10},{9,11},{10,... | collective-permute-start | bytes 7688 | tf_op jit(solution)/shard_map/ppermute | solution.py:22
  568.7 11.4 %collective-permute-start.2 = (f32[2,320]{0,1:T(8,128)S(1)}, f32[2,320]{0,1:T(8,128)S(1)}, u32[]{:S(2)}, u32[]{:S(2)}) collective-permute-start(f32[2,320]{0,1:T(8,128)S(1)} %slice_bitcast_fusion), channel_id=1, source_target_pairs={{0,3},{1,2},{2,1},{3,0},{4,7},{5,6},{6,5},{7,4},{8,11},{9,10},{10,... | collective-permute-start | bytes 7688 | tf_op jit(solution)/shard_map/ppermute | solution.py:22
  570.5 9.6 %collective-permute-start = (f32[2,320]{0,1:T(8,128)S(1)}, f32[2,320]{0,1:T(8,128)S(1)}, u32[]{:S(2)}, u32[]{:S(2)}) collective-permute-start(f32[2,320]{0,1:T(8,128)S(1)} %slice_bitcast_fusion), channel_id=1, source_target_pairs={{0,1},{1,0},{2,3},{3,2},{4,5},{5,4},{6,7},{7,6},{8,9},{9,8},{10,11... | collective-permute-start | bytes 7688 | tf_op jit(solution)/shard_map/ppermute | solution.py:22
  570.8 9.3 %copy-start = (f32[320,128]{1,0:T(8,128)S(1)}, f32[320,128]{1,0:T(8,128)}, u32[]{:S(2)}) copy-start(f32[320,128]{1,0:T(8,128)} %get-tuple-element.75) | copy-start | bytes 491524
  570.8 9.6 %copy-start.1 = (bf16[320]{0:T(512)(128)(2,1)S(1)}, bf16[320]{0:T(512)(128)(2,1)}, u32[]{:S(2)}) copy-start(bf16[320]{0:T(512)(128)(2,1)} %param.19) | copy-start | bytes 1924
  570.8 9.6 %copy-start.2 = (bf16[320]{0:T(512)(128)(2,1)S(1)}, bf16[320]{0:T(512)(128)(2,1)}, u32[]{:S(2)}) copy-start(bf16[320]{0:T(512)(128)(2,1)} %param.14) | copy-start | bytes 1924

commit v8 on v7

--- a/solution.py
+++ b/solution.py
@@ -788,7 +788,7 @@
 
 def act(norm, dy, w3, units):
     blocks, rows, width = norm.shape
-    per = max(1, 512 // rows)
+    per = max(1, 256 // rows)
     one = lambda cols: pl.BlockSpec((per, rows, cols), lambda i: (i, 0, 0))
     return pl.pallas_call(
         act_kernel,
@@ -886,14 +886,26 @@
 
 def finish(gu, dn, o, rows_a, rows_b):
     depth, units, q_cols = dn.shape[2], dn.shape[3], o.shape[2]
+    n_rows, width = rows_a.shape[0], rows_a.shape[2]
+    steps = n_rows if depth % (16 * n_rows) == 0 else 1
+    part = depth // steps
     shape = lambda cols: jax.ShapeDtypeStruct((depth, cols), F32)
     like = lambda a: jax.ShapeDtypeStruct(a.shape, a.dtype)
+    four = lambda cols: pl.BlockSpec((2, 2, part, cols), lambda i: (0, 0, i, 0))
+    out = lambda cols: pl.BlockSpec((part, cols), lambda i: (i, 0))
+    rows = pl.BlockSpec((n_rows // steps, rows_a.shape[1], width), lambda i: (i, 0, 0))
     return pl.pallas_call(
         finish_kernel,
+        grid=(steps,),
         out_shape=(
             shape(4 * units), shape(4 * units), shape(4 * units), shape(2 * q_cols),
             like(rows_a), like(rows_b),
         ),
+        in_specs=[
+            four(2 * units), four(units), pl.BlockSpec((2, part, q_cols), lambda i: (0, i, 0)),
+            rows, rows,
+        ],
+        out_specs=(out(4 * units), out(4 * units), out(4 * units), out(2 * q_cols), rows, rows),
         compiler_params=pltpu.CompilerParams(vmem_limit_bytes=VMEM_LIMIT),
         cost_estimate=pl.CostEstimate(flops=0, bytes_accessed=20 * 2**20, transcendentals=0),
         name="finish",

time: 587 us -> 587 us (level)
  transfers between devices with their start and end apart: 3 -> 3, of which waited for: 0 -> 0; matrix products, arithmetic and copies ran while one was open for 0% -> 0% of each run, Pallas kernels for 2% -> 1%
where the time goes in v8:
time: 587 us; the launch traced here: 580 us
  Pallas kernels  573 us (98%)
    pallas_call x1, Pallas kernels, back(): pl.pallas_call(lambda *refs: back_kernel(n_z, n_tp, scale, min(256, full_...  264 us
    pallas_call x1, Pallas kernels, front(): pl.pallas_call(lambda *refs: front_kernel(n_z, n_tp, scale, min(256, full...  250 us
    pallas_call x1, Pallas kernels, act(): pl.pallas_call(act_kernel, grid=(blocks // per,), out_shape=(jax.ShapeDty...  23.4 us
    pallas_call x1, Pallas kernels, terms(): pl.pallas_call(terms_kernel, grid=(n_z // group,), out_shape=(jax.ShapeDt...  22.6 us
  transfers between devices with their start and end apart: 3, of which 0 were waited for; matrix products, arithmetic and copies ran while one was open for 0% of the time, Pallas kernels for 1%

profile of v8, /device:TPU:0, one launch (start us, length us, event | category | flops | bytes accessed | tf_op | source)
XLA Modules:
  0.0 580.4 jit_solution(6632383446123583599)
XLA Ops:
  0.6 0.7 stack.9
  1.3 0.7 stack.10
  2.0 0.6 pad_maximum_fusion.refs_9_
  2.6 249.8 %front.1 = (bf16[2560,768]{1,0:T(8,128)(2,1)}, bf16[4,2,320,320]{3,2,1,0:T(8,128)(2,1)}, bf16[4,2,320,1328]{3,2,1,0:T(8,128)(2,1)}, f32[8,2560]{1,0:T(8,128)}, b...) custom-call(bf16[512,2560]{1,0:T(8,128)(2,1)} %bitcast.29, ...), custom_call_target="tpu_custom_call" | custom-call | tf_op jit(solution)/shard_map/front/pallas_call | solution.py:721
  252.4 23.4 %act.1 = (bf16[16,128,864]{2,1,0:T(8,128)(2,1)}, bf16[16,128,432]{2,1,0:T(8,128)(2,1)}) custom-call(bf16[16,128,2560]{2,1,0:T(8,128)(2,1)} %bitcast.24, bf16[16,128,2560]{2,1,0:T(8,128)(2,1)} %bitcast.22, bf16[2560,1328]{1,0:T(8,128)(2,1)} %bitcast.26), custom_call_target="tpu_custom_call" | custom-call | tf_op jit(solution)/shard_map/act/pallas_call | solution.py:793
  275.7 22.6 %terms.1 = (bf16[4,2,320,864]{3,2,1,0:T(8,128)(2,1)}, bf16[4,2,320,432]{3,2,1,0:T(8,128)(2,1)}) custom-call(bf16[16,128,2560]{2,1,0:T(8,128)(2,1)} %bitcast.25, bf16[16,128,2560]{2,1,0:T(8,128)(2,1)} %bitcast.23, bf16[16,128,864]{2,1,0:T(8,128)(2,1)} %get-tuple-element.50.d_gu, bf16[16,128,432]{2,1,0:T(8,128)(2,1)} %get-tuple-element.51.hidden), custom_call_target="tpu_custom_call" | custom-call | tf_op jit(solution)/shard_map/terms/pallas_call | solution.py:826
  298.3 263.7 %back.1 = (bf16[4,128,2560]{2,1,0:T(8,128)(2,1)}, bf16[4,128,2560]{2,1,0:T(8,128)(2,1)}, bf16[2,2,320,864]{3,2,1,0:T(8,128)(2,1)}, bf16[2,2,320,432]{3,2,1,0:T(8...) custom-call(bf16[512,2560]{1,0:T(8,128)(2,1)} %bitcast.30, bf16[512,2560]{1,0:T(8,128)(2,1)} %bitcast.32, ...), custom_call_target="tpu_custom_call" | custom-call | tf_op jit(solution)/shard_map/back/pallas_call | solution.py:1280
  562.1 5.7 finish_in.1
  567.7 0.9 slice_bitcast_fusion
  568.6 0.1 collective-permute-start.1
  568.7 1.8 collective-permute-start.2
  570.5 0.3 collective-permute-start
  570.8 0.0 copy-start
  570.8 0.0 copy-start.1
  570.8 0.0 copy-start.2
  570.9 8.4 %finish.1 = (f32[320,1728]{1,0:T(8,128)}, f32[320,1728]{1,0:T(8,128)}, f32[320,1728]{1,0:T(8,128)}, f32[320,640]{1,0:T(8,128)}, bf16[4,128,2560]{2,1,0:T(8,128)(2,1)}, /*index=5*/bf16[4,128,2560]{2,1,0:T(8,128)(2,1)}) custom-call(bf16[2,2,320,864]{3,2,1,0:T(8,128)(2,1)} %get-tuple-element.67.gu, bf16[2,2,320,432]{3,2,1,0:T(8,128)(2,1)} %get-tuple-element.68.dn, ...), custom_call_target="tpu_custom_call" | custom-call | bytes 20971520 | tf_op jit(solution)/shard_map/finish/pallas_call | solution.py:897
  579.2 0.0 collective-permute-done.1
  579.2 0.0 collective-permute-done.2
  579.2 0.0 collective-permute-done
  579.2 0.0 copy-done
  579.3 0.3 slice_reduce_fusion
  579.6 0.0 copy-done.1
  579.6 0.0 copy-done.2
  579.6 0.6 convert_divide_fusion
  (1 shorter events, 0.0 us)
Async XLA Ops:
  568.6 10.6 %collective-permute-start.1 = (f32[2,320]{0,1:T(8,128)S(1)}, f32[2,320]{0,1:T(8,128)S(1)}, u32[]{:S(2)}, u32[]{:S(2)}) collective-permute-start(f32[2,320]{0,1:T(8,128)S(1)} %slice_bitcast_fusion), channel_id=1, source_target_pairs={{0,2},{1,3},{2,0},{3,1},{4,6},{5,7},{6,4},{7,5},{8,10},{9,11},{10,... | collective-permute-start | bytes 7688 | tf_op jit(solution)/shard_map/ppermute | solution.py:22
  568.7 10.5 %collective-permute-start.2 = (f32[2,320]{0,1:T(8,128)S(1)}, f32[2,320]{0,1:T(8,128)S(1)}, u32[]{:S(2)}, u32[]{:S(2)}) collective-permute-start(f32[2,320]{0,1:T(8,128)S(1)} %slice_bitcast_fusion), channel_id=1, source_target_pairs={{0,3},{1,2},{2,1},{3,0},{4,7},{5,6},{6,5},{7,4},{8,11},{9,10},{10,... | collective-permute-start | bytes 7688 | tf_op jit(solution)/shard_map/ppermute | solution.py:22
  570.5 8.7 %collective-permute-start = (f32[2,320]{0,1:T(8,128)S(1)}, f32[2,320]{0,1:T(8,128)S(1)}, u32[]{:S(2)}, u32[]{:S(2)}) collective-permute-start(f32[2,320]{0,1:T(8,128)S(1)} %slice_bitcast_fusion), channel_id=1, source_target_pairs={{0,1},{1,0},{2,3},{3,2},{4,5},{5,4},{6,7},{7,6},{8,9},{9,8},{10,11... | collective-permute-start | bytes 7688 | tf_op jit(solution)/shard_map/ppermute | solution.py:22
  570.8 8.4 %copy-start = (f32[320,128]{1,0:T(8,128)S(1)}, f32[320,128]{1,0:T(8,128)}, u32[]{:S(2)}) copy-start(f32[320,128]{1,0:T(8,128)} %get-tuple-element.75) | copy-start | bytes 491524
  570.8 8.7 %copy-start.1 = (bf16[320]{0:T(512)(128)(2,1)S(1)}, bf16[320]{0:T(512)(128)(2,1)}, u32[]{:S(2)}) copy-start(bf16[320]{0:T(512)(128)(2,1)} %param.19) | copy-start | bytes 1924
  570.8 8.7 %copy-start.2 = (bf16[320]{0:T(512)(128)(2,1)S(1)}, bf16[320]{0:T(512)(128)(2,1)}, u32[]{:S(2)}) copy-start(bf16[320]{0:T(512)(128)(2,1)} %param.14) | copy-start | bytes 1924
